TPU v7x, 32 devices: a whole 2x2x4 slice. The times are simulated.
32 devices in a mesh: groups: 2 (over x), query: 8 (over z, y), target: 2 (over core).
Axes of the slice: x: 2, y: 2, z: 4, core: 2. Of those that a mesh axis runs over, the one named last changes fastest.
Arguments:
- query_input: bfloat16 [32, 960, 128], P(('groups', 'query')), parts along dimension 0, may hold values from -18 to 18
- target_input: bfloat16 [64, 960, 128], P(('groups', 'query', 'target')), parts along dimension 0, may hold values from -18 to 18
- conv_weight: bfloat16 [3, 3, 128, 128], replicated, may hold values from -0.1875 to 0.1875
- conv_bias: float32 [128], replicated, may hold values from -3 to 3
Outputs:
- flow: float32 [2, 16, 480], P(None, ('groups', 'query')), parts along dimension 1
There are 2 independent parts, one for each index of `groups`. A program takes and returns all parts, laid end to end along the dimension named above; an argument that names none is the same for every part. Nothing has to cross between parts.
All inputs are finite; a program needn't handle non-finite values.
Results may differ from a plain program's by a relative error of at most 0.0026.
Values may be sent and summed in bfloat16 or wider, within the bound.
No kernel may reach another device: no remote copies, remote signals or barrier semaphores. Data moves between devices by JAX's collectives and lax.ppermute only.
A program may use at most 64 MiB of HBM per device.

v0:
```python
import math

import jax
import jax.numpy as jnp
from jax import lax
from jax.sharding import PartitionSpec as P

CELL = 0.0625
FLOOR = -1e30


def passed_along(block, axis, distance):
    devices = range(lax.axis_size(axis))
    route = [(i - distance, i) for i in devices if i - distance in devices]
    return lax.ppermute(block, axis, route)


def shifted(value, axis, steps):
    count = lax.axis_size(axis)
    pairs = [(source, (source + steps) % count) for source in range(count)]
    return lax.ppermute(value, axis, pairs)


def merged(value, axis, join):
    pieces = jax.tree.map(lambda part: lax.all_gather(part, axis), value)
    head = jax.tree.map(lambda part: part[0], pieces)
    tail = jax.tree.map(lambda part: part[1:], pieces)
    total, _ = lax.scan(lambda total, slab: (join(total, slab), None), head, tail)
    return total


def swapped(block, axis, apart):
    count = lax.axis_size(axis)
    route = []
    for low in range(count):
        high = low | 1 << apart
        if high != low and high < count:
            route += [(low, high), (high, low)]
    return lax.ppermute(block, axis, route)


def convolve(frame, upper_rim, conv_weight, conv_bias):
    padded = jnp.concatenate([upper_rim, frame], axis=0)
    padded = jnp.pad(padded, ((0, 0), (1, 0), (0, 0)))
    out_rows = frame.shape[0] // 2
    out_cols = frame.shape[1] // 2
    channels = frame.shape[2]
    summed = jnp.zeros((out_rows * out_cols, conv_weight.shape[3]), jnp.float32)
    for tap_row in range(3):
        for tap_col in range(3):
            window = padded[
                tap_row : tap_row + 2 * out_rows : 2, tap_col : tap_col + 2 * out_cols : 2
            ]
            summed = summed + jnp.dot(
                window.reshape(out_rows * out_cols, channels),
                conv_weight[tap_row, tap_col],
                preferred_element_type=jnp.float32,
            )
    return (summed + conv_bias).astype(jnp.bfloat16)


def starting_state(count):
    return (
        jnp.full((count,), FLOOR, jnp.float32),
        jnp.zeros((count,), jnp.float32),
        jnp.zeros((count,), jnp.float32),
        jnp.zeros((count,), jnp.float32),
    )


def absorb(state_now, key_block, block_rows, queries):
    row_count, row_width, channels = key_block.shape
    key_matrix = key_block.reshape(row_count * row_width, channels)
    scores = jnp.einsum("qc,kc->qk", queries, key_matrix, preferred_element_type=jnp.float32) * (
        1.0 / math.sqrt(channels)
    )
    column_x = (
        lax.broadcasted_iota(jnp.int32, (row_count, row_width), 1).astype(jnp.float32) * CELL
    ).reshape(-1)
    row_y = (
        jnp.broadcast_to(block_rows[:, None], (row_count, row_width)).astype(jnp.float32) * CELL
    ).reshape(-1)
    running_max, weight_sum, sum_x, sum_y = state_now
    new_max = jnp.maximum(running_max, jnp.max(scores, axis=1))
    rescale = jnp.exp(running_max - new_max)
    weights = jnp.exp(scores - new_max[:, None])
    weight_sum = weight_sum * rescale + jnp.sum(weights, axis=1)
    sum_x = sum_x * rescale + jnp.dot(weights, column_x, precision=lax.Precision.HIGHEST)
    sum_y = sum_y * rescale + jnp.dot(weights, row_y, precision=lax.Precision.HIGHEST)
    return (new_max, weight_sum, sum_x, sum_y)


def fold_rows(state_now, shard_piece, global_rows, queries, block_keys):
    row_count = shard_piece.shape[0]
    row_width = shard_piece.shape[1]
    stride = max(1, block_keys // row_width)
    full_blocks = row_count // stride
    leftover = row_count - full_blocks * stride
    state_now = absorb(state_now, shard_piece, global_rows, queries)
    return state_now


def combine_partials(first_part, second_part):
    new_max = jnp.maximum(first_part[0], second_part[0])
    first_scale = jnp.exp(first_part[0] - new_max)
    second_scale = jnp.exp(second_part[0] - new_max)
    return (
        new_max,
        first_part[1] * first_scale + second_part[1] * second_scale,
        first_part[2] * first_scale + second_part[2] * second_scale,
        first_part[3] * first_scale + second_part[3] * second_scale,
    )


def displacement(mean_x, mean_y, positions, query_slot, band_rows, row_width):
    query_x = (positions % row_width).astype(jnp.float32) * CELL
    query_y = (query_slot * band_rows + positions // row_width).astype(jnp.float32) * CELL
    return jnp.stack([mean_x - query_x, mean_y - query_y])


def on_device(query_input, target_input, conv_weight, conv_bias):
    query_rim = passed_along(query_input[-1:], "query", 1)
    target_rim = passed_along(target_input[-1:], ("query", "target"), 1)
    queries = convolve(query_input, query_rim, conv_weight, conv_bias)
    targets = convolve(target_input, target_rim, conv_weight, conv_bias)
    row_width = query_input.shape[1] // 2
    band_rows = query_input.shape[0] // 2
    shard_rows = target_input.shape[0] // 2
    channels = targets.shape[1]
    target_block = targets.reshape(shard_rows, row_width, channels)
    query_slot = lax.axis_index("query")
    core_slot = lax.axis_index("target")
    core_count = lax.axis_size("target")
    query_total = lax.axis_size("query")
    query_count = band_rows * row_width
    block_slot = query_slot % 4
    upward = [queries]
    for step in range(3):
        upward.append(passed_along(upward[-1], "query", 1))
    downward = [queries]
    for step in range(3):
        downward.append(passed_along(downward[-1], "query", -1))
    candidates = jnp.stack(
        [downward[3], downward[2], downward[1], queries, upward[1], upward[2], upward[3]]
    )
    block_queries = jnp.concatenate(
        [
            lax.dynamic_index_in_dim(candidates, block_slot - member + 3, 0, keepdims=False)
            for member in range(4)
        ],
        axis=0,
    )
    local_rows = jnp.arange(shard_rows, dtype=jnp.int32)

    def share_rows(share_query):
        return (share_query * core_count + core_slot) * shard_rows + local_rows

    state_now = fold_rows(
        starting_state(4 * query_count), target_block, share_rows(query_slot), block_queries, 1024
    )
    hops = query_total // 4 - 1

    def hop(counter, carried):
        piece, state_inner = carried
        piece = shifted(piece, "query", 4)
        source = (query_slot - 4 * (counter + 1)) % query_total
        return (piece, fold_rows(state_inner, piece, share_rows(source), block_queries, 1024))

    target_piece, state_now = lax.fori_loop(0, hops, hop, (target_block, state_now))
    state_now = merged(state_now, "target", combine_partials)
    for bit in range(2):
        partner = swapped(state_now, "query", bit)
        state_now = combine_partials(state_now, partner)
    running_max, weight_sum, sum_x, sum_y = [
        lax.dynamic_slice_in_dim(member, block_slot * query_count, query_count, 0)
        for member in state_now
    ]
    positions = jnp.arange(query_count, dtype=jnp.int32)
    flow = displacement(
        sum_x / weight_sum, sum_y / weight_sum, positions, query_slot, band_rows, row_width
    )
    return flow.reshape(2, band_rows, row_width)


def solution(mesh):
    placed = (
        P(("groups", "query"), None, None),
        P(("groups", "query", "target"), None, None),
        P(),
        P(),
    )
    return jax.shard_map(
        on_device,
        mesh=mesh,
        in_specs=placed,
        out_specs=P(None, ("groups", "query"), None),
        check_vma=False,
    )
```

profile of v0, /device:TPU:0, one launch (start us, length us, event | category | flops | bytes accessed | tf_op | source)
XLA Modules:
  0.0 84.9 jit_solution(567079724396638801)
XLA Ops:
  0.0 1.0 %slice.138 = bf16[1,960,128]{2,1,0:T(8,128)(2,1)S(1)} slice(bf16[2,960,128]{2,1,0:T(8,128)(2,1)} %param.4), slice={[1:2], [0:960], [0:128]} | slice | bytes 491520 | tf_op jit(solution)/shard_map/slice | solution.py:122
  1.0 4.9 %collective-permute-start = (bf16[1,960,128]{2,1,0:T(8,128)(2,1)S(1)}, bf16[1,960,128]{2,1,0:T(8,128)(2,1)S(1)}, u32[]{:S(2)}, u32[]{:S(2)}) collective-permute-start(bf16[1,960,128]{2,1,0:T(8,128)(2,1)S(1)} %slice.138), channel_id=1, source_target_pairs={{0,2},{2,4},{4,6},{6,8},{8,10},{10,12},{12,14},{1,3},{3,5},{5,7},{... | collective-permute-start | bytes 737288 | tf_op jit(solution)/shard_map/ppermute | solution.py:15
  5.9 1.0 %slice.157 = bf16[1,960,128]{2,1,0:T(8,128)(2,1)S(1)} slice(bf16[2,960,128]{2,1,0:T(8,128)(2,1)} %param.5), slice={[1:2], [0:960], [0:128]} | slice | bytes 491520 | tf_op jit(solution)/shard_map/slice | solution.py:123
  6.9 1.5 %collective-permute-start.7 = (bf16[1,960,128]{2,1,0:T(8,128)(2,1)S(1)}, bf16[1,960,128]{2,1,0:T(8,128)(2,1)S(1)}, u32[]{:S(2)}, u32[]{:S(2)}) collective-permute-start(bf16[1,960,128]{2,1,0:T(8,128)(2,1)S(1)} %slice.157), channel_id=1, source_target_pairs={{0,1},{1,2},{2,3},{3,4},{4,5},{5,6},{6,7},{7,8},{8,9},{9,10},{10,1... | collective-permute-start | bytes 737288 | tf_op jit(solution)/shard_map/ppermute | solution.py:15
  8.4 2.9 %collective-permute-done = bf16[1,960,128]{2,1,0:T(8,128)(2,1)S(1)} collective-permute-done((bf16[1,960,128]{2,1,0:T(8,128)(2,1)S(1)}, bf16[1,960,128]{2,1,0:T(8,128)(2,1)S(1)}, u32[]{:S(2)}, u32[]{:S(2)}) %collective-permute-start) | collective-permute-done | bytes 245792 | tf_op jit(solution)/shard_map/ppermute | solution.py:15
  11.3 1.2 %fusion.26 = bf16[3,961,128]{2,1,0:T(8,128)(2,1)S(1)} fusion(bf16[2,960,128]{2,1,0:T(8,128)(2,1)} %param.4, bf16[1,960,128]{2,1,0:T(8,128)(2,1)S(1)} %collective-permute-done), kind=kLoop, calls=%fused_computation.47 | loop fusion | flops 2583168 | bytes 1475328 | tf_op jit(solution)/shard_map/concatenate | solution.py:43
  12.6 0.4 slice.139
  13.0 0.4 slice.141
  13.4 0.4 slice.143
  13.8 0.4 slice.145
  14.2 0.4 slice.147
  14.6 0.4 slice.149
  15.0 0.4 slice.151
  15.4 0.4 slice.153
  16.0 0.2 convolution_add_fusion.15
  16.2 0.2 convolution_add_fusion.14
  16.3 0.2 convolution_add_fusion.13
  16.5 0.2 convolution_add_fusion.12
  16.7 0.2 convolution_add_fusion.11
  17.0 0.2 convolution_add_fusion.9
  17.2 0.4 slice.155
  17.6 0.2 fusion.20
  17.8 1.3 %collective-permute-start.1 = (bf16[480,128]{1,0:T(8,128)(2,1)S(1)}, bf16[480,128]{1,0:T(8,128)(2,1)S(1)}, u32[]{:S(2)}, u32[]{:S(2)}) collective-permute-start(bf16[480,128]{1,0:T(8,128)(2,1)S(1)} %fusion.20), channel_id=1, source_target_pairs={{2,0},{4,2},{6,4},{8,6},{10,8},{12,10},{14,12},{3,1},{5,3},{7,5},{... | collective-permute-start | bytes 368648 | tf_op jit(solution)/shard_map/ppermute | solution.py:15
  19.1 5.0 %collective-permute-start.4 = (bf16[480,128]{1,0:T(8,128)(2,1)S(1)}, bf16[480,128]{1,0:T(8,128)(2,1)S(1)}, u32[]{:S(2)}, u32[]{:S(2)}) collective-permute-start(bf16[480,128]{1,0:T(8,128)(2,1)S(1)} %fusion.20), channel_id=1, source_target_pairs={{0,2},{2,4},{4,6},{6,8},{8,10},{10,12},{12,14},{1,3},{3,5},{5,7},{... | collective-permute-start | bytes 368648 | tf_op jit(solution)/shard_map/ppermute | solution.py:15
  24.2 0.2 fusion.27
  24.4 0.4 slice.158
  24.8 0.4 slice.159
  25.2 0.4 slice.160
  25.6 0.4 slice.161
  26.0 0.4 slice.162
  26.4 0.4 slice.163
  26.8 0.4 slice.164
  27.2 0.4 slice.165
  27.6 0.4 slice.166
  28.9 0.2 convolution_add_fusion.3
  29.0 0.2 convolution_add_fusion.2
  29.2 1.3 %collective-permute-start.2 = (bf16[480,128]{1,0:T(8,128)(2,1)S(1)}, bf16[480,128]{1,0:T(8,128)(2,1)S(1)}, u32[]{:S(2)}, u32[]{:S(2)}) collective-permute-start(bf16[480,128]{1,0:T(8,128)(2,1)S(1)} %collective-permute-done.1), channel_id=1, source_target_pairs={{2,0},{4,2},{6,4},{8,6},{10,8},{12,10},{14,12},{3,1},{5,3},{7,5},{... | collective-permute-start | bytes 368648 | tf_op jit(solution)/shard_map/ppermute | solution.py:15
  30.7 5.5 %collective-permute-start.5 = (bf16[480,128]{1,0:T(8,128)(2,1)S(1)}, bf16[480,128]{1,0:T(8,128)(2,1)S(1)}, u32[]{:S(2)}, u32[]{:S(2)}) collective-permute-start(bf16[480,128]{1,0:T(8,128)(2,1)S(1)} %collective-permute-done.4), channel_id=1, source_target_pairs={{0,2},{2,4},{4,6},{6,8},{8,10},{10,12},{12,14},{1,3},{3,5},{5,7},{... | collective-permute-start | bytes 368648 | tf_op jit(solution)/shard_map/ppermute | solution.py:15
  36.2 0.7 collective-permute-done.2
  36.9 1.3 %collective-permute-start.3 = (bf16[480,128]{1,0:T(8,128)(2,1)S(1)}, bf16[480,128]{1,0:T(8,128)(2,1)S(1)}, u32[]{:S(2)}, u32[]{:S(2)}) collective-permute-start(bf16[480,128]{1,0:T(8,128)(2,1)S(1)} %collective-permute-done.2), channel_id=1, source_target_pairs={{2,0},{4,2},{6,4},{8,6},{10,8},{12,10},{14,12},{3,1},{5,3},{7,5},{... | collective-permute-start | bytes 368648 | tf_op jit(solution)/shard_map/ppermute | solution.py:15
  38.2 0.2 fusion.21
  38.4 6.1 %collective-permute-start.8 = (bf16[1,480,128]{2,1,0:T(8,128)(2,1)S(1)}, bf16[1,480,128]{2,1,0:T(8,128)(2,1)S(1)}, u32[]{:S(2)}, u32[]{:S(2)}) collective-permute-start(bf16[1,480,128]{2,1,0:T(8,128)(2,1)S(1)} %bitcast.138), channel_id=1, source_target_pairs={{0,8},{2,10},{4,12},{6,14},{8,0},{10,2},{12,4},{14,6},{1,9},{3,11}... | collective-permute-start | bytes 368648 | tf_op jit(solution)/shard_map/while/body/eval_jaxpr/ppermute | solution.py:21
  44.5 2.2 %collective-permute-start.6 = (bf16[480,128]{1,0:T(8,128)(2,1)S(1)}, bf16[480,128]{1,0:T(8,128)(2,1)S(1)}, u32[]{:S(2)}, u32[]{:S(2)}) collective-permute-start(bf16[480,128]{1,0:T(8,128)(2,1)S(1)} %collective-permute-done.5), channel_id=1, source_target_pairs={{0,2},{2,4},{4,6},{6,8},{8,10},{10,12},{12,14},{1,3},{3,5},{5,7},{... | collective-permute-start | bytes 368648 | tf_op jit(solution)/shard_map/ppermute | solution.py:15
  46.8 2.1 %collective-permute-done.6 = bf16[480,128]{1,0:T(8,128)(2,1)S(1)} collective-permute-done((bf16[480,128]{1,0:T(8,128)(2,1)S(1)}, bf16[480,128]{1,0:T(8,128)(2,1)S(1)}, u32[]{:S(2)}, u32[]{:S(2)}) %collective-permute-start.6) | collective-permute-done | bytes 122912 | tf_op jit(solution)/shard_map/ppermute | solution.py:15
  49.0 0.7 multiply_reduce_fusion.1
  49.7 0.7 multiply_reduce_fusion
  50.4 2.5 %fusion.24 = f32[1920]{0:T(1024)S(1)} fusion(f32[480,1]{0,1:T(1,128)S(1)} %bitcast.139, f32[1920,480]{0,1:T(8,128)S(1)} %get-tuple-element.97, f32[1920]{0:T(1024)S(1)} %get-tuple-element.94), kind=kOutput, calls=%fused_computation.45 | convolution fusion | flops 12902400 | bytes 3703680 | tf_op jit(solution)/shard_map/dot_general | solution.py:88
  52.9 1.2 %fusion.1 = (f32[1920]{0:T(1024)S(1)}, f32[1920]{0:T(1024)S(1)}) fusion(f32[1920,480]{0,1:T(8,128)S(1)} %get-tuple-element.97, f32[1920]{0:T(1024)S(1)} %get-tuple-element.94, f32[1920]{0:T(1024)S(1)} %get-tuple-element.95, f32[1920,480]{0,1:T(8,128)S(1)} %get-tuple-element.99), kind=kLoop, calls=%fused_computation.5 | loop fusion | flops 5525760 | bytes 7403520 | tf_op jit(solution)/shard_map/reduce_sum | solution.py:87
  54.1 2.5 %fusion.22 = f32[1920]{0:T(1024)S(1)} fusion(f32[480,1]{0,1:T(1,128)S(1)} %bitcast.140, f32[1920,480]{0,1:T(8,128)S(1)} %get-tuple-element.99, f32[1920]{0:T(1024)S(1)} %get-tuple-element.95), kind=kOutput, calls=%fused_computation.43 | convolution fusion | flops 12902400 | bytes 3703680 | tf_op jit(solution)/shard_map/while/body/eval_jaxpr/dot_general | solution.py:88
  56.7 2.0 %all-gather.3 = f32[2,1,1920]{2,1,0:T(1,128)S(1)} all-gather(f32[1,1,1920]{2,1,0:T(1,128)S(1)} %get-tuple-element.87), channel_id=1, replica_groups=mesh['groups'=2,'query'=8,'target'=2] {'target'}, dimensions={0}, use_global_device_ids=true | all-gather | bytes 23040 | tf_op jit(solution)/shard_map/all_gather | solution.py:25
  58.8 2.5 %fusion.25 = f32[1920]{0:T(1024)S(1)} fusion(f32[1920,480]{0,1:T(8,128)S(1)} %get-tuple-element.97, f32[1920]{0:T(1024)S(1)} %get-tuple-element.94, f32[]{:T(128)S(6)} %mul.154), kind=kOutput, calls=%fused_computation.46 | convolution fusion | flops 12902400 | bytes 3701764 | tf_op jit(solution)/shard_map/dot_general | solution.py:89
  61.3 2.5 %fusion.23 = f32[1920]{0:T(1024)S(1)} fusion(f32[1920,480]{0,1:T(8,128)S(1)} %get-tuple-element.99, f32[1920]{0:T(1024)S(1)} %get-tuple-element.95, f32[]{:T(128)S(6)} %mul.157), kind=kOutput, calls=%fused_computation.44 | convolution fusion | flops 12902400 | bytes 3701764 | tf_op jit(solution)/shard_map/while/body/eval_jaxpr/dot_general | solution.py:89
  63.8 1.8 %all-gather.2 = f32[2,1,1920]{2,1,0:T(1,128)S(1)} all-gather(f32[1,1,1920]{2,1,0:T(1,128)S(1)} %reshape.188), channel_id=2, replica_groups=mesh['groups'=2,'query'=8,'target'=2] {'target'}, dimensions={0}, use_global_device_ids=true | all-gather | bytes 23040 | tf_op jit(solution)/shard_map/all_gather | solution.py:25
  65.7 3.0 %collective-permute-start.10 = (f32[1920]{0:T(1024)S(1)}, f32[1920]{0:T(1024)S(1)}, u32[]{:S(2)}, u32[]{:S(2)}) collective-permute-start(f32[1920]{0:T(1024)S(1)} %get-tuple-element.63), channel_id=1, source_target_pairs={{0,2},{2,0},{4,6},{6,4},{8,10},{10,8},{12,14},{14,12},{1,3},{3,1},... | collective-permute-start | bytes 23048 | tf_op jit(solution)/shard_map/ppermute | solution.py:39
  68.7 1.8 %all-gather.4 = f32[2,1,1920]{2,1,0:T(1,128)S(1)} all-gather(f32[1,1,1920]{2,1,0:T(1,128)S(1)} %get-tuple-element.86), channel_id=1, replica_groups=mesh['groups'=2,'query'=8,'target'=2] {'target'}, dimensions={0}, use_global_device_ids=true | all-gather | bytes 23040 | tf_op jit(solution)/shard_map/all_gather | solution.py:25
  70.6 1.8 %all-gather.5 = f32[2,1,1920]{2,1,0:T(1,128)S(1)} all-gather(f32[1,1,1920]{2,1,0:T(1,128)S(1)} %reshape.194), channel_id=3, replica_groups=mesh['groups'=2,'query'=8,'target'=2] {'target'}, dimensions={0}, use_global_device_ids=true | all-gather | bytes 23040 | tf_op jit(solution)/shard_map/all_gather | solution.py:25
  72.5 3.9 %collective-permute-start.11 = (f32[1920]{0:T(1024)S(1)}, f32[1920]{0:T(1024)S(1)}, u32[]{:S(2)}, u32[]{:S(2)}) collective-permute-start(f32[1920]{0:T(1024)S(1)} %get-tuple-element.93), channel_id=1, source_target_pairs={{0,4},{4,0},{2,6},{6,2},{8,12},{12,8},{10,14},{14,10},{1,5},{5,1},... | collective-permute-start | bytes 23048 | tf_op jit(solution)/shard_map/ppermute | solution.py:39
  76.5 1.9 %collective-permute-start.15 = (f32[1920]{0:T(1024)S(1)}, f32[1920]{0:T(1024)S(1)}, u32[]{:S(2)}, u32[]{:S(2)}) collective-permute-start(f32[1920]{0:T(1024)S(1)} %get-tuple-element.82), channel_id=1, source_target_pairs={{0,2},{2,0},{4,6},{6,4},{8,10},{10,8},{12,14},{14,12},{1,3},{3,1},... | collective-permute-start | bytes 23048 | tf_op jit(solution)/shard_map/ppermute | solution.py:39
  78.5 1.5 %collective-permute-done.13 = f32[1920]{0:T(1024)S(1)} collective-permute-done((f32[1920]{0:T(1024)S(1)}, f32[1920]{0:T(1024)S(1)}, u32[]{:S(2)}, u32[]{:S(2)}) %collective-permute-start.13) | collective-permute-done | bytes 7712 | tf_op jit(solution)/shard_map/ppermute | solution.py:39
  80.2 0.4 collective-permute-start.14
  80.6 1.7 %collective-permute-start.16 = (f32[1920]{0:T(1024)S(1)}, f32[1920]{0:T(1024)S(1)}, u32[]{:S(2)}, u32[]{:S(2)}) collective-permute-start(f32[1920]{0:T(1024)S(1)} %get-tuple-element.80), channel_id=1, source_target_pairs={{0,4},{4,0},{2,6},{6,2},{8,12},{12,8},{10,14},{14,10},{1,5},{5,1},... | collective-permute-start | bytes 23048 | tf_op jit(solution)/shard_map/ppermute | solution.py:39
  82.2 1.6 %collective-permute-done.14 = f32[1920]{0:T(1024)S(1)} collective-permute-done((f32[1920]{0:T(1024)S(1)}, f32[1920]{0:T(1024)S(1)}, u32[]{:S(2)}, u32[]{:S(2)}) %collective-permute-start.14) | collective-permute-done | bytes 7712 | tf_op jit(solution)/shard_map/ppermute | solution.py:39
  84.0 0.2 collective-permute-done.16
  84.3 0.6 reshape.177
  (52 shorter events, 2.4 us)
Async XLA Ops:
  0.0 15.8 %copy-start = (bf16[3,3,128,128]{3,2,1,0:T(8,128)(2,1)S(1)}, bf16[3,3,128,128]{3,2,1,0:T(8,128)(2,1)}, u32[]{:S(2)}) copy-start(bf16[3,3,128,128]{3,2,1,0:T(8,128)(2,1)} %param.6) | copy-start | bytes 884740
  1.0 10.3 %collective-permute-start = (bf16[1,960,128]{2,1,0:T(8,128)(2,1)S(1)}, bf16[1,960,128]{2,1,0:T(8,128)(2,1)S(1)}, u32[]{:S(2)}, u32[]{:S(2)}) collective-permute-start(bf16[1,960,128]{2,1,0:T(8,128)(2,1)S(1)} %slice.138), channel_id=1, source_target_pairs={{0,2},{2,4},{4,6},{6,8},{8,10},{10,12},{12,14},{1,3},{3,5},{5,7},{... | collective-permute-start | bytes 737288 | tf_op jit(solution)/shard_map/ppermute | solution.py:15
  6.9 17.3 %collective-permute-start.7 = (bf16[1,960,128]{2,1,0:T(8,128)(2,1)S(1)}, bf16[1,960,128]{2,1,0:T(8,128)(2,1)S(1)}, u32[]{:S(2)}, u32[]{:S(2)}) collective-permute-start(bf16[1,960,128]{2,1,0:T(8,128)(2,1)S(1)} %slice.157), channel_id=1, source_target_pairs={{0,1},{1,2},{2,3},{3,4},{4,5},{5,6},{6,7},{7,8},{8,9},{9,10},{10,1... | collective-permute-start | bytes 737288 | tf_op jit(solution)/shard_map/ppermute | solution.py:15
  12.6 5.1 %copy-start.2 = (f32[128]{0:T(128)S(1)}, f32[128]{0:T(128)}, u32[]{:S(2)}) copy-start(f32[128]{0:T(128)} %param.7) | copy-start | bytes 1540
  13.0 11.2 %copy-start.1 = (bf16[2,960,128]{2,1,0:T(8,128)(2,1)S(1)}, bf16[2,960,128]{2,1,0:T(8,128)(2,1)}, u32[]{:S(2)}) copy-start(bf16[2,960,128]{2,1,0:T(8,128)(2,1)} %param.5) | copy-start | bytes 1474564
  17.8 11.4 %collective-permute-start.1 = (bf16[480,128]{1,0:T(8,128)(2,1)S(1)}, bf16[480,128]{1,0:T(8,128)(2,1)S(1)}, u32[]{:S(2)}, u32[]{:S(2)}) collective-permute-start(bf16[480,128]{1,0:T(8,128)(2,1)S(1)} %fusion.20), channel_id=1, source_target_pairs={{2,0},{4,2},{6,4},{8,6},{10,8},{12,10},{14,12},{3,1},{5,3},{7,5},{... | collective-permute-start | bytes 368648 | tf_op jit(solution)/shard_map/ppermute | solution.py:15
  19.1 11.6 %collective-permute-start.4 = (bf16[480,128]{1,0:T(8,128)(2,1)S(1)}, bf16[480,128]{1,0:T(8,128)(2,1)S(1)}, u32[]{:S(2)}, u32[]{:S(2)}) collective-permute-start(bf16[480,128]{1,0:T(8,128)(2,1)S(1)} %fusion.20), channel_id=1, source_target_pairs={{0,2},{2,4},{4,6},{6,8},{8,10},{10,12},{12,14},{1,3},{3,5},{5,7},{... | collective-permute-start | bytes 368648 | tf_op jit(solution)/shard_map/ppermute | solution.py:15
  29.2 7.7 %collective-permute-start.2 = (bf16[480,128]{1,0:T(8,128)(2,1)S(1)}, bf16[480,128]{1,0:T(8,128)(2,1)S(1)}, u32[]{:S(2)}, u32[]{:S(2)}) collective-permute-start(bf16[480,128]{1,0:T(8,128)(2,1)S(1)} %collective-permute-done.1), channel_id=1, source_target_pairs={{2,0},{4,2},{6,4},{8,6},{10,8},{12,10},{14,12},{3,1},{5,3},{7,5},{... | collective-permute-start | bytes 368648 | tf_op jit(solution)/shard_map/ppermute | solution.py:15
  30.7 13.7 %collective-permute-start.5 = (bf16[480,128]{1,0:T(8,128)(2,1)S(1)}, bf16[480,128]{1,0:T(8,128)(2,1)S(1)}, u32[]{:S(2)}, u32[]{:S(2)}) collective-permute-start(bf16[480,128]{1,0:T(8,128)(2,1)S(1)} %collective-permute-done.4), channel_id=1, source_target_pairs={{0,2},{2,4},{4,6},{6,8},{8,10},{10,12},{12,14},{1,3},{3,5},{5,7},{... | collective-permute-start | bytes 368648 | tf_op jit(solution)/shard_map/ppermute | solution.py:15
  36.9 9.8 %collective-permute-start.3 = (bf16[480,128]{1,0:T(8,128)(2,1)S(1)}, bf16[480,128]{1,0:T(8,128)(2,1)S(1)}, u32[]{:S(2)}, u32[]{:S(2)}) collective-permute-start(bf16[480,128]{1,0:T(8,128)(2,1)S(1)} %collective-permute-done.2), channel_id=1, source_target_pairs={{2,0},{4,2},{6,4},{8,6},{10,8},{12,10},{14,12},{3,1},{5,3},{7,5},{... | collective-permute-start | bytes 368648 | tf_op jit(solution)/shard_map/ppermute | solution.py:15
  38.4 11.3 %collective-permute-start.8 = (bf16[1,480,128]{2,1,0:T(8,128)(2,1)S(1)}, bf16[1,480,128]{2,1,0:T(8,128)(2,1)S(1)}, u32[]{:S(2)}, u32[]{:S(2)}) collective-permute-start(bf16[1,480,128]{2,1,0:T(8,128)(2,1)S(1)} %bitcast.138), channel_id=1, source_target_pairs={{0,8},{2,10},{4,12},{6,14},{8,0},{10,2},{12,4},{14,6},{1,9},{3,11}... | collective-permute-start | bytes 368648 | tf_op jit(solution)/shard_map/while/body/eval_jaxpr/ppermute | solution.py:21
  44.5 4.5 %collective-permute-start.6 = (bf16[480,128]{1,0:T(8,128)(2,1)S(1)}, bf16[480,128]{1,0:T(8,128)(2,1)S(1)}, u32[]{:S(2)}, u32[]{:S(2)}) collective-permute-start(bf16[480,128]{1,0:T(8,128)(2,1)S(1)} %collective-permute-done.5), channel_id=1, source_target_pairs={{0,2},{2,4},{4,6},{6,8},{8,10},{10,12},{12,14},{1,3},{3,5},{5,7},{... | collective-permute-start | bytes 368648 | tf_op jit(solution)/shard_map/ppermute | solution.py:15
  65.7 6.7 %collective-permute-start.10 = (f32[1920]{0:T(1024)S(1)}, f32[1920]{0:T(1024)S(1)}, u32[]{:S(2)}, u32[]{:S(2)}) collective-permute-start(f32[1920]{0:T(1024)S(1)} %get-tuple-element.63), channel_id=1, source_target_pairs={{0,2},{2,0},{4,6},{6,4},{8,10},{10,8},{12,14},{14,12},{1,3},{3,1},... | collective-permute-start | bytes 23048 | tf_op jit(solution)/shard_map/ppermute | solution.py:39
  68.7 3.8 %collective-permute-start.9 = (f32[1920]{0:T(1024)S(1)}, f32[1920]{0:T(1024)S(1)}, u32[]{:S(2)}, u32[]{:S(2)}) collective-permute-start(f32[1920]{0:T(1024)S(1)} %get-tuple-element.64), channel_id=1, source_target_pairs={{0,2},{2,0},{4,6},{6,4},{8,10},{10,8},{12,14},{14,12},{1,3},{3,1},... | collective-permute-start | bytes 23048 | tf_op jit(solution)/shard_map/ppermute | solution.py:39
  72.5 6.0 %collective-permute-start.11 = (f32[1920]{0:T(1024)S(1)}, f32[1920]{0:T(1024)S(1)}, u32[]{:S(2)}, u32[]{:S(2)}) collective-permute-start(f32[1920]{0:T(1024)S(1)} %get-tuple-element.93), channel_id=1, source_target_pairs={{0,4},{4,0},{2,6},{6,2},{8,12},{12,8},{10,14},{14,10},{1,5},{5,1},... | collective-permute-start | bytes 23048 | tf_op jit(solution)/shard_map/ppermute | solution.py:39
  76.4 3.7 %collective-permute-start.13 = (f32[1920]{0:T(1024)S(1)}, f32[1920]{0:T(1024)S(1)}, u32[]{:S(2)}, u32[]{:S(2)}) collective-permute-start(f32[1920]{0:T(1024)S(1)} %get-tuple-element.83), channel_id=1, source_target_pairs={{0,2},{2,0},{4,6},{6,4},{8,10},{10,8},{12,14},{14,12},{1,3},{3,1},... | collective-permute-start | bytes 23048 | tf_op jit(solution)/shard_map/ppermute | solution.py:39
  76.5 3.7 %collective-permute-start.15 = (f32[1920]{0:T(1024)S(1)}, f32[1920]{0:T(1024)S(1)}, u32[]{:S(2)}, u32[]{:S(2)}) collective-permute-start(f32[1920]{0:T(1024)S(1)} %get-tuple-element.82), channel_id=1, source_target_pairs={{0,2},{2,0},{4,6},{6,4},{8,10},{10,8},{12,14},{14,12},{1,3},{3,1},... | collective-permute-start | bytes 23048 | tf_op jit(solution)/shard_map/ppermute | solution.py:39
  78.4 3.8 %collective-permute-start.12 = (f32[1920]{0:T(1024)S(1)}, f32[1920]{0:T(1024)S(1)}, u32[]{:S(2)}, u32[]{:S(2)}) collective-permute-start(f32[1920]{0:T(1024)S(1)} %get-tuple-element.92), channel_id=1, source_target_pairs={{0,4},{4,0},{2,6},{6,2},{8,12},{12,8},{10,14},{14,10},{1,5},{5,1},... | collective-permute-start | bytes 23048 | tf_op jit(solution)/shard_map/ppermute | solution.py:39
  80.2 3.7 %collective-permute-start.14 = (f32[1920]{0:T(1024)S(1)}, f32[1920]{0:T(1024)S(1)}, u32[]{:S(2)}, u32[]{:S(2)}) collective-permute-start(f32[1920]{0:T(1024)S(1)} %get-tuple-element.81), channel_id=1, source_target_pairs={{0,4},{4,0},{2,6},{6,2},{8,12},{12,8},{10,14},{14,10},{1,5},{5,1},... | collective-permute-start | bytes 23048 | tf_op jit(solution)/shard_map/ppermute | solution.py:39
  80.6 3.7 %collective-permute-start.16 = (f32[1920]{0:T(1024)S(1)}, f32[1920]{0:T(1024)S(1)}, u32[]{:S(2)}, u32[]{:S(2)}) collective-permute-start(f32[1920]{0:T(1024)S(1)} %get-tuple-element.80), channel_id=1, source_target_pairs={{0,4},{4,0},{2,6},{6,2},{8,12},{12,8},{10,14},{14,10},{1,5},{5,1},... | collective-permute-start | bytes 23048 | tf_op jit(solution)/shard_map/ppermute | solution.py:39
where the time goes:
time: 85.3 us; the launch traced here: 84.9 us
  starting transfers between devices  40.1 us (47%)
  matrix products  14.5 us (17%)
  local copies, waits for them, and re-layouts  10 us (12%)
  waiting for transfers between devices  9.27 us (11%)
  blocking collectives  7.45 us (9%)
  other arithmetic  2.93 us (3%)
    ppermute x8, starting transfers between devices, passed_along(): return lax.ppermute(block, axis, route)  22.9 us
    ppermute x8, starting transfers between devices, swapped(): return lax.ppermute(block, axis, route)  11.1 us
    all_gather x4, blocking collectives, merged(): pieces = jax.tree.map(lambda part: lax.all_gather(part, axis), value)  7.45 us
    slice x18, local copies, waits for them, and re-layouts, convolve(): padded[tap_row:tap_row + 2 * out_rows:2, tap_col:tap_col + 2 * out_cols:2]  7.1 us
    ppermute x1, starting transfers between devices, shifted(): return lax.ppermute(value, axis, pairs)  6.07 us
    ppermute x8, waiting for transfers between devices, passed_along(): return lax.ppermute(block, axis, route)  5.72 us
    dot_general x2, matrix products, absorb(): jnp.dot(weights, column_x, precision=lax.Precision.HIGHEST)  5.02 us
    dot_general x2, matrix products, absorb(): jnp.dot(weights, row_y, precision=lax.Precision.HIGHEST)  5.02 us
  transfers between devices with their start and end apart: 17, of which 7 were waited for; matrix products, arithmetic and copies ran while one was open for 16% of the time, Pallas kernels for 0%

commit v1 on v0

v1 whole, which is shorter than its diff:
```python
import functools
import math

import jax
import jax.numpy as jnp
from jax import lax
from jax.experimental import pallas as pl
from jax.experimental.pallas import tpu as pltpu
from jax.sharding import PartitionSpec as P

CELL = 0.0625
LOG2E = math.log2(math.e)
VMEM_LIMIT = 32 * 1024 * 1024


def sent(value, axis, target_of):
    count = lax.axis_size(axis)
    route = [(i, target_of(i)) for i in range(count)]
    route = [(i, to) for i, to in route if 0 <= to < count]
    return lax.ppermute(value, axis, route)


def column_taps(row, stage):
    out_cols = row.shape[0] // 2
    stage[pl.ds(8, row.shape[0]), :] = row.astype(jnp.float32)
    return [
        stage[pl.ds(7 + tap, out_cols, stride=2), :].astype(jnp.bfloat16) for tap in range(3)
    ]


def tap_row_sum(row, weight_ref, tap_row, stage):
    taps = column_taps(row, stage)
    total = None
    for tap_col in range(3):
        term = jnp.dot(
            taps[tap_col], weight_ref[tap_row, tap_col], preferred_element_type=jnp.float32
        )
        total = term if total is None else total + term
    return total


def rim_kernel(query_ref, target_ref, weight_ref, query_rim_ref, target_rim_ref, *stages):
    for stage in stages:
        stage[pl.ds(0, 8), :] = jnp.zeros((8, stage.shape[1]), jnp.float32)
    pairs = ((query_ref, query_rim_ref), (target_ref, target_rim_ref))
    for (frame_ref, rim_ref), stage in zip(pairs, stages):
        rim_ref[...] = tap_row_sum(frame_ref[0], weight_ref, 0, stage).astype(rim_ref.dtype)


def rim_partials(query_input, target_input, conv_weight):
    rows, cols, channels = query_input.shape
    out_channels = conv_weight.shape[3]
    rim = jax.ShapeDtypeStruct((cols // 2, out_channels), jnp.bfloat16)
    last_row = pl.BlockSpec((1, cols, channels), lambda i: (rows - 1, 0, 0))
    first_taps = pl.BlockSpec((1,) + conv_weight.shape[1:], lambda i: (0, 0, 0, 0))
    whole = pl.BlockSpec((cols // 2, out_channels), lambda i: (0, 0))
    return pl.pallas_call(
        rim_kernel,
        grid=(1,),
        out_shape=(rim, rim),
        in_specs=[last_row, last_row, first_taps],
        out_specs=(whole, whole),
        scratch_shapes=[pltpu.VMEM((cols + 8, channels), jnp.float32)] * 2,
        compiler_params=pltpu.CompilerParams(vmem_limit_bytes=VMEM_LIMIT),
        name="rim_partials",
    )(query_input, target_input, conv_weight)


def own_kernel(query_ref, target_ref, weight_ref, bias_ref, query_out, target_out, *stages):
    for stage in stages:
        stage[pl.ds(0, 8), :] = jnp.zeros((8, stage.shape[1]), jnp.float32)
    for which, (frame_ref, out_ref) in enumerate(((query_ref, query_out), (target_ref, target_out))):
        total = bias_ref[...]
        for tap_row in (1, 2):
            total = total + tap_row_sum(
                frame_ref[tap_row - 1], weight_ref, tap_row, stages[2 * which + tap_row - 1]
            )
        out_ref[...] = total


def own_partials(query_input, target_input, conv_weight, conv_bias):
    rows, cols, channels = query_input.shape
    out_channels = conv_weight.shape[3]
    part = jax.ShapeDtypeStruct((cols // 2, out_channels), jnp.float32)
    flops = 2 * 2 * 6 * (cols // 2) * channels * out_channels
    return pl.pallas_call(
        own_kernel,
        out_shape=(part, part),
        scratch_shapes=[pltpu.VMEM((cols + 8, channels), jnp.float32)] * 4,
        compiler_params=pltpu.CompilerParams(vmem_limit_bytes=VMEM_LIMIT),
        cost_estimate=pl.CostEstimate(flops=flops, bytes_accessed=1 << 22, transcendentals=0),
        name="own_partials",
    )(query_input, target_input, conv_weight, conv_bias.reshape(1, out_channels))


def match_kernel(members, shares, row_y_ref, *refs):
    query_refs = refs[:members]
    target_refs = refs[members : members + shares]
    out_refs = refs[members + shares : 2 * members + shares]
    scores_refs = refs[2 * members + shares :]
    channels = query_refs[0].shape[1]
    row_width = target_refs[0].shape[0]
    lanes = query_refs[0].shape[0]
    steps = row_width // 8
    scale = LOG2E / math.sqrt(channels)
    for member in range(members):
        highest = None
        for share in range(shares):
            scores_ref = scores_refs[(member % 2) * shares + share]
            scores_ref[...] = lax.dot_general(
                target_refs[share][...],
                query_refs[member][...],
                (((1,), (1,)), ((), ())),
                preferred_element_type=jnp.float32,
            )
            for step in range(steps):
                block = scores_ref[pl.ds(8 * step, 8), :]
                highest = block if highest is None else jnp.maximum(highest, block)
        highest = jnp.max(highest, axis=0, keepdims=True)
        spread = jnp.broadcast_to(highest, (8, lanes))
        weight_sum = sum_x = sum_y = None
        offset = lax.broadcasted_iota(jnp.int32, (8, lanes), 0).astype(jnp.float32)
        for share in range(shares):
            scores_ref = scores_refs[(member % 2) * shares + share]
            plain = jnp.zeros((8, lanes), jnp.float32)
            stacked = jnp.zeros((8, lanes), jnp.float32)
            for step in reversed(range(steps)):
                weights = jnp.exp2((scores_ref[pl.ds(8 * step, 8), :] - spread) * scale)
                if step == 0:
                    plain = plain + weights
                else:
                    plain = plain + weights
                    stacked = stacked + plain
            part_x = jnp.sum(8.0 * stacked + offset * plain, axis=0, keepdims=True) * CELL
            part_sum = jnp.sum(plain, axis=0, keepdims=True)
            part_y = part_sum * row_y_ref[share]
            if weight_sum is None:
                weight_sum, sum_x, sum_y = part_sum, part_x, part_y
            else:
                weight_sum, sum_x, sum_y = weight_sum + part_sum, sum_x + part_x, sum_y + part_y
        out_refs[member][...] = jnp.concatenate([highest, weight_sum, sum_x, sum_y], axis=0)


def match(queries, targets, row_y):
    members, shares = len(queries), len(targets)
    lanes, channels = queries[0].shape
    row_width = targets[0].shape[0]
    vmem = pl.BlockSpec(memory_space=pltpu.VMEM)
    return pl.pallas_call(
        functools.partial(match_kernel, members, shares),
        out_shape=(jax.ShapeDtypeStruct((4, lanes), jnp.float32),) * members,
        in_specs=[pl.BlockSpec(memory_space=pltpu.SMEM)] + [vmem] * (members + shares),
        out_specs=(vmem,) * members,
        scratch_shapes=[pltpu.VMEM((row_width, lanes), jnp.float32)] * (2 * shares),
        compiler_params=pltpu.CompilerParams(vmem_limit_bytes=VMEM_LIMIT),
        cost_estimate=pl.CostEstimate(
            flops=2 * members * shares * lanes * row_width * channels,
            bytes_accessed=1 << 22,
            transcendentals=members * shares * lanes * row_width,
        ),
        name="match",
    )(row_y, *queries, *targets)


def combined(first, second, scale):
    highest = jnp.maximum(first[..., :1, :], second[..., :1, :])
    first_scale = jnp.exp2((first[..., :1, :] - highest) * scale)
    second_scale = jnp.exp2((second[..., :1, :] - highest) * scale)
    sums = first[..., 1:, :] * first_scale + second[..., 1:, :] * second_scale
    return jnp.concatenate([highest, sums], axis=-2)


def on_device(query_input, target_input, conv_weight, conv_bias):
    query_slot = lax.axis_index("query")
    core_slot = lax.axis_index("target")
    core_count = lax.axis_size("target")
    query_total = lax.axis_size("query")
    row_width = query_input.shape[1] // 2
    channels = conv_weight.shape[3]

    query_rim, target_rim = rim_partials(query_input, target_input, conv_weight)
    query_rim = sent(query_rim, "query", lambda i: i + 1)
    target_rim = sent(target_rim, ("query", "target"), lambda i: i + 1)
    query_part, target_part = own_partials(query_input, target_input, conv_weight, conv_bias)
    queries = (query_part + query_rim.astype(jnp.float32)).astype(jnp.bfloat16)
    targets = (target_part + target_rim.astype(jnp.float32)).astype(jnp.bfloat16)

    block_queries = [queries] + [
        sent(queries, "query", lambda i, member=member: i ^ member) for member in (1, 2, 3)
    ]
    shares = [targets]
    for _ in range(query_total // 4 - 1):
        shares.append(sent(shares[-1], "query", lambda i: (i + 4) % query_total))
    share_slots = [(query_slot - 4 * hop) % query_total for hop in range(query_total // 4)]
    row_y = jnp.stack(
        [(slot * core_count + core_slot).astype(jnp.float32) * CELL for slot in share_slots]
    )
    states = match(block_queries, shares, row_y)

    scale = LOG2E / math.sqrt(channels)
    near = sent(jnp.concatenate([states[1], states[3]], axis=0), "query", lambda i: i ^ 1)
    own = combined(states[0], near[:4], scale)
    other = combined(states[2], near[4:], scale)
    own = combined(own, sent(other, "query", lambda i: i ^ 2), scale)
    total = combined(own, sent(own, "target", lambda i: i ^ 1), scale)
    columns = jnp.arange(row_width, dtype=jnp.int32).astype(jnp.float32) * CELL
    flow_x = total[2] / total[1] - columns
    flow_y = total[3] / total[1] - query_slot.astype(jnp.float32) * CELL
    return jnp.stack([flow_x, flow_y]).reshape(2, 1, row_width)


def solution(mesh):
    placed = (
        P(("groups", "query"), None, None),
        P(("groups", "query", "target"), None, None),
        P(),
        P(),
    )
    return jax.shard_map(
        on_device,
        mesh=mesh,
        in_specs=placed,
        out_specs=P(None, ("groups", "query"), None),
        check_vma=False,
    )
```

time: 85.3 us -> 37.8 us (0.44)
  starting transfers between devices: 40.1 us -> 15.8 us
  matrix products: 14.5 us -> 0 us
  blocking collectives: 7.45 us -> 0 us
  local copies, waits for them, and re-layouts: 10 us -> 3.62 us
  waiting for transfers between devices: 9.27 us -> 14 us
  Pallas kernels: 0 us -> 3.61 us
  other arithmetic: 2.93 us -> 0.29 us
    ppermute x17 -> x9, starting transfers between devices: 40.1 us -> 15.8 us  [sent(): return lax.ppermute(value, axis, route)]
    dot_general x24 -> x0, matrix products: 14.5 us -> none  [the longest x2 5.02 us: absorb(): jnp.dot(weights, column_x, precision=lax.Precision.HIGHEST)]
    slice x24 -> x0, local copies, waits for them, and re-layouts: 9.23 us -> none  [the longest x18 7.1 us: convolve(): padded[tap_row:tap_row + 2 * out_rows:2, tap_col:tap_col + 2 * out_cols:2]]
    all_gather x4 -> x0, blocking collectives: 7.45 us -> none  [merged(): pieces = jax.tree.map(lambda part: lax.all_gather(part, axis), value)]
    ppermute x17 -> x9, waiting for transfers between devices: 9.27 us -> 14 us  [sent(): return lax.ppermute(value, axis, route)]
    pallas_call x0 -> x3, Pallas kernels: none -> 3.61 us  [the longest x1 2.72 us: match(): pl.pallas_call(functools.partial(match_kernel, members, shares), out_shap...]
    unnamed x14 -> x8, local copies, waits for them, and re-layouts: 0.13 us -> 3.03 us
    concatenate x2 -> x3, other arithmetic: 1.42 us -> 0.03 us  [the longest x2 0.02 us: combined(): return jnp.concatenate([highest, sums], axis=-2)]
  transfers between devices with their start and end apart: 17 -> 9, of which waited for: 7 -> 6; matrix products, arithmetic and copies ran while one was open for 16% -> 0% of each run, Pallas kernels for 0% -> 1%
where the time goes in v1:
time: 37.8 us; the launch traced here: 37.5 us
  starting transfers between devices  15.8 us (42%)
  waiting for transfers between devices  14 us (37%)
  local copies, waits for them, and re-layouts  3.62 us (10%)
  Pallas kernels  3.61 us (10%)
    ppermute x9, starting transfers between devices, sent(): return lax.ppermute(value, axis, route)  15.8 us
    ppermute x9, waiting for transfers between devices, sent(): return lax.ppermute(value, axis, route)  14 us
    unnamed x8, local copies, waits for them, and re-layouts  3.03 us
    pallas_call x1, Pallas kernels, match(): pl.pallas_call(functools.partial(match_kernel, members, shares), out_shap...  2.72 us
  transfers between devices with their start and end apart: 9, of which 6 were waited for; matrix products, arithmetic and copies ran while one was open for 0% of the time, Pallas kernels for 1%

profile of v1, /device:TPU:0, one launch (start us, length us, event | category | flops | bytes accessed | tf_op | source)
XLA Modules:
  0.0 37.5 jit_solution(16318046491147676108)
XLA Ops:
  0.0 0.0 copy-start
  0.0 1.0 %copy-done = bf16[2,960,128]{2,1,0:T(8,128)(2,1)S(1)} copy-done((bf16[2,960,128]{2,1,0:T(8,128)(2,1)S(1)}, bf16[2,960,128]{2,1,0:T(8,128)(2,1)}, u32[]{:S(2)}) %copy-start) | copy-done | bytes 491544
  1.0 0.0 copy-start.1
  1.0 1.0 %copy-done.1 = bf16[2,960,128]{2,1,0:T(8,128)(2,1)S(1)} copy-done((bf16[2,960,128]{2,1,0:T(8,128)(2,1)S(1)}, bf16[2,960,128]{2,1,0:T(8,128)(2,1)}, u32[]{:S(2)}) %copy-start.1) | copy-done | bytes 491544
  2.1 0.0 copy-start.2
  2.1 1.0 %copy-done.2 = bf16[3,3,128,128]{3,2,1,0:T(8,128)(2,1)S(1)} copy-done((bf16[3,3,128,128]{3,2,1,0:T(8,128)(2,1)S(1)}, bf16[3,3,128,128]{3,2,1,0:T(8,128)(2,1)}, u32[]{:S(2)}) %copy-start.2) | copy-done | bytes 294936
  3.0 0.3 rim_partials.1
  3.4 2.4 %collective-permute-start.4 = (bf16[480,128]{1,0:T(8,128)(2,1)S(1)}, bf16[480,128]{1,0:T(8,128)(2,1)S(1)}, u32[]{:S(2)}, u32[]{:S(2)}) collective-permute-start(bf16[480,128]{1,0:T(8,128)(2,1)S(1)} %get-tuple-element.16), channel_id=1, source_target_pairs={{0,1},{1,2},{2,3},{3,4},{4,5},{5,6},{6,7},{7,8},{8,9},{9,10},{10,1... | collective-permute-start | bytes 368648 | tf_op jit(solution)/shard_map/ppermute | solution.py:20
  5.8 0.0 copy-start.3
  5.8 4.4 %collective-permute-start = (bf16[480,128]{1,0:T(8,128)(2,1)S(1)}, bf16[480,128]{1,0:T(8,128)(2,1)S(1)}, u32[]{:S(2)}, u32[]{:S(2)}) collective-permute-start(bf16[480,128]{1,0:T(8,128)(2,1)S(1)} %get-tuple-element.14), channel_id=1, source_target_pairs={{0,2},{2,4},{4,6},{6,8},{8,10},{10,12},{12,14},{1,3},{3,5},{5,7},{... | collective-permute-start | bytes 368648 | tf_op jit(solution)/shard_map/ppermute | solution.py:20
  10.2 0.0 copy-done.3
  10.2 0.5 %own_partials.1 = (f32[480,128]{1,0:T(8,128)S(1)}, f32[480,128]{1,0:T(8,128)S(1)}) custom-call(bf16[2,960,128]{2,1,0:T(8,128)(2,1)S(1)} %copy-done, bf16[2,960,128]{2,1,0:T(8,128)(2,1)S(1)} %copy-done.1, bf16[3,3,128,128]{3,2,1,0:T(8,128)(2,1)S(1)} %copy-done.2, f32[1,128]{1,0:T(1,128)S(1)} %bitcast.13), custom_call_target="tpu_custom_call" | custom-call | flops 188743680 | bytes 4194304 | tf_op jit(solution)/shard_map/own_partials/pallas_call | solution.py:86
  10.8 0.0 collective-permute-done.4
  10.8 3.8 %collective-permute-start.5 = (bf16[480,128]{1,0:T(8,128)(2,1)S(1)}, bf16[480,128]{1,0:T(8,128)(2,1)S(1)}, u32[]{:S(2)}, u32[]{:S(2)}) collective-permute-start(bf16[480,128]{1,0:T(8,128)(2,1)S(1)} %add_convert_fusion.refs_4_), channel_id=1, source_target_pairs={{0,8},{2,10},{4,12},{6,14},{8,0},{10,2},{12,4},{14,6},{1,9},{3,11}... | collective-permute-start | bytes 368648 | tf_op jit(solution)/shard_map/ppermute | solution.py:20
  14.6 0.0 collective-permute-done
  14.7 2.2 %collective-permute-start.3 = (bf16[480,128]{1,0:T(8,128)(2,1)S(1)}, bf16[480,128]{1,0:T(8,128)(2,1)S(1)}, u32[]{:S(2)}, u32[]{:S(2)}) collective-permute-start(bf16[480,128]{1,0:T(8,128)(2,1)S(1)} %add_convert_fusion.1.refs_0_), channel_id=1, source_target_pairs={{0,6},{2,4},{4,2},{6,0},{8,14},{10,12},{12,10},{14,8},{1,7},{3,5},... | collective-permute-start | bytes 368648 | tf_op jit(solution)/shard_map/ppermute | solution.py:20
  16.9 0.4 %collective-permute-start.2 = (bf16[480,128]{1,0:T(8,128)(2,1)S(1)}, bf16[480,128]{1,0:T(8,128)(2,1)S(1)}, u32[]{:S(2)}, u32[]{:S(2)}) collective-permute-start(bf16[480,128]{1,0:T(8,128)(2,1)S(1)} %add_convert_fusion.1.refs_0_), channel_id=1, source_target_pairs={{0,4},{2,6},{4,0},{6,2},{8,12},{10,14},{12,8},{14,10},{1,5},{3,7},... | collective-permute-start | bytes 368648 | tf_op jit(solution)/shard_map/ppermute | solution.py:20
  17.3 1.0 %collective-permute-start.1 = (bf16[480,128]{1,0:T(8,128)(2,1)S(1)}, bf16[480,128]{1,0:T(8,128)(2,1)S(1)}, u32[]{:S(2)}, u32[]{:S(2)}) collective-permute-start(bf16[480,128]{1,0:T(8,128)(2,1)S(1)} %add_convert_fusion.1.refs_0_), channel_id=1, source_target_pairs={{0,2},{2,0},{4,6},{6,4},{8,10},{10,8},{12,14},{14,12},{1,3},{3,1},... | collective-permute-start | bytes 368648 | tf_op jit(solution)/shard_map/ppermute | solution.py:20
  18.3 0.1 pad_maximum_fusion.3.row_y_ref
  18.4 2.7 %collective-permute-done.5.refs_5_ = bf16[480,128]{1,0:T(8,128)(2,1)S(1)} collective-permute-done((bf16[480,128]{1,0:T(8,128)(2,1)S(1)}, bf16[480,128]{1,0:T(8,128)(2,1)S(1)}, u32[]{:S(2)}, u32[]{:S(2)}) %collective-permute-start.5) | collective-permute-done | bytes 122912 | tf_op jit(solution)/shard_map/ppermute | solution.py:20
  21.1 1.6 %collective-permute-done.3.refs_3_ = bf16[480,128]{1,0:T(8,128)(2,1)S(1)} collective-permute-done((bf16[480,128]{1,0:T(8,128)(2,1)S(1)}, bf16[480,128]{1,0:T(8,128)(2,1)S(1)}, u32[]{:S(2)}, u32[]{:S(2)}) %collective-permute-start.3) | collective-permute-done | bytes 122912 | tf_op jit(solution)/shard_map/ppermute | solution.py:20
  22.7 2.5 %collective-permute-done.2.refs_2_ = bf16[480,128]{1,0:T(8,128)(2,1)S(1)} collective-permute-done((bf16[480,128]{1,0:T(8,128)(2,1)S(1)}, bf16[480,128]{1,0:T(8,128)(2,1)S(1)}, u32[]{:S(2)}, u32[]{:S(2)}) %collective-permute-start.2) | collective-permute-done | bytes 122912 | tf_op jit(solution)/shard_map/ppermute | solution.py:20
  25.2 0.0 collective-permute-done.1.refs_1_
  25.2 2.7 %match.1 = (f32[4,480]{1,0:T(4,128)S(1)}, f32[4,480]{1,0:T(4,128)S(1)}, f32[4,480]{1,0:T(4,128)S(1)}, f32[4,480]{1,0:T(4,128)S(1)}) custom-call(f32[2]{0:T(128)S(1)} %pad_maximum_fusion.3.row_y_ref, bf16[480,128]{1,0:T(8,128)(2,1)S(1)} %add_convert_fusion.1.refs_0_, bf16[480,128]{1,0:T(8,128)(2,1)S(1)} %collective-permute-done.1.refs_1_, ...), custom_call_target="tpu_custom_call" | custom-call | flops 471859200 | bytes 4194304 | tf_op jit(solution)/shard_map/match/pallas_call | solution.py:149
  27.9 0.4 %collective-permute-start.6 = (f32[8,480]{1,0:T(8,128)S(1)}, f32[8,480]{1,0:T(8,128)S(1)}, u32[]{:S(2)}, u32[]{:S(2)}) collective-permute-start(f32[8,480]{1,0:T(8,128)S(1)} %pad_maximum_fusion), channel_id=1, source_target_pairs={{0,2},{2,0},{4,6},{6,4},{8,10},{10,8},{12,14},{14,12},{1,3},{3,1},... | collective-permute-start | bytes 46088 | tf_op jit(solution)/shard_map/ppermute | solution.py:20
  28.3 3.4 %collective-permute-done.6 = f32[8,480]{1,0:T(8,128)S(1)} collective-permute-done((f32[8,480]{1,0:T(8,128)S(1)}, f32[8,480]{1,0:T(8,128)S(1)}, u32[]{:S(2)}, u32[]{:S(2)}) %collective-permute-start.6) | collective-permute-done | bytes 15392 | tf_op jit(solution)/shard_map/ppermute | solution.py:20
  31.8 1.1 %collective-permute-start.7 = (f32[4,480]{1,0:T(4,128)S(1)}, f32[4,480]{1,0:T(4,128)S(1)}, u32[]{:S(2)}, u32[]{:S(2)}) collective-permute-start(f32[4,480]{1,0:T(4,128)S(1)} %pad_maximum_fusion.1), channel_id=1, source_target_pairs={{0,4},{2,6},{4,0},{6,2},{8,12},{10,14},{12,8},{14,10},{1,5},{3,7},... | collective-permute-start | bytes 23048 | tf_op jit(solution)/shard_map/ppermute | solution.py:20
  32.9 2.6 %collective-permute-done.7 = f32[4,480]{1,0:T(4,128)S(1)} collective-permute-done((f32[4,480]{1,0:T(4,128)S(1)}, f32[4,480]{1,0:T(4,128)S(1)}, u32[]{:S(2)}, u32[]{:S(2)}) %collective-permute-start.7) | collective-permute-done | bytes 7712 | tf_op jit(solution)/shard_map/ppermute | solution.py:20
  35.6 0.1 collective-permute-start.8
  35.7 1.2 %collective-permute-done.8 = f32[4,480]{1,0:T(4,128)S(1)} collective-permute-done((f32[4,480]{1,0:T(4,128)S(1)}, f32[4,480]{1,0:T(4,128)S(1)}, u32[]{:S(2)}, u32[]{:S(2)}) %collective-permute-start.8) | collective-permute-done | bytes 7712 | tf_op jit(solution)/shard_map/ppermute | solution.py:20
  36.9 0.6 %copy.5 = f32[2,1,480]{2,1,0:T(1,128)} copy(f32[2,1,480]{2,0,1:T(2,128)S(1)} %maximum_bitcast_fusion) | data formatting | bytes 7680 | tf_op jit(solution)/shard_map/reshape | solution.py:209
  (15 shorter events, 0.2 us)
Async XLA Ops:
  0.0 1.0 %copy-start = (bf16[2,960,128]{2,1,0:T(8,128)(2,1)S(1)}, bf16[2,960,128]{2,1,0:T(8,128)(2,1)}, u32[]{:S(2)}) copy-start(bf16[2,960,128]{2,1,0:T(8,128)(2,1)} %query_ref.3) | copy-start | bytes 1474564
  1.0 1.0 %copy-start.1 = (bf16[2,960,128]{2,1,0:T(8,128)(2,1)S(1)}, bf16[2,960,128]{2,1,0:T(8,128)(2,1)}, u32[]{:S(2)}) copy-start(bf16[2,960,128]{2,1,0:T(8,128)(2,1)} %target_ref.3) | copy-start | bytes 1474564
  2.1 1.0 %copy-start.2 = (bf16[3,3,128,128]{3,2,1,0:T(8,128)(2,1)S(1)}, bf16[3,3,128,128]{3,2,1,0:T(8,128)(2,1)}, u32[]{:S(2)}) copy-start(bf16[3,3,128,128]{3,2,1,0:T(8,128)(2,1)} %weight_ref.3) | copy-start | bytes 884740
  3.4 7.4 %collective-permute-start.4 = (bf16[480,128]{1,0:T(8,128)(2,1)S(1)}, bf16[480,128]{1,0:T(8,128)(2,1)S(1)}, u32[]{:S(2)}, u32[]{:S(2)}) collective-permute-start(bf16[480,128]{1,0:T(8,128)(2,1)S(1)} %get-tuple-element.16), channel_id=1, source_target_pairs={{0,1},{1,2},{2,3},{3,4},{4,5},{5,6},{6,7},{7,8},{8,9},{9,10},{10,1... | collective-permute-start | bytes 368648 | tf_op jit(solution)/shard_map/ppermute | solution.py:20
  5.8 4.5 %copy-start.3 = (f32[128]{0:T(128)S(1)}, f32[128]{0:T(128)}, u32[]{:S(2)}) copy-start(f32[128]{0:T(128)} %param.7) | copy-start | bytes 1540
  5.8 8.9 %collective-permute-start = (bf16[480,128]{1,0:T(8,128)(2,1)S(1)}, bf16[480,128]{1,0:T(8,128)(2,1)S(1)}, u32[]{:S(2)}, u32[]{:S(2)}) collective-permute-start(bf16[480,128]{1,0:T(8,128)(2,1)S(1)} %get-tuple-element.14), channel_id=1, source_target_pairs={{0,2},{2,4},{4,6},{6,8},{8,10},{10,12},{12,14},{1,3},{3,5},{5,7},{... | collective-permute-start | bytes 368648 | tf_op jit(solution)/shard_map/ppermute | solution.py:20
  10.8 10.3 %collective-permute-start.5 = (bf16[480,128]{1,0:T(8,128)(2,1)S(1)}, bf16[480,128]{1,0:T(8,128)(2,1)S(1)}, u32[]{:S(2)}, u32[]{:S(2)}) collective-permute-start(bf16[480,128]{1,0:T(8,128)(2,1)S(1)} %add_convert_fusion.refs_4_), channel_id=1, source_target_pairs={{0,8},{2,10},{4,12},{6,14},{8,0},{10,2},{12,4},{14,6},{1,9},{3,11}... | collective-permute-start | bytes 368648 | tf_op jit(solution)/shard_map/ppermute | solution.py:20
  14.7 8.0 %collective-permute-start.3 = (bf16[480,128]{1,0:T(8,128)(2,1)S(1)}, bf16[480,128]{1,0:T(8,128)(2,1)S(1)}, u32[]{:S(2)}, u32[]{:S(2)}) collective-permute-start(bf16[480,128]{1,0:T(8,128)(2,1)S(1)} %add_convert_fusion.1.refs_0_), channel_id=1, source_target_pairs={{0,6},{2,4},{4,2},{6,0},{8,14},{10,12},{12,10},{14,8},{1,7},{3,5},... | collective-permute-start | bytes 368648 | tf_op jit(solution)/shard_map/ppermute | solution.py:20
  16.9 8.3 %collective-permute-start.2 = (bf16[480,128]{1,0:T(8,128)(2,1)S(1)}, bf16[480,128]{1,0:T(8,128)(2,1)S(1)}, u32[]{:S(2)}, u32[]{:S(2)}) collective-permute-start(bf16[480,128]{1,0:T(8,128)(2,1)S(1)} %add_convert_fusion.1.refs_0_), channel_id=1, source_target_pairs={{0,4},{2,6},{4,0},{6,2},{8,12},{10,14},{12,8},{14,10},{1,5},{3,7},... | collective-permute-start | bytes 368648 | tf_op jit(solution)/shard_map/ppermute | solution.py:20
  17.3 7.8 %collective-permute-start.1 = (bf16[480,128]{1,0:T(8,128)(2,1)S(1)}, bf16[480,128]{1,0:T(8,128)(2,1)S(1)}, u32[]{:S(2)}, u32[]{:S(2)}) collective-permute-start(bf16[480,128]{1,0:T(8,128)(2,1)S(1)} %add_convert_fusion.1.refs_0_), channel_id=1, source_target_pairs={{0,2},{2,0},{4,6},{6,4},{8,10},{10,8},{12,14},{14,12},{1,3},{3,1},... | collective-permute-start | bytes 368648 | tf_op jit(solution)/shard_map/ppermute | solution.py:20
  27.9 3.8 %collective-permute-start.6 = (f32[8,480]{1,0:T(8,128)S(1)}, f32[8,480]{1,0:T(8,128)S(1)}, u32[]{:S(2)}, u32[]{:S(2)}) collective-permute-start(f32[8,480]{1,0:T(8,128)S(1)} %pad_maximum_fusion), channel_id=1, source_target_pairs={{0,2},{2,0},{4,6},{6,4},{8,10},{10,8},{12,14},{14,12},{1,3},{3,1},... | collective-permute-start | bytes 46088 | tf_op jit(solution)/shard_map/ppermute | solution.py:20
  31.8 3.7 %collective-permute-start.7 = (f32[4,480]{1,0:T(4,128)S(1)}, f32[4,480]{1,0:T(4,128)S(1)}, u32[]{:S(2)}, u32[]{:S(2)}) collective-permute-start(f32[4,480]{1,0:T(4,128)S(1)} %pad_maximum_fusion.1), channel_id=1, source_target_pairs={{0,4},{2,6},{4,0},{6,2},{8,12},{10,14},{12,8},{14,10},{1,5},{3,7},... | collective-permute-start | bytes 23048 | tf_op jit(solution)/shard_map/ppermute | solution.py:20
  35.6 1.2 %collective-permute-start.8 = (f32[4,480]{1,0:T(4,128)S(1)}, f32[4,480]{1,0:T(4,128)S(1)}, u32[]{:S(2)}, u32[]{:S(2)}) collective-permute-start(f32[4,480]{1,0:T(4,128)S(1)} %pad_maximum_fusion.2), channel_id=1, source_target_pairs={{0,1},{1,0},{2,3},{3,2},{4,5},{5,4},{6,7},{7,6},{8,9},{9,8},{10,11... | collective-permute-start | bytes 23048 | tf_op jit(solution)/shard_map/ppermute | solution.py:20

commit v2 on v1

--- a/solution.py
+++ b/solution.py
@@ -39,41 +39,65 @@
     return total
 
 
-def rim_kernel(query_ref, target_ref, weight_ref, query_rim_ref, target_rim_ref, *stages):
+def rim_kernel(query_hbm, target_hbm, weight_hbm, rim_ref, rows_ref, taps_ref, sems, *stages):
+    last = query_hbm.shape[0] - 1
+    out_cols = rim_ref.shape[0] // 2
+    copies = [
+        pltpu.make_async_copy(weight_hbm.at[pl.ds(0, 1)], taps_ref, sems.at[2]),
+        pltpu.make_async_copy(target_hbm.at[last], rows_ref.at[0], sems.at[0]),
+        pltpu.make_async_copy(query_hbm.at[last], rows_ref.at[1], sems.at[1]),
+    ]
+    for copy in copies:
+        copy.start()
     for stage in stages:
         stage[pl.ds(0, 8), :] = jnp.zeros((8, stage.shape[1]), jnp.float32)
-    pairs = ((query_ref, query_rim_ref), (target_ref, target_rim_ref))
-    for (frame_ref, rim_ref), stage in zip(pairs, stages):
-        rim_ref[...] = tap_row_sum(frame_ref[0], weight_ref, 0, stage).astype(rim_ref.dtype)
+    for copy in copies:
+        copy.wait()
+    for which, stage in enumerate(stages):
+        rim_ref[pl.ds(which * out_cols, out_cols), :] = tap_row_sum(
+            rows_ref[which], taps_ref, 0, stage
+        ).astype(rim_ref.dtype)
 
 
 def rim_partials(query_input, target_input, conv_weight):
-    rows, cols, channels = query_input.shape
+    _, cols, channels = query_input.shape
     out_channels = conv_weight.shape[3]
-    rim = jax.ShapeDtypeStruct((cols // 2, out_channels), jnp.bfloat16)
-    last_row = pl.BlockSpec((1, cols, channels), lambda i: (rows - 1, 0, 0))
-    first_taps = pl.BlockSpec((1,) + conv_weight.shape[1:], lambda i: (0, 0, 0, 0))
-    whole = pl.BlockSpec((cols // 2, out_channels), lambda i: (0, 0))
+    hbm = pl.BlockSpec(memory_space=pltpu.HBM)
     return pl.pallas_call(
         rim_kernel,
-        grid=(1,),
-        out_shape=(rim, rim),
-        in_specs=[last_row, last_row, first_taps],
-        out_specs=(whole, whole),
-        scratch_shapes=[pltpu.VMEM((cols + 8, channels), jnp.float32)] * 2,
+        out_shape=jax.ShapeDtypeStruct((cols, out_channels), jnp.bfloat16),
+        in_specs=[hbm] * 3,
+        out_specs=pl.BlockSpec(memory_space=pltpu.VMEM),
+        scratch_shapes=[
+            pltpu.VMEM((2, cols, channels), jnp.bfloat16),
+            pltpu.VMEM((1,) + conv_weight.shape[1:], jnp.bfloat16),
+            pltpu.SemaphoreType.DMA((3,)),
+        ]
+        + [pltpu.VMEM((cols + 8, channels), jnp.float32)] * 2,
         compiler_params=pltpu.CompilerParams(vmem_limit_bytes=VMEM_LIMIT),
         name="rim_partials",
     )(query_input, target_input, conv_weight)
 
 
-def own_kernel(query_ref, target_ref, weight_ref, bias_ref, query_out, target_out, *stages):
+def own_kernel(
+    query_hbm, target_hbm, weight_hbm, bias_ref, query_out, target_out, frames, taps_ref, sems, *stages
+):
+    copies = [
+        pltpu.make_async_copy(query_hbm, frames.at[0], sems.at[0]),
+        pltpu.make_async_copy(target_hbm, frames.at[1], sems.at[1]),
+        pltpu.make_async_copy(weight_hbm, taps_ref, sems.at[2]),
+    ]
+    for copy in copies:
+        copy.start()
     for stage in stages:
         stage[pl.ds(0, 8), :] = jnp.zeros((8, stage.shape[1]), jnp.float32)
-    for which, (frame_ref, out_ref) in enumerate(((query_ref, query_out), (target_ref, target_out))):
+    for copy in copies:
+        copy.wait()
+    for which, out_ref in enumerate((query_out, target_out)):
         total = bias_ref[...]
         for tap_row in (1, 2):
             total = total + tap_row_sum(
-                frame_ref[tap_row - 1], weight_ref, tap_row, stages[2 * which + tap_row - 1]
+                frames[which, tap_row - 1], taps_ref, tap_row, stages[2 * which + tap_row - 1]
             )
         out_ref[...] = total
 
@@ -86,7 +110,14 @@
     return pl.pallas_call(
         own_kernel,
         out_shape=(part, part),
-        scratch_shapes=[pltpu.VMEM((cols + 8, channels), jnp.float32)] * 4,
+        in_specs=[pl.BlockSpec(memory_space=pltpu.HBM)] * 3 + [pl.BlockSpec(memory_space=pltpu.VMEM)],
+        out_specs=(pl.BlockSpec(memory_space=pltpu.VMEM),) * 2,
+        scratch_shapes=[
+            pltpu.VMEM((2, rows, cols, channels), jnp.bfloat16),
+            pltpu.VMEM(conv_weight.shape, jnp.bfloat16),
+            pltpu.SemaphoreType.DMA((3,)),
+        ]
+        + [pltpu.VMEM((cols + 8, channels), jnp.float32)] * 4,
         compiler_params=pltpu.CompilerParams(vmem_limit_bytes=VMEM_LIMIT),
         cost_estimate=pl.CostEstimate(flops=flops, bytes_accessed=1 << 22, transcendentals=0),
         name="own_partials",
@@ -170,42 +201,62 @@
     return jnp.concatenate([highest, sums], axis=-2)
 
 
+def routed(value, route):
+    slots, cores = lax.axis_size("query"), lax.axis_size("target")
+    pairs = []
+    for slot in range(slots):
+        for core in range(cores):
+            to = route(slot, core)
+            if to is not None:
+                pairs.append((slot * cores + core, to[0] * cores + to[1]))
+    return lax.ppermute(value, ("query", "target"), pairs)
+
+
 def on_device(query_input, target_input, conv_weight, conv_bias):
-    query_slot = lax.axis_index("query")
-    core_slot = lax.axis_index("target")
-    core_count = lax.axis_size("target")
-    query_total = lax.axis_size("query")
+    slot = lax.axis_index("query")
+    core = lax.axis_index("target")
+    slots, cores = lax.axis_size("query"), lax.axis_size("target")
     row_width = query_input.shape[1] // 2
     channels = conv_weight.shape[3]
-
-    query_rim, target_rim = rim_partials(query_input, target_input, conv_weight)
-    query_rim = sent(query_rim, "query", lambda i: i + 1)
-    target_rim = sent(target_rim, ("query", "target"), lambda i: i + 1)
+    scale = LOG2E / math.sqrt(channels)
+    group = slots // 4
+    first_core = core == 0
+
+    def line(s, member):
+        return (s // group ^ member) * group + s % group
+
+    def near(s, hop):
+        return s // group * group + (s + hop) % group
+
+    rim = rim_partials(query_input, target_input, conv_weight)
+    rim = routed(rim, lambda s, c: (s, 1) if c == 0 else ((s + 1) % slots, 0))
+    rim = jnp.where((slot == 0) & first_core, 0, rim.astype(jnp.float32))
     query_part, target_part = own_partials(query_input, target_input, conv_weight, conv_bias)
-    queries = (query_part + query_rim.astype(jnp.float32)).astype(jnp.bfloat16)
-    targets = (target_part + target_rim.astype(jnp.float32)).astype(jnp.bfloat16)
-
-    block_queries = [queries] + [
-        sent(queries, "query", lambda i, member=member: i ^ member) for member in (1, 2, 3)
-    ]
-    shares = [targets]
-    for _ in range(query_total // 4 - 1):
-        shares.append(sent(shares[-1], "query", lambda i: (i + 4) % query_total))
-    share_slots = [(query_slot - 4 * hop) % query_total for hop in range(query_total // 4)]
-    row_y = jnp.stack(
-        [(slot * core_count + core_slot).astype(jnp.float32) * CELL for slot in share_slots]
-    )
-    states = match(block_queries, shares, row_y)
-
-    scale = LOG2E / math.sqrt(channels)
-    near = sent(jnp.concatenate([states[1], states[3]], axis=0), "query", lambda i: i ^ 1)
-    own = combined(states[0], near[:4], scale)
-    other = combined(states[2], near[4:], scale)
-    own = combined(own, sent(other, "query", lambda i: i ^ 2), scale)
-    total = combined(own, sent(own, "target", lambda i: i ^ 1), scale)
+    queries = (query_part + rim[row_width:]).astype(jnp.bfloat16)
+    targets = (target_part + rim[:row_width]).astype(jnp.bfloat16)
+
+    rows = [targets, routed(targets, lambda s, c: (s, 1 - c))]
+    row_ids = [slot * cores + core, slot * cores + 1 - core]
+    for hop in range(1, group):
+        rows.append(routed(targets, lambda s, c: (near(s, hop), c)))
+        row_ids.append(near(slot, -hop) * cores + core)
+    far = routed(queries, lambda s, c: (line(s, 3), 1) if c == 0 else (s, 0))
+    mid = routed(queries, lambda s, c: (line(s, 2), 1) if c == 0 else (s, 0))
+    close = routed(queries, lambda s, c: (line(s, 1), 0) if c == 0 else (near(s, 1), 1))
+    for hop in range(1, group):
+        rows.append(routed(rows[hop + 1], lambda s, c: (s, 1 - c)))
+        row_ids.append(near(slot, -hop) * cores + 1 - core)
+    row_y = jnp.stack(row_ids).astype(jnp.float32) * CELL
+
+    (late,) = match([jnp.where(first_core, queries, far)], rows, row_y)
+    (early,) = match([jnp.where(first_core, close, mid)], rows, row_y)
+    far_part = routed(late, lambda s, c: (line(s, 3), c))
+    part = routed(early, lambda s, c: (line(s, 1 + c), c))
+    own = combined(jnp.where(first_core, late, far_part), part, scale)
+    total = combined(own, routed(own, lambda s, c: (s, 1 - c)), scale)
     columns = jnp.arange(row_width, dtype=jnp.int32).astype(jnp.float32) * CELL
     flow_x = total[2] / total[1] - columns
-    flow_y = total[3] / total[1] - query_slot.astype(jnp.float32) * CELL
+    flow_y = total[3] / total[1] - slot.astype(jnp.float32) * CELL
     return jnp.stack([flow_x, flow_y]).reshape(2, 1, row_width)
 
 

time: 37.8 us -> 32.7 us (0.87)
  starting transfers between devices: 15.8 us -> 7.05 us
  Pallas kernels: 3.61 us -> 6.27 us
  local copies, waits for them, and re-layouts: 3.62 us -> 4.27 us
  waiting for transfers between devices: 14 us -> 14.4 us
    ppermute x9 -> x10, starting transfers between devices: 15.8 us -> 7.05 us  [routed(): return lax.ppermute(value, ('query', 'target'), pairs)]
    pallas_call x2, Pallas kernels: 0.89 us -> 2.39 us  [the longest x1 1.25 us: own_partials(): pl.pallas_call(own_kernel, out_shape=(part, part), in_specs=[pl.BlockSpec...]
    pallas_call x1 -> x2, Pallas kernels: 2.72 us -> 3.89 us  [match(): pl.pallas_call(functools.partial(match_kernel, members, shares), out_shap...]
    unnamed x8 -> x14, local copies, waits for them, and re-layouts: 3.03 us -> 3.68 us
    ppermute x9 -> x10, waiting for transfers between devices: 14 us -> 14.4 us  [routed(): return lax.ppermute(value, ('query', 'target'), pairs)]
  transfers between devices with their start and end apart: 9 -> 10, of which waited for: 6 -> 7; matrix products, arithmetic and copies ran while one was open for 0% -> 0% of each run, Pallas kernels for 1% -> 10%
where the time goes in v2:
time: 32.7 us; the launch traced here: 32.5 us
  waiting for transfers between devices  14.4 us (44%)
  starting transfers between devices  7.05 us (22%)
  Pallas kernels  6.27 us (19%)
  local copies, waits for them, and re-layouts  4.27 us (13%)
    ppermute x10, waiting for transfers between devices, routed(): return lax.ppermute(value, ('query', 'target'), pairs)  14.4 us
    ppermute x10, starting transfers between devices, routed(): return lax.ppermute(value, ('query', 'target'), pairs)  7.05 us
    pallas_call x2, Pallas kernels, match(): pl.pallas_call(functools.partial(match_kernel, members, shares), out_shap...  3.89 us
    unnamed x14, local copies, waits for them, and re-layouts  3.68 us
    pallas_call x1, Pallas kernels, own_partials(): pl.pallas_call(own_kernel, out_shape=(part, part), in_specs=[pl.BlockSpec...  1.25 us
    pallas_call x1, Pallas kernels, rim_partials(): pl.pallas_call(rim_kernel, out_shape=jax.ShapeDtypeStruct((cols, out_chan...  1.13 us
  transfers between devices with their start and end apart: 10, of which 7 were waited for; matrix products, arithmetic and copies ran while one was open for 0% of the time, Pallas kernels for 10%

profile of v2, /device:TPU:0, one launch (start us, length us, event | category | flops | bytes accessed | tf_op | source)
XLA Modules:
  0.0 32.5 jit_solution(14144126362888826096)
XLA Ops:
  0.0 0.0 copy-start
  0.0 1.0 %copy-done = bf16[2,960,128]{2,1,0:T(8,128)(2,1)S(1)} copy-done((bf16[2,960,128]{2,1,0:T(8,128)(2,1)S(1)}, bf16[2,960,128]{2,1,0:T(8,128)(2,1)}, u32[]{:S(2)}) %copy-start) | copy-done | bytes 491544
  1.0 0.0 copy-start.2
  1.0 1.0 %copy-done.2 = bf16[2,960,128]{2,1,0:T(8,128)(2,1)S(1)} copy-done((bf16[2,960,128]{2,1,0:T(8,128)(2,1)S(1)}, bf16[2,960,128]{2,1,0:T(8,128)(2,1)}, u32[]{:S(2)}) %copy-start.2) | copy-done | bytes 491544
  2.1 0.0 copy-start.4
  2.1 1.0 %copy-done.4 = bf16[3,3,128,128]{3,2,1,0:T(8,128)(2,1)S(1)} copy-done((bf16[3,3,128,128]{3,2,1,0:T(8,128)(2,1)S(1)}, bf16[3,3,128,128]{3,2,1,0:T(8,128)(2,1)}, u32[]{:S(2)}) %copy-start.4) | copy-done | bytes 294936
  3.0 0.0 copy-start.1
  3.0 0.0 copy-start.3
  3.0 0.0 copy-start.5
  3.0 1.1 %rim_partials.1 = bf16[960,128]{1,0:T(8,128)(2,1)S(1)} custom-call(bf16[2,960,128]{2,1,0:T(8,128)(2,1)S(1)} %copy-done, bf16[2,960,128]{2,1,0:T(8,128)(2,1)S(1)} %copy-done.2, bf16[3,3,128,128]{3,2,1,0:T(8,128)(2,1)S(1)} %copy-done.4), custom_call_target="tpu_custom_call" | custom-call | tf_op jit(solution)/shard_map/rim_partials/pallas_call | solution.py:66
  4.2 0.5 %collective-permute-start = (bf16[960,128]{1,0:T(8,128)(2,1)S(1)}, bf16[960,128]{1,0:T(8,128)(2,1)S(1)}, u32[]{:S(2)}, u32[]{:S(2)}) collective-permute-start(bf16[960,128]{1,0:T(8,128)(2,1)S(1)} %rim_partials.1), channel_id=1, source_target_pairs={{0,1},{1,2},{2,3},{3,4},{4,5},{5,6},{6,7},{7,8},{8,9},{9,10},{10,1... | collective-permute-start | bytes 737288 | tf_op jit(solution)/shard_map/ppermute | solution.py:212
  4.7 0.0 copy-start.6
  4.7 0.0 copy-done.1
  4.7 0.0 copy-done.3
  4.7 0.0 copy-done.5
  4.7 0.6 %copy-done.6 = f32[128]{0:T(128)S(1)} copy-done((f32[128]{0:T(128)S(1)}, f32[128]{0:T(128)}, u32[]{:S(2)}) %copy-start.6) | copy-done | bytes 536
  5.3 1.3 %own_partials.1 = (f32[480,128]{1,0:T(8,128)S(1)}, f32[480,128]{1,0:T(8,128)S(1)}) custom-call(bf16[2,960,128]{2,1,0:T(8,128)(2,1)S(1)} %copy-done.1, bf16[2,960,128]{2,1,0:T(8,128)(2,1)S(1)} %copy-done.3, bf16[3,3,128,128]{3,2,1,0:T(8,128)(2,1)S(1)} %copy-done.5, f32[1,128]{1,0:T(1,128)S(1)} %bitcast.11), custom_call_target="tpu_custom_call" | custom-call | flops 188743680 | bytes 4194304 | tf_op jit(solution)/shard_map/own_partials/pallas_call | solution.py:110
  6.6 7.0 %collective-permute-done = bf16[960,128]{1,0:T(8,128)(2,1)S(1)} collective-permute-done((bf16[960,128]{1,0:T(8,128)(2,1)S(1)}, bf16[960,128]{1,0:T(8,128)(2,1)S(1)}, u32[]{:S(2)}, u32[]{:S(2)}) %collective-permute-start) | collective-permute-done | bytes 245792 | tf_op jit(solution)/shard_map/ppermute | solution.py:212
  13.6 0.1 fusion
  13.7 0.1 collective-permute-start.3
  13.8 0.1 collective-permute-start.1
  13.9 0.1 fusion.10.row_y_ref
  14.0 0.4 %collective-permute-start.2 = (bf16[480,128]{1,0:T(8,128)(2,1)S(1)}, bf16[480,128]{1,0:T(8,128)(2,1)S(1)}, u32[]{:S(2)}, u32[]{:S(2)}) collective-permute-start(bf16[480,128]{1,0:T(8,128)(2,1)S(1)} %get-tuple-element.11.refs_1_), channel_id=1, source_target_pairs={{0,1},{1,0},{2,3},{3,2},{4,5},{5,4},{6,7},{7,6},{8,9},{9,8},{10,11... | collective-permute-start | bytes 368648 | tf_op jit(solution)/shard_map/ppermute | solution.py:212
  14.4 1.4 %collective-permute-start.7 = (bf16[480,128]{1,0:T(8,128)(2,1)S(1)}, bf16[480,128]{1,0:T(8,128)(2,1)S(1)}, u32[]{:S(2)}, u32[]{:S(2)}) collective-permute-start(bf16[480,128]{1,0:T(8,128)(2,1)S(1)} %get-tuple-element.12), channel_id=1, source_target_pairs={{0,9},{1,0},{2,11},{3,2},{4,13},{5,4},{6,15},{7,6},{8,1},{9,8},{10... | collective-permute-start | bytes 368648 | tf_op jit(solution)/shard_map/ppermute | solution.py:212
  15.8 1.6 %collective-permute-start.6 = (bf16[480,128]{1,0:T(8,128)(2,1)S(1)}, bf16[480,128]{1,0:T(8,128)(2,1)S(1)}, u32[]{:S(2)}, u32[]{:S(2)}) collective-permute-start(bf16[480,128]{1,0:T(8,128)(2,1)S(1)} %get-tuple-element.12), channel_id=1, source_target_pairs={{0,4},{1,3},{2,6},{3,1},{4,0},{5,7},{6,2},{7,5},{8,12},{9,11},{10,... | collective-permute-start | bytes 368648 | tf_op jit(solution)/shard_map/ppermute | solution.py:212
  17.4 2.2 %collective-permute-done.3.refs_3_ = bf16[480,128]{1,0:T(8,128)(2,1)S(1)} collective-permute-done((bf16[480,128]{1,0:T(8,128)(2,1)S(1)}, bf16[480,128]{1,0:T(8,128)(2,1)S(1)}, u32[]{:S(2)}, u32[]{:S(2)}) %collective-permute-start.3) | collective-permute-done | bytes 122912 | tf_op jit(solution)/shard_map/ppermute | solution.py:212
  19.6 0.0 collective-permute-start.4
  19.6 0.0 collective-permute-done.1
  19.6 0.0 collective-permute-done.7
  19.7 1.2 %collective-permute-done.6 = bf16[480,128]{1,0:T(8,128)(2,1)S(1)} collective-permute-done((bf16[480,128]{1,0:T(8,128)(2,1)S(1)}, bf16[480,128]{1,0:T(8,128)(2,1)S(1)}, u32[]{:S(2)}, u32[]{:S(2)}) %collective-permute-start.6) | collective-permute-done | bytes 122912 | tf_op jit(solution)/shard_map/ppermute | solution.py:212
  20.9 0.0 collective-permute-done.2.refs_2_
  20.9 0.1 collective-permute-done.4.refs_4_
  21.0 1.9 %match.2 = f32[4,480]{1,0:T(4,128)S(1)} custom-call(f32[4]{0:T(128)S(1)} %fusion.10.row_y_ref, bf16[480,128]{1,0:T(8,128)(2,1)S(1)} %broadcast_select_fusion.1.refs_0_, bf16[480,128]{1,0:T(8,128)(2,1)S(1)} %get-tuple-element.11.refs_1_, bf16[480,128]{1,0:T(8,128)(2,1)S(1)} %collective-permute-done.2.refs_2_, ...), custom_call_target="tpu_custom_call" | custom-call | flops 235929600 | bytes 4194304 | tf_op jit(solution)/shard_map/match/pallas_call | solution.py:180
  22.9 1.9 %collective-permute-start.5 = (f32[4,480]{1,0:T(4,128)S(1)}, f32[4,480]{1,0:T(4,128)S(1)}, u32[]{:S(2)}, u32[]{:S(2)}) collective-permute-start(f32[4,480]{1,0:T(4,128)S(1)} %match.2), channel_id=1, source_target_pairs={{0,12},{1,13},{2,14},{3,15},{4,8},{5,9},{6,10},{7,11},{8,4},{9,5},... | collective-permute-start | bytes 23048 | tf_op jit(solution)/shard_map/ppermute | solution.py:212
  24.8 1.9 %match.3 = f32[4,480]{1,0:T(4,128)S(1)} custom-call(f32[4]{0:T(128)S(1)} %fusion.10.row_y_ref, bf16[480,128]{1,0:T(8,128)(2,1)S(1)} %broadcast_select_fusion.refs_0_, bf16[480,128]{1,0:T(8,128)(2,1)S(1)} %get-tuple-element.11.refs_1_, bf16[480,128]{1,0:T(8,128)(2,1)S(1)} %collective-permute-done.2.refs_2_, ...), custom_call_target="tpu_custom_call" | custom-call | flops 235929600 | bytes 4194304 | tf_op jit(solution)/shard_map/match/pallas_call | solution.py:180
  26.7 0.6 %collective-permute-start.8 = (f32[4,480]{1,0:T(4,128)S(1)}, f32[4,480]{1,0:T(4,128)S(1)}, u32[]{:S(2)}, u32[]{:S(2)}) collective-permute-start(f32[4,480]{1,0:T(4,128)S(1)} %match.3), channel_id=1, source_target_pairs={{0,4},{1,9},{2,6},{3,11},{4,0},{5,13},{6,2},{7,15},{8,12},{9,1},{1... | collective-permute-start | bytes 23048 | tf_op jit(solution)/shard_map/ppermute | solution.py:212
  27.3 1.1 %collective-permute-done.5 = f32[4,480]{1,0:T(4,128)S(1)} collective-permute-done((f32[4,480]{1,0:T(4,128)S(1)}, f32[4,480]{1,0:T(4,128)S(1)}, u32[]{:S(2)}, u32[]{:S(2)}) %collective-permute-start.5) | collective-permute-done | bytes 7712 | tf_op jit(solution)/shard_map/ppermute | solution.py:212
  28.4 2.0 %collective-permute-done.8 = f32[4,480]{1,0:T(4,128)S(1)} collective-permute-done((f32[4,480]{1,0:T(4,128)S(1)}, f32[4,480]{1,0:T(4,128)S(1)}, u32[]{:S(2)}, u32[]{:S(2)}) %collective-permute-start.8) | collective-permute-done | bytes 7712 | tf_op jit(solution)/shard_map/ppermute | solution.py:212
  30.5 0.5 %collective-permute-start.9 = (f32[4,480]{1,0:T(4,128)S(1)}, f32[4,480]{1,0:T(4,128)S(1)}, u32[]{:S(2)}, u32[]{:S(2)}) collective-permute-start(f32[4,480]{1,0:T(4,128)S(1)} %pad_maximum_fusion), channel_id=1, source_target_pairs={{0,1},{1,0},{2,3},{3,2},{4,5},{5,4},{6,7},{7,6},{8,9},{9,8},{10,11... | collective-permute-start | bytes 23048 | tf_op jit(solution)/shard_map/ppermute | solution.py:212
  31.0 0.8 %collective-permute-done.9 = f32[4,480]{1,0:T(4,128)S(1)} collective-permute-done((f32[4,480]{1,0:T(4,128)S(1)}, f32[4,480]{1,0:T(4,128)S(1)}, u32[]{:S(2)}, u32[]{:S(2)}) %collective-permute-start.9) | collective-permute-done | bytes 7712 | tf_op jit(solution)/shard_map/ppermute | solution.py:212
  31.9 0.6 %copy.5 = f32[2,1,480]{2,1,0:T(1,128)} copy(f32[2,1,480]{2,0,1:T(2,128)S(1)} %maximum_bitcast_fusion) | data formatting | bytes 7680 | tf_op jit(solution)/shard_map/reshape | solution.py:260
  (12 shorter events, 0.2 us)
Async XLA Ops:
  0.0 1.0 %copy-start = (bf16[2,960,128]{2,1,0:T(8,128)(2,1)S(1)}, bf16[2,960,128]{2,1,0:T(8,128)(2,1)}, u32[]{:S(2)}) copy-start(bf16[2,960,128]{2,1,0:T(8,128)(2,1)} %query_hbm.3) | copy-start | bytes 1474564
  1.0 1.0 %copy-start.2 = (bf16[2,960,128]{2,1,0:T(8,128)(2,1)S(1)}, bf16[2,960,128]{2,1,0:T(8,128)(2,1)}, u32[]{:S(2)}) copy-start(bf16[2,960,128]{2,1,0:T(8,128)(2,1)} %target_hbm.3) | copy-start | bytes 1474564
  2.1 1.0 %copy-start.4 = (bf16[3,3,128,128]{3,2,1,0:T(8,128)(2,1)S(1)}, bf16[3,3,128,128]{3,2,1,0:T(8,128)(2,1)}, u32[]{:S(2)}) copy-start(bf16[3,3,128,128]{3,2,1,0:T(8,128)(2,1)} %weight_hbm.3) | copy-start | bytes 884740
  3.0 1.7 %copy-start.1 = (bf16[2,960,128]{2,1,0:T(8,128)(2,1)S(1)}, bf16[2,960,128]{2,1,0:T(8,128)(2,1)}, u32[]{:S(2)}) copy-start(bf16[2,960,128]{2,1,0:T(8,128)(2,1)} %query_hbm.3) | copy-start | bytes 1474564
  3.0 1.7 %copy-start.3 = (bf16[2,960,128]{2,1,0:T(8,128)(2,1)S(1)}, bf16[2,960,128]{2,1,0:T(8,128)(2,1)}, u32[]{:S(2)}) copy-start(bf16[2,960,128]{2,1,0:T(8,128)(2,1)} %target_hbm.3) | copy-start | bytes 1474564
  3.0 1.7 %copy-start.5 = (bf16[3,3,128,128]{3,2,1,0:T(8,128)(2,1)S(1)}, bf16[3,3,128,128]{3,2,1,0:T(8,128)(2,1)}, u32[]{:S(2)}) copy-start(bf16[3,3,128,128]{3,2,1,0:T(8,128)(2,1)} %weight_hbm.3) | copy-start | bytes 884740
  4.2 9.4 %collective-permute-start = (bf16[960,128]{1,0:T(8,128)(2,1)S(1)}, bf16[960,128]{1,0:T(8,128)(2,1)S(1)}, u32[]{:S(2)}, u32[]{:S(2)}) collective-permute-start(bf16[960,128]{1,0:T(8,128)(2,1)S(1)} %rim_partials.1), channel_id=1, source_target_pairs={{0,1},{1,2},{2,3},{3,4},{4,5},{5,6},{6,7},{7,8},{8,9},{9,10},{10,1... | collective-permute-start | bytes 737288 | tf_op jit(solution)/shard_map/ppermute | solution.py:212
  4.7 0.7 %copy-start.6 = (f32[128]{0:T(128)S(1)}, f32[128]{0:T(128)}, u32[]{:S(2)}) copy-start(f32[128]{0:T(128)} %param.7) | copy-start | bytes 1540
  13.7 5.9 %collective-permute-start.3 = (bf16[480,128]{1,0:T(8,128)(2,1)S(1)}, bf16[480,128]{1,0:T(8,128)(2,1)S(1)}, u32[]{:S(2)}, u32[]{:S(2)}) collective-permute-start(bf16[480,128]{1,0:T(8,128)(2,1)S(1)} %get-tuple-element.11.refs_1_), channel_id=1, source_target_pairs={{0,2},{1,3},{2,0},{3,1},{4,6},{5,7},{6,4},{7,5},{8,10},{9,11},{10,... | collective-permute-start | bytes 368648 | tf_op jit(solution)/shard_map/ppermute | solution.py:212
  13.8 5.9 %collective-permute-start.1 = (bf16[480,128]{1,0:T(8,128)(2,1)S(1)}, bf16[480,128]{1,0:T(8,128)(2,1)S(1)}, u32[]{:S(2)}, u32[]{:S(2)}) collective-permute-start(bf16[480,128]{1,0:T(8,128)(2,1)S(1)} %get-tuple-element.12), channel_id=1, source_target_pairs={{0,13},{1,0},{2,15},{3,2},{4,9},{5,4},{6,11},{7,6},{8,5},{9,8},{10... | collective-permute-start | bytes 368648 | tf_op jit(solution)/shard_map/ppermute | solution.py:212
  14.0 6.9 %collective-permute-start.2 = (bf16[480,128]{1,0:T(8,128)(2,1)S(1)}, bf16[480,128]{1,0:T(8,128)(2,1)S(1)}, u32[]{:S(2)}, u32[]{:S(2)}) collective-permute-start(bf16[480,128]{1,0:T(8,128)(2,1)S(1)} %get-tuple-element.11.refs_1_), channel_id=1, source_target_pairs={{0,1},{1,0},{2,3},{3,2},{4,5},{5,4},{6,7},{7,6},{8,9},{9,8},{10,11... | collective-permute-start | bytes 368648 | tf_op jit(solution)/shard_map/ppermute | solution.py:212
  14.4 5.2 %collective-permute-start.7 = (bf16[480,128]{1,0:T(8,128)(2,1)S(1)}, bf16[480,128]{1,0:T(8,128)(2,1)S(1)}, u32[]{:S(2)}, u32[]{:S(2)}) collective-permute-start(bf16[480,128]{1,0:T(8,128)(2,1)S(1)} %get-tuple-element.12), channel_id=1, source_target_pairs={{0,9},{1,0},{2,11},{3,2},{4,13},{5,4},{6,15},{7,6},{8,1},{9,8},{10... | collective-permute-start | bytes 368648 | tf_op jit(solution)/shard_map/ppermute | solution.py:212
  15.8 5.0 %collective-permute-start.6 = (bf16[480,128]{1,0:T(8,128)(2,1)S(1)}, bf16[480,128]{1,0:T(8,128)(2,1)S(1)}, u32[]{:S(2)}, u32[]{:S(2)}) collective-permute-start(bf16[480,128]{1,0:T(8,128)(2,1)S(1)} %get-tuple-element.12), channel_id=1, source_target_pairs={{0,4},{1,3},{2,6},{3,1},{4,0},{5,7},{6,2},{7,5},{8,12},{9,11},{10,... | collective-permute-start | bytes 368648 | tf_op jit(solution)/shard_map/ppermute | solution.py:212
  19.6 1.3 %collective-permute-start.4 = (bf16[480,128]{1,0:T(8,128)(2,1)S(1)}, bf16[480,128]{1,0:T(8,128)(2,1)S(1)}, u32[]{:S(2)}, u32[]{:S(2)}) collective-permute-start(bf16[480,128]{1,0:T(8,128)(2,1)S(1)} %collective-permute-done.3.refs_3_), channel_id=1, source_target_pairs={{0,1},{1,0},{2,3},{3,2},{4,5},{5,4},{6,7},{7,6},{8,9},{9,8},{10,11... | collective-permute-start | bytes 368648 | tf_op jit(solution)/shard_map/ppermute | solution.py:212
  22.9 5.5 %collective-permute-start.5 = (f32[4,480]{1,0:T(4,128)S(1)}, f32[4,480]{1,0:T(4,128)S(1)}, u32[]{:S(2)}, u32[]{:S(2)}) collective-permute-start(f32[4,480]{1,0:T(4,128)S(1)} %match.2), channel_id=1, source_target_pairs={{0,12},{1,13},{2,14},{3,15},{4,8},{5,9},{6,10},{7,11},{8,4},{9,5},... | collective-permute-start | bytes 23048 | tf_op jit(solution)/shard_map/ppermute | solution.py:212
  26.7 3.7 %collective-permute-start.8 = (f32[4,480]{1,0:T(4,128)S(1)}, f32[4,480]{1,0:T(4,128)S(1)}, u32[]{:S(2)}, u32[]{:S(2)}) collective-permute-start(f32[4,480]{1,0:T(4,128)S(1)} %match.3), channel_id=1, source_target_pairs={{0,4},{1,9},{2,6},{3,11},{4,0},{5,13},{6,2},{7,15},{8,12},{9,1},{1... | collective-permute-start | bytes 23048 | tf_op jit(solution)/shard_map/ppermute | solution.py:212
  30.5 1.3 %collective-permute-start.9 = (f32[4,480]{1,0:T(4,128)S(1)}, f32[4,480]{1,0:T(4,128)S(1)}, u32[]{:S(2)}, u32[]{:S(2)}) collective-permute-start(f32[4,480]{1,0:T(4,128)S(1)} %pad_maximum_fusion), channel_id=1, source_target_pairs={{0,1},{1,0},{2,3},{3,2},{4,5},{5,4},{6,7},{7,6},{8,9},{9,8},{10,11... | collective-permute-start | bytes 23048 | tf_op jit(solution)/shard_map/ppermute | solution.py:212

commit v3 on v2

v3 whole, which is shorter than its diff:
```python
import functools
import math

import jax
import jax.numpy as jnp
from jax import lax
from jax.experimental import pallas as pl
from jax.experimental.pallas import tpu as pltpu
from jax.sharding import PartitionSpec as P

CELL = 0.0625
LOG2E = math.log2(math.e)
VMEM_LIMIT = 32 * 1024 * 1024
RIM_VMEM = (64 * 1024 - 10752) * 1024


def column_taps(row, stage):
    out_cols = row.shape[0] // 2
    stage[pl.ds(8, row.shape[0]), :] = row.astype(jnp.float32)
    return [
        stage[pl.ds(7 + tap, out_cols, stride=2), :].astype(jnp.bfloat16) for tap in range(3)
    ]


def tap_row_sum(row, weight_ref, tap_row, stage):
    taps = column_taps(row, stage)
    total = None
    for tap_col in range(3):
        term = jnp.dot(
            taps[tap_col], weight_ref[tap_row, tap_col], preferred_element_type=jnp.float32
        )
        total = term if total is None else total + term
    return total


def rim_kernel(
    first_core_ref, query_hbm, target_hbm, weight_hbm, far_rim_ref, near_rim_ref, rows_ref, taps_ref, sems, *stages
):
    last = query_hbm.shape[0] - 1
    copies = [
        pltpu.make_async_copy(weight_hbm.at[pl.ds(0, 1)], taps_ref, sems.at[2]),
        pltpu.make_async_copy(target_hbm.at[last], rows_ref.at[0], sems.at[0]),
        pltpu.make_async_copy(query_hbm.at[last], rows_ref.at[1], sems.at[1]),
    ]
    for copy in copies:
        copy.start()
    for stage in stages:
        stage[pl.ds(0, 8), :] = jnp.zeros((8, stage.shape[1]), jnp.float32)
    for copy in copies:
        copy.wait()
    target_rim = tap_row_sum(rows_ref[0], taps_ref, 0, stages[0])
    query_rim = tap_row_sum(rows_ref[1], taps_ref, 0, stages[1])
    near_rim_ref[...] = target_rim.astype(near_rim_ref.dtype)
    far_rim_ref[...] = jnp.where(first_core_ref[0] == 1, query_rim, target_rim).astype(far_rim_ref.dtype)


def rim_partials(first_core, query_input, target_input, conv_weight):
    _, cols, channels = query_input.shape
    out_channels = conv_weight.shape[3]
    hbm = pl.BlockSpec(memory_space=pltpu.HBM)
    return pl.pallas_call(
        rim_kernel,
        out_shape=(jax.ShapeDtypeStruct((cols // 2, out_channels), jnp.bfloat16),) * 2,
        in_specs=[pl.BlockSpec(memory_space=pltpu.SMEM)] + [hbm] * 3,
        out_specs=(pl.BlockSpec(memory_space=pltpu.VMEM),) * 2,
        scratch_shapes=[
            pltpu.VMEM((2, cols, channels), jnp.bfloat16),
            pltpu.VMEM((1,) + conv_weight.shape[1:], jnp.bfloat16),
            pltpu.SemaphoreType.DMA((3,)),
        ]
        + [pltpu.VMEM((cols + 8, channels), jnp.float32)] * 2,
        compiler_params=pltpu.CompilerParams(vmem_limit_bytes=RIM_VMEM),
        name="rim_partials",
    )(first_core, query_input, target_input, conv_weight)


def own_kernel(query_ref, target_ref, weight_ref, bias_ref, query_out, target_out, *stages):
    for stage in stages:
        stage[pl.ds(0, 8), :] = jnp.zeros((8, stage.shape[1]), jnp.float32)
    pairs = ((target_ref, target_out), (query_ref, query_out))
    for which, (frame_ref, out_ref) in enumerate(pairs):
        total = bias_ref[...]
        for tap_row in (1, 2):
            total = total + tap_row_sum(
                frame_ref[tap_row - 1], weight_ref, tap_row, stages[2 * which + tap_row - 1]
            )
        out_ref[...] = total


def own_partials(query_input, target_input, conv_weight, conv_bias):
    _, cols, channels = query_input.shape
    out_channels = conv_weight.shape[3]
    part = jax.ShapeDtypeStruct((cols // 2, out_channels), jnp.float32)
    flops = 2 * 2 * 6 * (cols // 2) * channels * out_channels
    return pl.pallas_call(
        own_kernel,
        out_shape=(part, part),
        scratch_shapes=[pltpu.VMEM((cols + 8, channels), jnp.float32)] * 4,
        compiler_params=pltpu.CompilerParams(vmem_limit_bytes=VMEM_LIMIT),
        cost_estimate=pl.CostEstimate(flops=flops, bytes_accessed=1 << 22, transcendentals=0),
        name="own_partials",
    )(query_input, target_input, conv_weight, conv_bias.reshape(1, out_channels))


def merged(state, part, scale):
    top = jnp.maximum(state[0], part[0])
    keep = jnp.exp2((state[0] - top) * scale)
    gain = jnp.exp2((part[0] - top) * scale)
    return (top, *[old * keep + new * gain for old, new in zip(state[1:], part[1:])])


def match_kernel(shares, row_y_ref, query_ref, *refs):
    target_refs = refs[:shares]
    state_refs = refs[shares : -1 - shares]
    out_ref = refs[-1 - shares]
    scores_refs = refs[-shares:]
    lanes, channels = query_ref.shape
    steps = target_refs[0].shape[0] // 8
    scale = LOG2E / math.sqrt(channels)
    offset = lax.broadcasted_iota(jnp.int32, (8, lanes), 0).astype(jnp.float32)
    state = None
    for state_ref in state_refs:
        state = tuple(state_ref[pl.ds(i, 1), :] for i in range(4))
    for share in range(shares):
        scores_ref = scores_refs[share]
        scores_ref[...] = lax.dot_general(
            target_refs[share][...],
            query_ref[...],
            (((1,), (1,)), ((), ())),
            preferred_element_type=jnp.float32,
        )
        highest = scores_ref[pl.ds(0, 8), :]
        for step in range(1, steps):
            highest = jnp.maximum(highest, scores_ref[pl.ds(8 * step, 8), :])
        highest = jnp.max(highest, axis=0, keepdims=True)
        spread = jnp.broadcast_to(highest, (8, lanes))
        plain = jnp.zeros((8, lanes), jnp.float32)
        stacked = jnp.zeros((8, lanes), jnp.float32)
        for step in reversed(range(steps)):
            plain = plain + jnp.exp2((scores_ref[pl.ds(8 * step, 8), :] - spread) * scale)
            if step:
                stacked = stacked + plain
        part_x = jnp.sum(8.0 * stacked + offset * plain, axis=0, keepdims=True) * CELL
        part_sum = jnp.sum(plain, axis=0, keepdims=True)
        part = (highest, part_sum, part_x, part_sum * row_y_ref[share])
        state = part if state is None else merged(state, part, scale)
    out_ref[...] = jnp.concatenate(state, axis=0)


def match(queries, targets, row_y, state=None):
    shares = len(targets)
    lanes, channels = queries.shape
    row_width = targets[0].shape[0]
    states = [] if state is None else [state]
    vmem = pl.BlockSpec(memory_space=pltpu.VMEM)
    return pl.pallas_call(
        functools.partial(match_kernel, shares),
        out_shape=jax.ShapeDtypeStruct((4, lanes), jnp.float32),
        in_specs=[pl.BlockSpec(memory_space=pltpu.SMEM)] + [vmem] * (1 + shares + len(states)),
        out_specs=vmem,
        scratch_shapes=[pltpu.VMEM((row_width, lanes), jnp.float32)] * shares,
        compiler_params=pltpu.CompilerParams(vmem_limit_bytes=VMEM_LIMIT),
        cost_estimate=pl.CostEstimate(
            flops=2 * shares * lanes * row_width * channels,
            bytes_accessed=1 << 22,
            transcendentals=shares * lanes * row_width,
        ),
        name="match",
    )(row_y, queries, *targets, *states)


def combined(first, second, scale):
    highest = jnp.maximum(first[..., :1, :], second[..., :1, :])
    first_scale = jnp.exp2((first[..., :1, :] - highest) * scale)
    second_scale = jnp.exp2((second[..., :1, :] - highest) * scale)
    sums = first[..., 1:, :] * first_scale + second[..., 1:, :] * second_scale
    return jnp.concatenate([highest, sums], axis=-2)


def routed(value, route):
    slots, cores = lax.axis_size("query"), lax.axis_size("target")
    pairs = []
    for slot in range(slots):
        for core in range(cores):
            to = route(slot, core)
            if to is not None:
                pairs.append((slot * cores + core, to[0] * cores + to[1]))
    return lax.ppermute(value, ("query", "target"), pairs)


def on_device(query_input, target_input, conv_weight, conv_bias):
    slot = lax.axis_index("query")
    core = lax.axis_index("target")
    slots = lax.axis_size("query")
    row_width = query_input.shape[1] // 2
    channels = conv_weight.shape[3]
    scale = LOG2E / math.sqrt(channels)
    first = core == 0

    def pick(on_first, on_second):
        return jnp.where(first, on_first, on_second)

    def swapped(value):
        return routed(value, lambda s, c: (s, 1 - c))

    far_rim, near_rim = rim_partials(
        first.astype(jnp.int32).reshape(1), query_input, target_input, conv_weight
    )
    near_rim = swapped(near_rim)
    far_rim = routed(far_rim, lambda s, c: ((s + 1) % slots, c)).astype(jnp.float32)
    far_rim = jnp.where(slot == 0, 0.0, far_rim)
    query_part, target_part = own_partials(query_input, target_input, conv_weight, conv_bias)
    odd = (target_part + pick(0.0, near_rim.astype(jnp.float32))).astype(jnp.bfloat16)
    handed = swapped(odd)
    odd_away = [
        routed(odd, lambda s, c: (s, 1) if c == 0 else ((s + 4 * hop) % slots, 0))
        for hop in range(1, max(2, slots // 4))
    ]
    whole = (pick(query_part, handed.astype(jnp.float32)) + far_rim).astype(jnp.bfloat16)
    even_away = [
        routed(whole, lambda s, c: (s ^ 2, 0) if c == 0 else ((s + 4 * hop) % slots, 1))
        for hop in range(1, max(2, slots // 4))
    ]
    corner = routed(whole, lambda s, c: (s ^ 3, 1) if c == 0 else (s, 0))
    beside = routed(whole, lambda s, c: (s ^ 1, 1) if c == 0 else (s, 0))

    def row_y(ids):
        return jnp.stack(ids).astype(jnp.float32) * CELL

    members = [pick(whole, corner), pick(even_away[0], beside)]
    rows = [pick(corner, whole), pick(handed, odd)]
    ids = row_y([2 * slot, 2 * slot + 1])
    states = [match(member, rows, ids) for member in members]
    for hop in range(1, slots // 4):
        source = (slot - 4 * hop) % slots
        row = pick(odd_away[hop - 1], even_away[hop - 1])
        rows = [row, swapped(row)]
        ids = row_y([2 * source + 1 - core, 2 * source + core])
        states = [match(member, rows, ids, state) for member, state in zip(members, states)]
    state, other = states
    corner_state = routed(state, lambda s, c: (s ^ 3, c))
    other = routed(other, lambda s, c: (s ^ (2 if c == 0 else 1), c))
    own = combined(pick(state, corner_state), other, scale)
    total = combined(own, swapped(own), scale)
    columns = jnp.arange(row_width, dtype=jnp.int32).astype(jnp.float32) * CELL
    flow_x = total[2] / total[1] - columns
    flow_y = total[3] / total[1] - slot.astype(jnp.float32) * CELL
    return jnp.stack([flow_x, flow_y]).reshape(2, 1, row_width)


def solution(mesh):
    placed = (
        P(("groups", "query"), None, None),
        P(("groups", "query", "target"), None, None),
        P(),
        P(),
    )
    return jax.shard_map(
        on_device,
        mesh=mesh,
        in_specs=placed,
        out_specs=P(None, ("groups", "query"), None),
        check_vma=False,
    )
```

time: 32.7 us -> 30.1 us (0.920)
  local copies, waits for them, and re-layouts: 4.27 us -> 1.25 us
  waiting for transfers between devices: 14.4 us -> 12.7 us
  starting transfers between devices: 7.05 us -> 8.16 us
  Pallas kernels: 6.27 us -> 7.26 us
    unnamed x14 -> x8, local copies, waits for them, and re-layouts: 3.68 us -> 0.66 us
    ppermute x10 -> x11, waiting for transfers between devices: 14.4 us -> 12.7 us  [routed(): return lax.ppermute(value, ('query', 'target'), pairs)]
    ppermute x10 -> x11, starting transfers between devices: 7.05 us -> 8.16 us  [routed(): return lax.ppermute(value, ('query', 'target'), pairs)]
    pallas_call x4 -> x6, Pallas kernels: 6.27 us -> 7.26 us  [the longest x4 5.13 us: match(): pl.pallas_call(functools.partial(match_kernel, shares), out_shape=jax.Sha...]
  transfers between devices with their start and end apart: 10 -> 11, of which waited for: 7 -> 6; matrix products, arithmetic and copies ran while one was open for 0% -> 1% of each run, Pallas kernels for 10% -> 15%
where the time goes in v3:
time: 30.1 us; the launch traced here: 30 us
  waiting for transfers between devices  12.7 us (42%)
  starting transfers between devices  8.16 us (27%)
  Pallas kernels  7.26 us (24%)
  local copies, waits for them, and re-layouts  1.25 us (4%)
  other arithmetic  0.41 us (1%)
    ppermute x11, waiting for transfers between devices, routed(): return lax.ppermute(value, ('query', 'target'), pairs)  12.7 us
    ppermute x11, starting transfers between devices, routed(): return lax.ppermute(value, ('query', 'target'), pairs)  8.16 us
    pallas_call x4, Pallas kernels, match(): pl.pallas_call(functools.partial(match_kernel, shares), out_shape=jax.Sha...  5.13 us
    pallas_call x1, Pallas kernels, rim_partials(): pl.pallas_call(rim_kernel, out_shape=(jax.ShapeDtypeStruct((cols // 2, ou...  1.59 us
    unnamed x8, local copies, waits for them, and re-layouts  0.66 us
  transfers between devices with their start and end apart: 11, of which 6 were waited for; matrix products, arithmetic and copies ran while one was open for 1% of the time, Pallas kernels for 15%

profile of v3, /device:TPU:0, one launch (start us, length us, event | category | flops | bytes accessed | tf_op | source)
XLA Modules:
  0.0 30.0 jit_solution(2801546155673318366)
XLA Ops:
  0.0 0.0 copy-start
  0.0 0.0 copy-start.1
  0.0 0.0 copy-start.2
  0.0 1.6 %rim_partials.1 = (bf16[480,128]{1,0:T(8,128)(2,1)S(1)}, bf16[480,128]{1,0:T(8,128)(2,1)S(1)}) custom-call(s32[1]{0:T(128)} %bitcast.3.first_core_ref, bf16[2,960,128]{2,1,0:T(8,128)(2,1)} %query_hbm.1, bf16[2,960,128]{2,1,0:T(8,128)(2,1)} %target_hbm.1, bf16[3,3,128,128]{3,2,1,0:T(8,128)(2,1)} %weight_hbm.1), custom_call_target="tpu_custom_call" | custom-call | tf_op jit(solution)/shard_map/rim_partials/pallas_call | solution.py:61
  1.6 0.5 %collective-permute-start = (bf16[480,128]{1,0:T(8,128)(2,1)S(1)}, bf16[480,128]{1,0:T(8,128)(2,1)S(1)}, u32[]{:S(2)}, u32[]{:S(2)}) collective-permute-start(bf16[480,128]{1,0:T(8,128)(2,1)S(1)} %get-tuple-element.11), channel_id=1, source_target_pairs={{0,1},{1,0},{2,3},{3,2},{4,5},{5,4},{6,7},{7,6},{8,9},{9,8},{10,11... | collective-permute-start | bytes 368648 | tf_op jit(solution)/shard_map/ppermute | solution.py:188
  2.1 2.6 %collective-permute-start.2 = (bf16[480,128]{1,0:T(8,128)(2,1)S(1)}, bf16[480,128]{1,0:T(8,128)(2,1)S(1)}, u32[]{:S(2)}, u32[]{:S(2)}) collective-permute-start(bf16[480,128]{1,0:T(8,128)(2,1)S(1)} %get-tuple-element.12), channel_id=1, source_target_pairs={{0,2},{1,3},{2,4},{3,5},{4,6},{5,7},{6,8},{7,9},{8,10},{9,11},{10,... | collective-permute-start | bytes 368648 | tf_op jit(solution)/shard_map/ppermute | solution.py:188
  4.7 0.0 copy-start.3
  4.7 0.0 copy-done
  4.7 0.0 copy-done.1
  4.7 0.0 copy-done.2
  4.7 0.6 %copy-done.3 = f32[128]{0:T(128)S(1)} copy-done((f32[128]{0:T(128)S(1)}, f32[128]{0:T(128)}, u32[]{:S(2)}) %copy-start.3) | copy-done | bytes 536
  5.4 0.5 %own_partials.1 = (f32[480,128]{1,0:T(8,128)S(1)}, f32[480,128]{1,0:T(8,128)S(1)}) custom-call(bf16[2,960,128]{2,1,0:T(8,128)(2,1)S(1)} %copy-done, bf16[2,960,128]{2,1,0:T(8,128)(2,1)S(1)} %copy-done.1, bf16[3,3,128,128]{3,2,1,0:T(8,128)(2,1)S(1)} %copy-done.2, f32[1,128]{1,0:T(1,128)S(1)} %bitcast.12), custom_call_target="tpu_custom_call" | custom-call | flops 188743680 | bytes 4194304 | tf_op jit(solution)/shard_map/own_partials/pallas_call | solution.py:95
  5.9 0.0 collective-permute-done
  6.0 0.2 collective-permute-start.1
  6.2 0.1 fusion.8.row_y_ref
  6.3 0.1 fusion.9.row_y_ref
  6.4 0.3 %collective-permute-start.4 = (bf16[480,128]{1,0:T(8,128)(2,1)S(1)}, bf16[480,128]{1,0:T(8,128)(2,1)S(1)}, u32[]{:S(2)}, u32[]{:S(2)}) collective-permute-start(bf16[480,128]{1,0:T(8,128)(2,1)S(1)} %add_convert_fusion.1), channel_id=1, source_target_pairs={{0,1},{1,8},{2,3},{3,10},{4,5},{5,12},{6,7},{7,14},{8,9},{9,0},{10... | collective-permute-start | bytes 368648 | tf_op jit(solution)/shard_map/ppermute | solution.py:188
  6.7 5.0 %collective-permute-done.2 = bf16[480,128]{1,0:T(8,128)(2,1)S(1)} collective-permute-done((bf16[480,128]{1,0:T(8,128)(2,1)S(1)}, bf16[480,128]{1,0:T(8,128)(2,1)S(1)}, u32[]{:S(2)}, u32[]{:S(2)}) %collective-permute-start.2) | collective-permute-done | bytes 122912 | tf_op jit(solution)/shard_map/ppermute | solution.py:188
  11.7 0.0 collective-permute-done.1
  11.7 0.1 add_convert_fusion
  11.8 0.1 collective-permute-start.8
  11.9 0.1 collective-permute-start.5
  11.9 2.0 %collective-permute-start.3 = (bf16[480,128]{1,0:T(8,128)(2,1)S(1)}, bf16[480,128]{1,0:T(8,128)(2,1)S(1)}, u32[]{:S(2)}, u32[]{:S(2)}) collective-permute-start(bf16[480,128]{1,0:T(8,128)(2,1)S(1)} %add_convert_fusion), channel_id=1, source_target_pairs={{0,7},{1,0},{2,5},{3,2},{4,3},{5,4},{6,1},{7,6},{8,15},{9,8},{10,1... | collective-permute-start | bytes 368648 | tf_op jit(solution)/shard_map/ppermute | solution.py:188
  14.0 0.0 collective-permute-done.4
  14.0 0.3 %collective-permute-done.8 = bf16[480,128]{1,0:T(8,128)(2,1)S(1)} collective-permute-done((bf16[480,128]{1,0:T(8,128)(2,1)S(1)}, bf16[480,128]{1,0:T(8,128)(2,1)S(1)}, u32[]{:S(2)}, u32[]{:S(2)}) %collective-permute-start.8) | collective-permute-done | bytes 122912 | tf_op jit(solution)/shard_map/ppermute | solution.py:188
  14.3 3.8 %collective-permute-done.5 = bf16[480,128]{1,0:T(8,128)(2,1)S(1)} collective-permute-done((bf16[480,128]{1,0:T(8,128)(2,1)S(1)}, bf16[480,128]{1,0:T(8,128)(2,1)S(1)}, u32[]{:S(2)}, u32[]{:S(2)}) %collective-permute-start.5) | collective-permute-done | bytes 122912 | tf_op jit(solution)/shard_map/ppermute | solution.py:188
  18.1 0.1 collective-permute-start.6
  18.2 0.0 collective-permute-done.3
  18.3 1.3 %match.4.refs_2_ = f32[4,480]{1,0:T(4,128)S(1)} custom-call(f32[2]{0:T(128)S(1)} %fusion.9.row_y_ref, bf16[480,128]{1,0:T(8,128)(2,1)S(1)} %get-tuple-element.15.query_ref, bf16[480,128]{1,0:T(8,128)(2,1)S(1)} %get-tuple-element.16.refs_0_, bf16[480,128]{1,0:T(8,128)(2,1)S(1)} %broadcast_select_fusion.1.refs_1_), custom_call_target="tpu_custom_call" | custom-call | flops 117964800 | bytes 4194304 | tf_op jit(solution)/shard_map/match/pallas_call | solution.py:156
  19.5 1.3 %match.6.refs_2_ = f32[4,480]{1,0:T(4,128)S(1)} custom-call(f32[2]{0:T(128)S(1)} %fusion.9.row_y_ref, bf16[480,128]{1,0:T(8,128)(2,1)S(1)} %get-tuple-element.18.query_ref, bf16[480,128]{1,0:T(8,128)(2,1)S(1)} %get-tuple-element.16.refs_0_, bf16[480,128]{1,0:T(8,128)(2,1)S(1)} %broadcast_select_fusion.1.refs_1_), custom_call_target="tpu_custom_call" | custom-call | flops 117964800 | bytes 4194304 | tf_op jit(solution)/shard_map/match/pallas_call | solution.py:156
  20.8 0.0 collective-permute-done.6.refs_1_
  20.8 1.3 %match.5 = f32[4,480]{1,0:T(4,128)S(1)} custom-call(f32[2]{0:T(128)S(1)} %fusion.8.row_y_ref, bf16[480,128]{1,0:T(8,128)(2,1)S(1)} %get-tuple-element.15.query_ref, bf16[480,128]{1,0:T(8,128)(2,1)S(1)} %get-tuple-element.17.refs_0_, bf16[480,128]{1,0:T(8,128)(2,1)S(1)} %collective-permute-done.6.refs_1_, f32[4,480]{1,0:T(4,128)S(1)} %match.4.refs_2_), custom_call_target="tpu_custom_call" | custom-call | flops 117964800 | bytes 4194304 | tf_op jit(solution)/shard_map/match/pallas_call | solution.py:156
  22.1 0.9 %collective-permute-start.7 = (f32[4,480]{1,0:T(4,128)S(1)}, f32[4,480]{1,0:T(4,128)S(1)}, u32[]{:S(2)}, u32[]{:S(2)}) collective-permute-start(f32[4,480]{1,0:T(4,128)S(1)} %match.5), channel_id=1, source_target_pairs={{0,6},{1,7},{2,4},{3,5},{4,2},{5,3},{6,0},{7,1},{8,14},{9,15},{10,... | collective-permute-start | bytes 23048 | tf_op jit(solution)/shard_map/ppermute | solution.py:188
  23.0 1.3 %match.7 = f32[4,480]{1,0:T(4,128)S(1)} custom-call(f32[2]{0:T(128)S(1)} %fusion.8.row_y_ref, bf16[480,128]{1,0:T(8,128)(2,1)S(1)} %get-tuple-element.18.query_ref, bf16[480,128]{1,0:T(8,128)(2,1)S(1)} %get-tuple-element.17.refs_0_, bf16[480,128]{1,0:T(8,128)(2,1)S(1)} %collective-permute-done.6.refs_1_, f32[4,480]{1,0:T(4,128)S(1)} %match.6.refs_2_), custom_call_target="tpu_custom_call" | custom-call | flops 117964800 | bytes 4194304 | tf_op jit(solution)/shard_map/match/pallas_call | solution.py:156
  24.3 1.3 %collective-permute-start.9 = (f32[4,480]{1,0:T(4,128)S(1)}, f32[4,480]{1,0:T(4,128)S(1)}, u32[]{:S(2)}, u32[]{:S(2)}) collective-permute-start(f32[4,480]{1,0:T(4,128)S(1)} %match.7), channel_id=1, source_target_pairs={{0,4},{1,3},{2,6},{3,1},{4,0},{5,7},{6,2},{7,5},{8,12},{9,11},{10,... | collective-permute-start | bytes 23048 | tf_op jit(solution)/shard_map/ppermute | solution.py:188
  25.6 1.1 %collective-permute-done.7 = f32[4,480]{1,0:T(4,128)S(1)} collective-permute-done((f32[4,480]{1,0:T(4,128)S(1)}, f32[4,480]{1,0:T(4,128)S(1)}, u32[]{:S(2)}, u32[]{:S(2)}) %collective-permute-start.7) | collective-permute-done | bytes 7712 | tf_op jit(solution)/shard_map/ppermute | solution.py:188
  26.7 1.2 %collective-permute-done.9 = f32[4,480]{1,0:T(4,128)S(1)} collective-permute-done((f32[4,480]{1,0:T(4,128)S(1)}, f32[4,480]{1,0:T(4,128)S(1)}, u32[]{:S(2)}, u32[]{:S(2)}) %collective-permute-start.9) | collective-permute-done | bytes 7712 | tf_op jit(solution)/shard_map/ppermute | solution.py:188
  28.1 0.1 collective-permute-start.10
  28.1 1.2 %collective-permute-done.10 = f32[4,480]{1,0:T(4,128)S(1)} collective-permute-done((f32[4,480]{1,0:T(4,128)S(1)}, f32[4,480]{1,0:T(4,128)S(1)}, u32[]{:S(2)}, u32[]{:S(2)}) %collective-permute-start.10) | collective-permute-done | bytes 7712 | tf_op jit(solution)/shard_map/ppermute | solution.py:188
  29.4 0.6 %copy.5 = f32[2,1,480]{2,1,0:T(1,128)} copy(f32[2,1,480]{2,0,1:T(2,128)S(1)} %maximum_bitcast_fusion) | data formatting | bytes 7680 | tf_op jit(solution)/shard_map/reshape | solution.py:248
  (13 shorter events, 0.2 us)
Async XLA Ops:
  0.0 4.7 %copy-start = (bf16[2,960,128]{2,1,0:T(8,128)(2,1)S(1)}, bf16[2,960,128]{2,1,0:T(8,128)(2,1)}, u32[]{:S(2)}) copy-start(bf16[2,960,128]{2,1,0:T(8,128)(2,1)} %query_hbm.1) | copy-start | bytes 1474564
  0.0 4.7 %copy-start.1 = (bf16[2,960,128]{2,1,0:T(8,128)(2,1)S(1)}, bf16[2,960,128]{2,1,0:T(8,128)(2,1)}, u32[]{:S(2)}) copy-start(bf16[2,960,128]{2,1,0:T(8,128)(2,1)} %target_hbm.1) | copy-start | bytes 1474564
  0.0 4.7 %copy-start.2 = (bf16[3,3,128,128]{3,2,1,0:T(8,128)(2,1)S(1)}, bf16[3,3,128,128]{3,2,1,0:T(8,128)(2,1)}, u32[]{:S(2)}) copy-start(bf16[3,3,128,128]{3,2,1,0:T(8,128)(2,1)} %weight_hbm.1) | copy-start | bytes 884740
  1.6 4.3 %collective-permute-start = (bf16[480,128]{1,0:T(8,128)(2,1)S(1)}, bf16[480,128]{1,0:T(8,128)(2,1)S(1)}, u32[]{:S(2)}, u32[]{:S(2)}) collective-permute-start(bf16[480,128]{1,0:T(8,128)(2,1)S(1)} %get-tuple-element.11), channel_id=1, source_target_pairs={{0,1},{1,0},{2,3},{3,2},{4,5},{5,4},{6,7},{7,6},{8,9},{9,8},{10,11... | collective-permute-start | bytes 368648 | tf_op jit(solution)/shard_map/ppermute | solution.py:188
  2.1 9.6 %collective-permute-start.2 = (bf16[480,128]{1,0:T(8,128)(2,1)S(1)}, bf16[480,128]{1,0:T(8,128)(2,1)S(1)}, u32[]{:S(2)}, u32[]{:S(2)}) collective-permute-start(bf16[480,128]{1,0:T(8,128)(2,1)S(1)} %get-tuple-element.12), channel_id=1, source_target_pairs={{0,2},{1,3},{2,4},{3,5},{4,6},{5,7},{6,8},{7,9},{8,10},{9,11},{10,... | collective-permute-start | bytes 368648 | tf_op jit(solution)/shard_map/ppermute | solution.py:188
  4.7 0.7 %copy-start.3 = (f32[128]{0:T(128)S(1)}, f32[128]{0:T(128)}, u32[]{:S(2)}) copy-start(f32[128]{0:T(128)} %param.7) | copy-start | bytes 1540
  6.0 5.8 %collective-permute-start.1 = (bf16[480,128]{1,0:T(8,128)(2,1)S(1)}, bf16[480,128]{1,0:T(8,128)(2,1)S(1)}, u32[]{:S(2)}, u32[]{:S(2)}) collective-permute-start(bf16[480,128]{1,0:T(8,128)(2,1)S(1)} %add_convert_fusion.1), channel_id=1, source_target_pairs={{0,1},{1,0},{2,3},{3,2},{4,5},{5,4},{6,7},{7,6},{8,9},{9,8},{10,11... | collective-permute-start | bytes 368648 | tf_op jit(solution)/shard_map/ppermute | solution.py:188
  6.4 7.6 %collective-permute-start.4 = (bf16[480,128]{1,0:T(8,128)(2,1)S(1)}, bf16[480,128]{1,0:T(8,128)(2,1)S(1)}, u32[]{:S(2)}, u32[]{:S(2)}) collective-permute-start(bf16[480,128]{1,0:T(8,128)(2,1)S(1)} %add_convert_fusion.1), channel_id=1, source_target_pairs={{0,1},{1,8},{2,3},{3,10},{4,5},{5,12},{6,7},{7,14},{8,9},{9,0},{10... | collective-permute-start | bytes 368648 | tf_op jit(solution)/shard_map/ppermute | solution.py:188
  11.8 2.5 %collective-permute-start.8 = (bf16[480,128]{1,0:T(8,128)(2,1)S(1)}, bf16[480,128]{1,0:T(8,128)(2,1)S(1)}, u32[]{:S(2)}, u32[]{:S(2)}) collective-permute-start(bf16[480,128]{1,0:T(8,128)(2,1)S(1)} %add_convert_fusion), channel_id=1, source_target_pairs={{0,3},{1,0},{2,1},{3,2},{4,7},{5,4},{6,5},{7,6},{8,11},{9,8},{10,9... | collective-permute-start | bytes 368648 | tf_op jit(solution)/shard_map/ppermute | solution.py:188
  11.9 6.3 %collective-permute-start.5 = (bf16[480,128]{1,0:T(8,128)(2,1)S(1)}, bf16[480,128]{1,0:T(8,128)(2,1)S(1)}, u32[]{:S(2)}, u32[]{:S(2)}) collective-permute-start(bf16[480,128]{1,0:T(8,128)(2,1)S(1)} %add_convert_fusion), channel_id=1, source_target_pairs={{0,4},{1,9},{2,6},{3,11},{4,0},{5,13},{6,2},{7,15},{8,12},{9,1},{1... | collective-permute-start | bytes 368648 | tf_op jit(solution)/shard_map/ppermute | solution.py:188
  11.9 6.3 %collective-permute-start.3 = (bf16[480,128]{1,0:T(8,128)(2,1)S(1)}, bf16[480,128]{1,0:T(8,128)(2,1)S(1)}, u32[]{:S(2)}, u32[]{:S(2)}) collective-permute-start(bf16[480,128]{1,0:T(8,128)(2,1)S(1)} %add_convert_fusion), channel_id=1, source_target_pairs={{0,7},{1,0},{2,5},{3,2},{4,3},{5,4},{6,1},{7,6},{8,15},{9,8},{10,1... | collective-permute-start | bytes 368648 | tf_op jit(solution)/shard_map/ppermute | solution.py:188
  18.1 2.7 %collective-permute-start.6 = (bf16[480,128]{1,0:T(8,128)(2,1)S(1)}, bf16[480,128]{1,0:T(8,128)(2,1)S(1)}, u32[]{:S(2)}, u32[]{:S(2)}) collective-permute-start(bf16[480,128]{1,0:T(8,128)(2,1)S(1)} %get-tuple-element.17.refs_0_), channel_id=1, source_target_pairs={{0,1},{1,0},{2,3},{3,2},{4,5},{5,4},{6,7},{7,6},{8,9},{9,8},{10,11... | collective-permute-start | bytes 368648 | tf_op jit(solution)/shard_map/ppermute | solution.py:188
  22.1 4.6 %collective-permute-start.7 = (f32[4,480]{1,0:T(4,128)S(1)}, f32[4,480]{1,0:T(4,128)S(1)}, u32[]{:S(2)}, u32[]{:S(2)}) collective-permute-start(f32[4,480]{1,0:T(4,128)S(1)} %match.5), channel_id=1, source_target_pairs={{0,6},{1,7},{2,4},{3,5},{4,2},{5,3},{6,0},{7,1},{8,14},{9,15},{10,... | collective-permute-start | bytes 23048 | tf_op jit(solution)/shard_map/ppermute | solution.py:188
  24.3 3.7 %collective-permute-start.9 = (f32[4,480]{1,0:T(4,128)S(1)}, f32[4,480]{1,0:T(4,128)S(1)}, u32[]{:S(2)}, u32[]{:S(2)}) collective-permute-start(f32[4,480]{1,0:T(4,128)S(1)} %match.7), channel_id=1, source_target_pairs={{0,4},{1,3},{2,6},{3,1},{4,0},{5,7},{6,2},{7,5},{8,12},{9,11},{10,... | collective-permute-start | bytes 23048 | tf_op jit(solution)/shard_map/ppermute | solution.py:188
  28.1 1.2 %collective-permute-start.10 = (f32[4,480]{1,0:T(4,128)S(1)}, f32[4,480]{1,0:T(4,128)S(1)}, u32[]{:S(2)}, u32[]{:S(2)}) collective-permute-start(f32[4,480]{1,0:T(4,128)S(1)} %pad_maximum_fusion), channel_id=1, source_target_pairs={{0,1},{1,0},{2,3},{3,2},{4,5},{5,4},{6,7},{7,6},{8,9},{9,8},{10,11... | collective-permute-start | bytes 23048 | tf_op jit(solution)/shard_map/ppermute | solution.py:188

commit v4 on v3

--- a/solution.py
+++ b/solution.py
@@ -34,8 +34,9 @@
 
 
 def rim_kernel(
-    first_core_ref, query_hbm, target_hbm, weight_hbm, far_rim_ref, near_rim_ref, rows_ref, taps_ref, sems, *stages
+    query_hbm, target_hbm, weight_hbm, far_rim_ref, near_rim_ref, rows_ref, taps_ref, sems, *stages
 ):
+    first = lax.axis_index("target") == 0
     last = query_hbm.shape[0] - 1
     copies = [
         pltpu.make_async_copy(weight_hbm.at[pl.ds(0, 1)], taps_ref, sems.at[2]),
@@ -51,17 +52,17 @@
     target_rim = tap_row_sum(rows_ref[0], taps_ref, 0, stages[0])
     query_rim = tap_row_sum(rows_ref[1], taps_ref, 0, stages[1])
     near_rim_ref[...] = target_rim.astype(near_rim_ref.dtype)
-    far_rim_ref[...] = jnp.where(first_core_ref[0] == 1, query_rim, target_rim).astype(far_rim_ref.dtype)
-
-
-def rim_partials(first_core, query_input, target_input, conv_weight):
+    far_rim_ref[...] = jnp.where(first, query_rim, target_rim).astype(far_rim_ref.dtype)
+
+
+def rim_partials(query_input, target_input, conv_weight):
     _, cols, channels = query_input.shape
     out_channels = conv_weight.shape[3]
     hbm = pl.BlockSpec(memory_space=pltpu.HBM)
     return pl.pallas_call(
         rim_kernel,
         out_shape=(jax.ShapeDtypeStruct((cols // 2, out_channels), jnp.bfloat16),) * 2,
-        in_specs=[pl.BlockSpec(memory_space=pltpu.SMEM)] + [hbm] * 3,
+        in_specs=[hbm] * 3,
         out_specs=(pl.BlockSpec(memory_space=pltpu.VMEM),) * 2,
         scratch_shapes=[
             pltpu.VMEM((2, cols, channels), jnp.bfloat16),
@@ -71,7 +72,7 @@
         + [pltpu.VMEM((cols + 8, channels), jnp.float32)] * 2,
         compiler_params=pltpu.CompilerParams(vmem_limit_bytes=RIM_VMEM),
         name="rim_partials",
-    )(first_core, query_input, target_input, conv_weight)
+    )(query_input, target_input, conv_weight)
 
 
 def own_kernel(query_ref, target_ref, weight_ref, bias_ref, query_out, target_out, *stages):
@@ -109,26 +110,25 @@
     return (top, *[old * keep + new * gain for old, new in zip(state[1:], part[1:])])
 
 
-def match_kernel(shares, row_y_ref, query_ref, *refs):
-    target_refs = refs[:shares]
-    state_refs = refs[shares : -1 - shares]
-    out_ref = refs[-1 - shares]
-    scores_refs = refs[-shares:]
-    lanes, channels = query_ref.shape
+def match_kernel(row_ids, *refs):
+    core = lax.axis_index("target")
+    query_refs, target_refs = refs[:2], refs[2:6]
+    state_refs, out_ref, scores_refs = refs[6:-3], refs[-3], refs[-2:]
+    lanes, channels = query_refs[0].shape
     steps = target_refs[0].shape[0] // 8
     scale = LOG2E / math.sqrt(channels)
+    queries = jnp.where(core == 0, query_refs[0][...], query_refs[1][...])
     offset = lax.broadcasted_iota(jnp.int32, (8, lanes), 0).astype(jnp.float32)
+    for share, scores_ref in enumerate(scores_refs):
+        first_ref, second_ref = target_refs[2 * share : 2 * share + 2]
+        targets = jnp.where(core == 0, first_ref[...], second_ref[...])
+        scores_ref[...] = lax.dot_general(
+            targets, queries, (((1,), (1,)), ((), ())), preferred_element_type=jnp.float32
+        )
     state = None
     for state_ref in state_refs:
         state = tuple(state_ref[pl.ds(i, 1), :] for i in range(4))
-    for share in range(shares):
-        scores_ref = scores_refs[share]
-        scores_ref[...] = lax.dot_general(
-            target_refs[share][...],
-            query_ref[...],
-            (((1,), (1,)), ((), ())),
-            preferred_element_type=jnp.float32,
-        )
+    for row_id, scores_ref in zip(row_ids(lax.axis_index("query"), core), scores_refs):
         highest = scores_ref[pl.ds(0, 8), :]
         for step in range(1, steps):
             highest = jnp.maximum(highest, scores_ref[pl.ds(8 * step, 8), :])
@@ -142,31 +142,30 @@
                 stacked = stacked + plain
         part_x = jnp.sum(8.0 * stacked + offset * plain, axis=0, keepdims=True) * CELL
         part_sum = jnp.sum(plain, axis=0, keepdims=True)
-        part = (highest, part_sum, part_x, part_sum * row_y_ref[share])
+        part = (highest, part_sum, part_x, part_sum * (row_id.astype(jnp.float32) * CELL))
         state = part if state is None else merged(state, part, scale)
     out_ref[...] = jnp.concatenate(state, axis=0)
 
 
-def match(queries, targets, row_y, state=None):
-    shares = len(targets)
-    lanes, channels = queries.shape
-    row_width = targets[0].shape[0]
-    states = [] if state is None else [state]
+def match(queries, targets, row_ids, state=None):
+    lanes, channels = queries[0].shape
+    row_width = targets[0][0].shape[0]
+    operands = [*queries, *targets[0], *targets[1]] + ([] if state is None else [state])
     vmem = pl.BlockSpec(memory_space=pltpu.VMEM)
     return pl.pallas_call(
-        functools.partial(match_kernel, shares),
+        functools.partial(match_kernel, row_ids),
         out_shape=jax.ShapeDtypeStruct((4, lanes), jnp.float32),
-        in_specs=[pl.BlockSpec(memory_space=pltpu.SMEM)] + [vmem] * (1 + shares + len(states)),
+        in_specs=[vmem] * len(operands),
         out_specs=vmem,
-        scratch_shapes=[pltpu.VMEM((row_width, lanes), jnp.float32)] * shares,
+        scratch_shapes=[pltpu.VMEM((row_width, lanes), jnp.float32)] * 2,
         compiler_params=pltpu.CompilerParams(vmem_limit_bytes=VMEM_LIMIT),
         cost_estimate=pl.CostEstimate(
-            flops=2 * shares * lanes * row_width * channels,
+            flops=4 * lanes * row_width * channels,
             bytes_accessed=1 << 22,
-            transcendentals=shares * lanes * row_width,
+            transcendentals=2 * lanes * row_width,
         ),
         name="match",
-    )(row_y, queries, *targets, *states)
+    )(*operands)
 
 
 def combined(first, second, scale):
@@ -203,9 +202,7 @@
     def swapped(value):
         return routed(value, lambda s, c: (s, 1 - c))
 
-    far_rim, near_rim = rim_partials(
-        first.astype(jnp.int32).reshape(1), query_input, target_input, conv_weight
-    )
+    far_rim, near_rim = rim_partials(query_input, target_input, conv_weight)
     near_rim = swapped(near_rim)
     far_rim = routed(far_rim, lambda s, c: ((s + 1) % slots, c)).astype(jnp.float32)
     far_rim = jnp.where(slot == 0, 0.0, far_rim)
@@ -224,18 +221,17 @@
     corner = routed(whole, lambda s, c: (s ^ 3, 1) if c == 0 else (s, 0))
     beside = routed(whole, lambda s, c: (s ^ 1, 1) if c == 0 else (s, 0))
 
-    def row_y(ids):
-        return jnp.stack(ids).astype(jnp.float32) * CELL
-
-    members = [pick(whole, corner), pick(even_away[0], beside)]
-    rows = [pick(corner, whole), pick(handed, odd)]
-    ids = row_y([2 * slot, 2 * slot + 1])
-    states = [match(member, rows, ids) for member in members]
+    members = [(whole, corner), (even_away[0], beside)]
+    rows = [(corner, whole), (handed, odd)]
+    states = [match(member, rows, lambda s, c: (2 * s, 2 * s + 1)) for member in members]
     for hop in range(1, slots // 4):
-        source = (slot - 4 * hop) % slots
-        row = pick(odd_away[hop - 1], even_away[hop - 1])
-        rows = [row, swapped(row)]
-        ids = row_y([2 * source + 1 - core, 2 * source + core])
+        away = swapped(pick(odd_away[hop - 1], even_away[hop - 1]))
+        rows = [(odd_away[hop - 1], even_away[hop - 1]), (away, away)]
+
+        def ids(s, c):
+            source = lax.rem(s - 4 * hop + slots, slots)
+            return 2 * source + 1 - c, 2 * source + c
+
         states = [match(member, rows, ids, state) for member, state in zip(members, states)]
     state, other = states
     corner_state = routed(state, lambda s, c: (s ^ 3, c))

time: 30.1 us -> 27.3 us (0.907)
  Pallas kernels: 7.26 us -> 5.21 us
  starting transfers between devices: 8.16 us -> 6.51 us
  waiting for transfers between devices: 12.7 us -> 13.8 us
    pallas_call x4, Pallas kernels: 5.13 us -> 3.08 us  [match(): pl.pallas_call(functools.partial(match_kernel, row_ids), out_shape=jax.Sh...]
    ppermute x11, starting transfers between devices: 8.16 us -> 6.51 us  [routed(): return lax.ppermute(value, ('query', 'target'), pairs)]
    ppermute x11, waiting for transfers between devices: 12.7 us -> 13.8 us  [routed(): return lax.ppermute(value, ('query', 'target'), pairs)]
  transfers between devices with their start and end apart: 11 -> 11, of which waited for: 6 -> 4; matrix products, arithmetic and copies ran while one was open for 1% -> 0% of each run, Pallas kernels for 15% -> 11%
where the time goes in v4:
time: 27.3 us; the launch traced here: 27.1 us
  waiting for transfers between devices  13.8 us (51%)
  starting transfers between devices  6.51 us (24%)
  Pallas kernels  5.21 us (19%)
  local copies, waits for them, and re-layouts  1.25 us (5%)
    ppermute x11, waiting for transfers between devices, routed(): return lax.ppermute(value, ('query', 'target'), pairs)  13.8 us
    ppermute x11, starting transfers between devices, routed(): return lax.ppermute(value, ('query', 'target'), pairs)  6.51 us
    pallas_call x4, Pallas kernels, match(): pl.pallas_call(functools.partial(match_kernel, row_ids), out_shape=jax.Sh...  3.08 us
    pallas_call x1, Pallas kernels, rim_partials(): pl.pallas_call(rim_kernel, out_shape=(jax.ShapeDtypeStruct((cols // 2, ou...  1.59 us
    unnamed x8, local copies, waits for them, and re-layouts  0.66 us
    reshape x1, local copies, waits for them, and re-layouts, on_device(): return jnp.stack([flow_x, flow_y]).reshape(2, 1, row_width)  0.6 us
  transfers between devices with their start and end apart: 11, of which 4 were waited for; matrix products, arithmetic and copies ran while one was open for 0% of the time, Pallas kernels for 11%

profile of v4, /device:TPU:0, one launch (start us, length us, event | category | flops | bytes accessed | tf_op | source)
XLA Modules:
  0.0 27.1 jit_solution(567876761203565555)
XLA Ops:
  0.0 0.0 copy-start.2
  0.0 0.0 copy-start.1
  0.0 0.0 copy-start
  0.0 1.6 %rim_partials.1 = (bf16[480,128]{1,0:T(8,128)(2,1)S(1)}, bf16[480,128]{1,0:T(8,128)(2,1)S(1)}) custom-call(bf16[2,960,128]{2,1,0:T(8,128)(2,1)} %query_hbm.1, bf16[2,960,128]{2,1,0:T(8,128)(2,1)} %target_hbm.1, bf16[3,3,128,128]{3,2,1,0:T(8,128)(2,1)} %weight_hbm.1), custom_call_target="tpu_custom_call" | custom-call | tf_op jit(solution)/shard_map/rim_partials/pallas_call | solution.py:62
  1.6 0.5 %collective-permute-start = (bf16[480,128]{1,0:T(8,128)(2,1)S(1)}, bf16[480,128]{1,0:T(8,128)(2,1)S(1)}, u32[]{:S(2)}, u32[]{:S(2)}) collective-permute-start(bf16[480,128]{1,0:T(8,128)(2,1)S(1)} %get-tuple-element.11), channel_id=1, source_target_pairs={{0,1},{1,0},{2,3},{3,2},{4,5},{5,4},{6,7},{7,6},{8,9},{9,8},{10,11... | collective-permute-start | bytes 368648 | tf_op jit(solution)/shard_map/ppermute | solution.py:187
  2.1 2.6 %collective-permute-start.2 = (bf16[480,128]{1,0:T(8,128)(2,1)S(1)}, bf16[480,128]{1,0:T(8,128)(2,1)S(1)}, u32[]{:S(2)}, u32[]{:S(2)}) collective-permute-start(bf16[480,128]{1,0:T(8,128)(2,1)S(1)} %get-tuple-element.12), channel_id=1, source_target_pairs={{0,2},{1,3},{2,4},{3,5},{4,6},{5,7},{6,8},{7,9},{8,10},{9,11},{10,... | collective-permute-start | bytes 368648 | tf_op jit(solution)/shard_map/ppermute | solution.py:187
  4.7 0.0 copy-start.3
  4.7 0.0 copy-done.2
  4.7 0.0 copy-done.1
  4.7 0.0 copy-done
  4.7 0.6 %copy-done.3 = f32[128]{0:T(128)S(1)} copy-done((f32[128]{0:T(128)S(1)}, f32[128]{0:T(128)}, u32[]{:S(2)}) %copy-start.3) | copy-done | bytes 536
  5.4 0.5 %own_partials.1 = (f32[480,128]{1,0:T(8,128)S(1)}, f32[480,128]{1,0:T(8,128)S(1)}) custom-call(bf16[2,960,128]{2,1,0:T(8,128)(2,1)S(1)} %copy-done, bf16[2,960,128]{2,1,0:T(8,128)(2,1)S(1)} %copy-done.1, bf16[3,3,128,128]{3,2,1,0:T(8,128)(2,1)S(1)} %copy-done.2, f32[1,128]{1,0:T(1,128)S(1)} %bitcast.7), custom_call_target="tpu_custom_call" | custom-call | flops 188743680 | bytes 4194304 | tf_op jit(solution)/shard_map/own_partials/pallas_call | solution.py:96
  5.9 0.0 collective-permute-done
  6.0 0.2 collective-permute-start.1
  6.2 0.3 %collective-permute-start.4 = (bf16[480,128]{1,0:T(8,128)(2,1)S(1)}, bf16[480,128]{1,0:T(8,128)(2,1)S(1)}, u32[]{:S(2)}, u32[]{:S(2)}) collective-permute-start(bf16[480,128]{1,0:T(8,128)(2,1)S(1)} %add_convert_fusion.1.refs_5_), channel_id=1, source_target_pairs={{0,1},{1,8},{2,3},{3,10},{4,5},{5,12},{6,7},{7,14},{8,9},{9,0},{10... | collective-permute-start | bytes 368648 | tf_op jit(solution)/shard_map/ppermute | solution.py:187
  6.5 5.2 %collective-permute-done.2 = bf16[480,128]{1,0:T(8,128)(2,1)S(1)} collective-permute-done((bf16[480,128]{1,0:T(8,128)(2,1)S(1)}, bf16[480,128]{1,0:T(8,128)(2,1)S(1)}, u32[]{:S(2)}, u32[]{:S(2)}) %collective-permute-start.2) | collective-permute-done | bytes 122912 | tf_op jit(solution)/shard_map/ppermute | solution.py:187
  11.7 0.0 collective-permute-done.1.refs_4_
  11.7 0.1 add_convert_fusion.refs_0_.refs_3_
  11.8 0.1 collective-permute-start.5
  11.9 0.2 collective-permute-start.8
  12.1 1.0 %collective-permute-start.3 = (bf16[480,128]{1,0:T(8,128)(2,1)S(1)}, bf16[480,128]{1,0:T(8,128)(2,1)S(1)}, u32[]{:S(2)}, u32[]{:S(2)}) collective-permute-start(bf16[480,128]{1,0:T(8,128)(2,1)S(1)} %add_convert_fusion.refs_0_.refs_3_), channel_id=1, source_target_pairs={{0,7},{1,0},{2,5},{3,2},{4,3},{5,4},{6,1},{7,6},{8,15},{9,8},{10,1... | collective-permute-start | bytes 368648 | tf_op jit(solution)/shard_map/ppermute | solution.py:187
  13.1 0.0 collective-permute-done.4.refs_2_
  13.1 4.9 %collective-permute-done.5.refs_3_.refs_0_ = bf16[480,128]{1,0:T(8,128)(2,1)S(1)} collective-permute-done((bf16[480,128]{1,0:T(8,128)(2,1)S(1)}, bf16[480,128]{1,0:T(8,128)(2,1)S(1)}, u32[]{:S(2)}, u32[]{:S(2)}) %collective-permute-start.5) | collective-permute-done | bytes 122912 | tf_op jit(solution)/shard_map/ppermute | solution.py:187
  18.0 0.1 collective-permute-start.6
  18.1 0.0 collective-permute-done.3.refs_1_.refs_2_
  18.1 0.8 %match.4.refs_6_ = f32[4,480]{1,0:T(4,128)S(1)} custom-call(bf16[480,128]{1,0:T(8,128)(2,1)S(1)} %add_convert_fusion.refs_0_.refs_3_, bf16[480,128]{1,0:T(8,128)(2,1)S(1)} %collective-permute-done.3.refs_1_.refs_2_, bf16[480,128]{1,0:T(8,128)(2,1)S(1)} %collective-permute-done.3.refs_1_.refs_2_, bf16[480,128]{1,0:T(8,128)(2,1)S(1)} %add_convert_fusion.refs_0_.refs_3_, ...), custom_call_target="tpu_custom_call" | custom-call | flops 117964800 | bytes 4194304 | tf_op jit(solution)/shard_map/match/pallas_call | solution.py:155
  18.9 0.0 collective-permute-done.8.refs_1_
  18.9 0.8 %match.6.refs_6_ = f32[4,480]{1,0:T(4,128)S(1)} custom-call(bf16[480,128]{1,0:T(8,128)(2,1)S(1)} %collective-permute-done.5.refs_3_.refs_0_, bf16[480,128]{1,0:T(8,128)(2,1)S(1)} %collective-permute-done.8.refs_1_, bf16[480,128]{1,0:T(8,128)(2,1)S(1)} %collective-permute-done.3.refs_1_.refs_2_, bf16[480,128]{1,0:T(8,128)(2,1)S(1)} %add_convert_fusion.refs_0_.refs_3_, ...), custom_call_target="tpu_custom_call" | custom-call | flops 117964800 | bytes 4194304 | tf_op jit(solution)/shard_map/match/pallas_call | solution.py:155
  19.6 0.0 collective-permute-done.6.refs_4_.refs_5_
  19.7 0.8 %match.5 = f32[4,480]{1,0:T(4,128)S(1)} custom-call(bf16[480,128]{1,0:T(8,128)(2,1)S(1)} %add_convert_fusion.refs_0_.refs_3_, bf16[480,128]{1,0:T(8,128)(2,1)S(1)} %collective-permute-done.3.refs_1_.refs_2_, bf16[480,128]{1,0:T(8,128)(2,1)S(1)} %collective-permute-done.4.refs_2_, bf16[480,128]{1,0:T(8,128)(2,1)S(1)} %collective-permute-done.5.refs_3_.refs_0_, ...), custom_call_target="tpu_custom_call" | custom-call | flops 117964800 | bytes 4194304 | tf_op jit(solution)/shard_map/match/pallas_call | solution.py:155
  20.4 0.1 collective-permute-start.7
  20.5 0.8 %match.7 = f32[4,480]{1,0:T(4,128)S(1)} custom-call(bf16[480,128]{1,0:T(8,128)(2,1)S(1)} %collective-permute-done.5.refs_3_.refs_0_, bf16[480,128]{1,0:T(8,128)(2,1)S(1)} %collective-permute-done.8.refs_1_, bf16[480,128]{1,0:T(8,128)(2,1)S(1)} %collective-permute-done.4.refs_2_, bf16[480,128]{1,0:T(8,128)(2,1)S(1)} %collective-permute-done.5.refs_3_.refs_0_, ...), custom_call_target="tpu_custom_call" | custom-call | flops 117964800 | bytes 4194304 | tf_op jit(solution)/shard_map/match/pallas_call | solution.py:155
  21.3 1.3 %collective-permute-start.9 = (f32[4,480]{1,0:T(4,128)S(1)}, f32[4,480]{1,0:T(4,128)S(1)}, u32[]{:S(2)}, u32[]{:S(2)}) collective-permute-start(f32[4,480]{1,0:T(4,128)S(1)} %match.7), channel_id=1, source_target_pairs={{0,4},{1,3},{2,6},{3,1},{4,0},{5,7},{6,2},{7,5},{8,12},{9,11},{10,... | collective-permute-start | bytes 23048 | tf_op jit(solution)/shard_map/ppermute | solution.py:187
  22.6 2.5 %collective-permute-done.7 = f32[4,480]{1,0:T(4,128)S(1)} collective-permute-done((f32[4,480]{1,0:T(4,128)S(1)}, f32[4,480]{1,0:T(4,128)S(1)}, u32[]{:S(2)}, u32[]{:S(2)}) %collective-permute-start.7) | collective-permute-done | bytes 7712 | tf_op jit(solution)/shard_map/ppermute | solution.py:187
  25.1 0.0 collective-permute-done.9
  25.2 0.1 collective-permute-start.10
  25.3 1.1 %collective-permute-done.10 = f32[4,480]{1,0:T(4,128)S(1)} collective-permute-done((f32[4,480]{1,0:T(4,128)S(1)}, f32[4,480]{1,0:T(4,128)S(1)}, u32[]{:S(2)}, u32[]{:S(2)}) %collective-permute-start.10) | collective-permute-done | bytes 7712 | tf_op jit(solution)/shard_map/ppermute | solution.py:187
  26.5 0.6 %copy.5 = f32[2,1,480]{2,1,0:T(1,128)} copy(f32[2,1,480]{2,0,1:T(2,128)S(1)} %maximum_bitcast_fusion) | data formatting | bytes 7680 | tf_op jit(solution)/shard_map/reshape | solution.py:244
  (11 shorter events, 0.2 us)
Async XLA Ops:
  0.0 4.7 %copy-start.2 = (bf16[3,3,128,128]{3,2,1,0:T(8,128)(2,1)S(1)}, bf16[3,3,128,128]{3,2,1,0:T(8,128)(2,1)}, u32[]{:S(2)}) copy-start(bf16[3,3,128,128]{3,2,1,0:T(8,128)(2,1)} %weight_hbm.1) | copy-start | bytes 884740
  0.0 4.7 %copy-start.1 = (bf16[2,960,128]{2,1,0:T(8,128)(2,1)S(1)}, bf16[2,960,128]{2,1,0:T(8,128)(2,1)}, u32[]{:S(2)}) copy-start(bf16[2,960,128]{2,1,0:T(8,128)(2,1)} %target_hbm.1) | copy-start | bytes 1474564
  0.0 4.7 %copy-start = (bf16[2,960,128]{2,1,0:T(8,128)(2,1)S(1)}, bf16[2,960,128]{2,1,0:T(8,128)(2,1)}, u32[]{:S(2)}) copy-start(bf16[2,960,128]{2,1,0:T(8,128)(2,1)} %query_hbm.1) | copy-start | bytes 1474564
  1.6 4.3 %collective-permute-start = (bf16[480,128]{1,0:T(8,128)(2,1)S(1)}, bf16[480,128]{1,0:T(8,128)(2,1)S(1)}, u32[]{:S(2)}, u32[]{:S(2)}) collective-permute-start(bf16[480,128]{1,0:T(8,128)(2,1)S(1)} %get-tuple-element.11), channel_id=1, source_target_pairs={{0,1},{1,0},{2,3},{3,2},{4,5},{5,4},{6,7},{7,6},{8,9},{9,8},{10,11... | collective-permute-start | bytes 368648 | tf_op jit(solution)/shard_map/ppermute | solution.py:187
  2.1 9.6 %collective-permute-start.2 = (bf16[480,128]{1,0:T(8,128)(2,1)S(1)}, bf16[480,128]{1,0:T(8,128)(2,1)S(1)}, u32[]{:S(2)}, u32[]{:S(2)}) collective-permute-start(bf16[480,128]{1,0:T(8,128)(2,1)S(1)} %get-tuple-element.12), channel_id=1, source_target_pairs={{0,2},{1,3},{2,4},{3,5},{4,6},{5,7},{6,8},{7,9},{8,10},{9,11},{10,... | collective-permute-start | bytes 368648 | tf_op jit(solution)/shard_map/ppermute | solution.py:187
  4.7 0.7 %copy-start.3 = (f32[128]{0:T(128)S(1)}, f32[128]{0:T(128)}, u32[]{:S(2)}) copy-start(f32[128]{0:T(128)} %param.7) | copy-start | bytes 1540
  6.0 5.8 %collective-permute-start.1 = (bf16[480,128]{1,0:T(8,128)(2,1)S(1)}, bf16[480,128]{1,0:T(8,128)(2,1)S(1)}, u32[]{:S(2)}, u32[]{:S(2)}) collective-permute-start(bf16[480,128]{1,0:T(8,128)(2,1)S(1)} %add_convert_fusion.1.refs_5_), channel_id=1, source_target_pairs={{0,1},{1,0},{2,3},{3,2},{4,5},{5,4},{6,7},{7,6},{8,9},{9,8},{10,11... | collective-permute-start | bytes 368648 | tf_op jit(solution)/shard_map/ppermute | solution.py:187
  6.2 6.9 %collective-permute-start.4 = (bf16[480,128]{1,0:T(8,128)(2,1)S(1)}, bf16[480,128]{1,0:T(8,128)(2,1)S(1)}, u32[]{:S(2)}, u32[]{:S(2)}) collective-permute-start(bf16[480,128]{1,0:T(8,128)(2,1)S(1)} %add_convert_fusion.1.refs_5_), channel_id=1, source_target_pairs={{0,1},{1,8},{2,3},{3,10},{4,5},{5,12},{6,7},{7,14},{8,9},{9,0},{10... | collective-permute-start | bytes 368648 | tf_op jit(solution)/shard_map/ppermute | solution.py:187
  11.8 6.2 %collective-permute-start.5 = (bf16[480,128]{1,0:T(8,128)(2,1)S(1)}, bf16[480,128]{1,0:T(8,128)(2,1)S(1)}, u32[]{:S(2)}, u32[]{:S(2)}) collective-permute-start(bf16[480,128]{1,0:T(8,128)(2,1)S(1)} %add_convert_fusion.refs_0_.refs_3_), channel_id=1, source_target_pairs={{0,4},{1,9},{2,6},{3,11},{4,0},{5,13},{6,2},{7,15},{8,12},{9,1},{1... | collective-permute-start | bytes 368648 | tf_op jit(solution)/shard_map/ppermute | solution.py:187
  11.9 7.0 %collective-permute-start.8 = (bf16[480,128]{1,0:T(8,128)(2,1)S(1)}, bf16[480,128]{1,0:T(8,128)(2,1)S(1)}, u32[]{:S(2)}, u32[]{:S(2)}) collective-permute-start(bf16[480,128]{1,0:T(8,128)(2,1)S(1)} %add_convert_fusion.refs_0_.refs_3_), channel_id=1, source_target_pairs={{0,3},{1,0},{2,1},{3,2},{4,7},{5,4},{6,5},{7,6},{8,11},{9,8},{10,9... | collective-permute-start | bytes 368648 | tf_op jit(solution)/shard_map/ppermute | solution.py:187
  12.1 6.0 %collective-permute-start.3 = (bf16[480,128]{1,0:T(8,128)(2,1)S(1)}, bf16[480,128]{1,0:T(8,128)(2,1)S(1)}, u32[]{:S(2)}, u32[]{:S(2)}) collective-permute-start(bf16[480,128]{1,0:T(8,128)(2,1)S(1)} %add_convert_fusion.refs_0_.refs_3_), channel_id=1, source_target_pairs={{0,7},{1,0},{2,5},{3,2},{4,3},{5,4},{6,1},{7,6},{8,15},{9,8},{10,1... | collective-permute-start | bytes 368648 | tf_op jit(solution)/shard_map/ppermute | solution.py:187
  18.0 1.6 %collective-permute-start.6 = (bf16[480,128]{1,0:T(8,128)(2,1)S(1)}, bf16[480,128]{1,0:T(8,128)(2,1)S(1)}, u32[]{:S(2)}, u32[]{:S(2)}) collective-permute-start(bf16[480,128]{1,0:T(8,128)(2,1)S(1)} %broadcast_select_fusion), channel_id=1, source_target_pairs={{0,1},{1,0},{2,3},{3,2},{4,5},{5,4},{6,7},{7,6},{8,9},{9,8},{10,11... | collective-permute-start | bytes 368648 | tf_op jit(solution)/shard_map/ppermute | solution.py:187
  20.4 4.7 %collective-permute-start.7 = (f32[4,480]{1,0:T(4,128)S(1)}, f32[4,480]{1,0:T(4,128)S(1)}, u32[]{:S(2)}, u32[]{:S(2)}) collective-permute-start(f32[4,480]{1,0:T(4,128)S(1)} %match.5), channel_id=1, source_target_pairs={{0,6},{1,7},{2,4},{3,5},{4,2},{5,3},{6,0},{7,1},{8,14},{9,15},{10,... | collective-permute-start | bytes 23048 | tf_op jit(solution)/shard_map/ppermute | solution.py:187
  21.3 3.8 %collective-permute-start.9 = (f32[4,480]{1,0:T(4,128)S(1)}, f32[4,480]{1,0:T(4,128)S(1)}, u32[]{:S(2)}, u32[]{:S(2)}) collective-permute-start(f32[4,480]{1,0:T(4,128)S(1)} %match.7), channel_id=1, source_target_pairs={{0,4},{1,3},{2,6},{3,1},{4,0},{5,7},{6,2},{7,5},{8,12},{9,11},{10,... | collective-permute-start | bytes 23048 | tf_op jit(solution)/shard_map/ppermute | solution.py:187
  25.2 1.2 %collective-permute-start.10 = (f32[4,480]{1,0:T(4,128)S(1)}, f32[4,480]{1,0:T(4,128)S(1)}, u32[]{:S(2)}, u32[]{:S(2)}) collective-permute-start(f32[4,480]{1,0:T(4,128)S(1)} %pad_maximum_fusion), channel_id=1, source_target_pairs={{0,1},{1,0},{2,3},{3,2},{4,5},{5,4},{6,7},{7,6},{8,9},{9,8},{10,11... | collective-permute-start | bytes 23048 | tf_op jit(solution)/shard_map/ppermute | solution.py:187

commit v5 on v4

--- a/solution.py
+++ b/solution.py
@@ -110,59 +110,68 @@
     return (top, *[old * keep + new * gain for old, new in zip(state[1:], part[1:])])
 
 
-def match_kernel(row_ids, *refs):
+def match_kernel(members, carried, row_ids, *refs):
     core = lax.axis_index("target")
-    query_refs, target_refs = refs[:2], refs[2:6]
-    state_refs, out_ref, scores_refs = refs[6:-3], refs[-3], refs[-2:]
-    lanes, channels = query_refs[0].shape
-    steps = target_refs[0].shape[0] // 8
+    refs = list(refs)
+    query_pairs = [(refs.pop(0), refs.pop(0)) for _ in range(members)]
+    target_pairs = [(refs.pop(0), refs.pop(0)) for _ in range(2)]
+    state_refs = [refs.pop(0) for _ in range(members if carried else 0)]
+    out_refs = [refs.pop(0) for _ in range(members)]
+    lanes, channels = query_pairs[0][0].shape
+    steps = target_pairs[0][0].shape[0] // 8
     scale = LOG2E / math.sqrt(channels)
-    queries = jnp.where(core == 0, query_refs[0][...], query_refs[1][...])
     offset = lax.broadcasted_iota(jnp.int32, (8, lanes), 0).astype(jnp.float32)
-    for share, scores_ref in enumerate(scores_refs):
-        first_ref, second_ref = target_refs[2 * share : 2 * share + 2]
-        targets = jnp.where(core == 0, first_ref[...], second_ref[...])
-        scores_ref[...] = lax.dot_general(
-            targets, queries, (((1,), (1,)), ((), ())), preferred_element_type=jnp.float32
-        )
-    state = None
-    for state_ref in state_refs:
-        state = tuple(state_ref[pl.ds(i, 1), :] for i in range(4))
-    for row_id, scores_ref in zip(row_ids(lax.axis_index("query"), core), scores_refs):
-        highest = scores_ref[pl.ds(0, 8), :]
-        for step in range(1, steps):
-            highest = jnp.maximum(highest, scores_ref[pl.ds(8 * step, 8), :])
-        highest = jnp.max(highest, axis=0, keepdims=True)
-        spread = jnp.broadcast_to(highest, (8, lanes))
-        plain = jnp.zeros((8, lanes), jnp.float32)
-        stacked = jnp.zeros((8, lanes), jnp.float32)
-        for step in reversed(range(steps)):
-            plain = plain + jnp.exp2((scores_ref[pl.ds(8 * step, 8), :] - spread) * scale)
-            if step:
-                stacked = stacked + plain
-        part_x = jnp.sum(8.0 * stacked + offset * plain, axis=0, keepdims=True) * CELL
-        part_sum = jnp.sum(plain, axis=0, keepdims=True)
-        part = (highest, part_sum, part_x, part_sum * (row_id.astype(jnp.float32) * CELL))
-        state = part if state is None else merged(state, part, scale)
-    out_ref[...] = jnp.concatenate(state, axis=0)
-
-
-def match(queries, targets, row_ids, state=None):
-    lanes, channels = queries[0].shape
+    targets = [jnp.where(core == 0, one[...], two[...]) for one, two in target_pairs]
+    for member, (one, two) in enumerate(query_pairs):
+        queries = jnp.where(core == 0, one[...], two[...])
+        for share in range(2):
+            refs[2 * member + share][...] = lax.dot_general(
+                targets[share],
+                queries,
+                (((1,), (1,)), ((), ())),
+                preferred_element_type=jnp.float32,
+            )
+    for member, out_ref in enumerate(out_refs):
+        state = None
+        if carried:
+            state = tuple(state_refs[member][pl.ds(i, 1), :] for i in range(4))
+        for share, row_id in enumerate(row_ids(lax.axis_index("query"), core)):
+            scores_ref = refs[2 * member + share]
+            highest = scores_ref[pl.ds(0, 8), :]
+            for step in range(1, steps):
+                highest = jnp.maximum(highest, scores_ref[pl.ds(8 * step, 8), :])
+            highest = jnp.max(highest, axis=0, keepdims=True)
+            spread = jnp.broadcast_to(highest, (8, lanes))
+            plain = jnp.zeros((8, lanes), jnp.float32)
+            stacked = jnp.zeros((8, lanes), jnp.float32)
+            for step in reversed(range(steps)):
+                plain = plain + jnp.exp2((scores_ref[pl.ds(8 * step, 8), :] - spread) * scale)
+                if step:
+                    stacked = stacked + plain
+            part_x = jnp.sum(8.0 * stacked + offset * plain, axis=0, keepdims=True) * CELL
+            part_sum = jnp.sum(plain, axis=0, keepdims=True)
+            part = (highest, part_sum, part_x, part_sum * (row_id.astype(jnp.float32) * CELL))
+            state = part if state is None else merged(state, part, scale)
+        out_ref[...] = jnp.concatenate(state, axis=0)
+
+
+def match(members, targets, row_ids, states=()):
+    lanes, channels = members[0][0].shape
     row_width = targets[0][0].shape[0]
-    operands = [*queries, *targets[0], *targets[1]] + ([] if state is None else [state])
+    count = len(members)
+    operands = [ref for pair in (*members, *targets) for ref in pair] + list(states)
     vmem = pl.BlockSpec(memory_space=pltpu.VMEM)
     return pl.pallas_call(
-        functools.partial(match_kernel, row_ids),
-        out_shape=jax.ShapeDtypeStruct((4, lanes), jnp.float32),
+        functools.partial(match_kernel, count, bool(states), row_ids),
+        out_shape=(jax.ShapeDtypeStruct((4, lanes), jnp.float32),) * count,
         in_specs=[vmem] * len(operands),
-        out_specs=vmem,
-        scratch_shapes=[pltpu.VMEM((row_width, lanes), jnp.float32)] * 2,
+        out_specs=(vmem,) * count,
+        scratch_shapes=[pltpu.VMEM((row_width, lanes), jnp.float32)] * (2 * count),
         compiler_params=pltpu.CompilerParams(vmem_limit_bytes=VMEM_LIMIT),
         cost_estimate=pl.CostEstimate(
-            flops=4 * lanes * row_width * channels,
+            flops=4 * count * lanes * row_width * channels,
             bytes_accessed=1 << 22,
-            transcendentals=2 * lanes * row_width,
+            transcendentals=2 * count * lanes * row_width,
         ),
         name="match",
     )(*operands)
@@ -215,15 +224,15 @@
     ]
     whole = (pick(query_part, handed.astype(jnp.float32)) + far_rim).astype(jnp.bfloat16)
     even_away = [
-        routed(whole, lambda s, c: (s ^ 2, 0) if c == 0 else ((s + 4 * hop) % slots, 1))
+        routed(whole, lambda s, c: (s ^ 1, 0) if c == 0 else ((s + 4 * hop) % slots, 1))
         for hop in range(1, max(2, slots // 4))
     ]
+    below = routed(whole, lambda s, c: (s ^ 2, 1) if c == 0 else (s, 0))
     corner = routed(whole, lambda s, c: (s ^ 3, 1) if c == 0 else (s, 0))
-    beside = routed(whole, lambda s, c: (s ^ 1, 1) if c == 0 else (s, 0))
-
-    members = [(whole, corner), (even_away[0], beside)]
-    rows = [(corner, whole), (handed, odd)]
-    states = [match(member, rows, lambda s, c: (2 * s, 2 * s + 1)) for member in members]
+
+    members = [(whole, below), (even_away[0], corner)]
+    rows = [(below, whole), (handed, odd)]
+    states = [match([member], rows, lambda s, c: (2 * s, 2 * s + 1))[0] for member in members]
     for hop in range(1, slots // 4):
         away = swapped(pick(odd_away[hop - 1], even_away[hop - 1]))
         rows = [(odd_away[hop - 1], even_away[hop - 1]), (away, away)]
@@ -232,11 +241,11 @@
             source = lax.rem(s - 4 * hop + slots, slots)
             return 2 * source + 1 - c, 2 * source + c
 
-        states = [match(member, rows, ids, state) for member, state in zip(members, states)]
+        states = match(members, rows, ids, states)
     state, other = states
-    corner_state = routed(state, lambda s, c: (s ^ 3, c))
-    other = routed(other, lambda s, c: (s ^ (2 if c == 0 else 1), c))
-    own = combined(pick(state, corner_state), other, scale)
+    other = routed(other, lambda s, c: (s ^ (1 if c == 0 else 3), c))
+    below_state = routed(state, lambda s, c: (s ^ (1 if c == 0 else 2), c))
+    own = combined(pick(state, below_state), other, scale)
     total = combined(own, swapped(own), scale)
     columns = jnp.arange(row_width, dtype=jnp.int32).astype(jnp.float32) * CELL
     flow_x = total[2] / total[1] - columns

time: 27.3 us -> 26.4 us (0.967)
  waiting for transfers between devices: 13.8 us -> 12 us
  starting transfers between devices: 6.51 us -> 7.72 us
  Pallas kernels: 5.21 us -> 4.91 us
    ppermute x11, waiting for transfers between devices: 13.8 us -> 12 us  [routed(): return lax.ppermute(value, ('query', 'target'), pairs)]
    ppermute x11, starting transfers between devices: 6.51 us -> 7.72 us  [routed(): return lax.ppermute(value, ('query', 'target'), pairs)]
    pallas_call x4 -> x3, Pallas kernels: 3.08 us -> 2.78 us  [match(): pl.pallas_call(functools.partial(match_kernel, count, bool(states), row_i...]
  transfers between devices with their start and end apart: 11 -> 11, of which waited for: 4 -> 5; matrix products, arithmetic and copies ran while one was open for 0% -> 0% of each run, Pallas kernels for 11% -> 8%
where the time goes in v5:
time: 26.4 us; the launch traced here: 26.2 us
  waiting for transfers between devices  12 us (45%)
  starting transfers between devices  7.72 us (29%)
  Pallas kernels  4.91 us (19%)
  local copies, waits for them, and re-layouts  1.25 us (5%)
    ppermute x11, waiting for transfers between devices, routed(): return lax.ppermute(value, ('query', 'target'), pairs)  12 us
    ppermute x11, starting transfers between devices, routed(): return lax.ppermute(value, ('query', 'target'), pairs)  7.72 us
    pallas_call x3, Pallas kernels, match(): pl.pallas_call(functools.partial(match_kernel, count, bool(states), row_i...  2.78 us
    pallas_call x1, Pallas kernels, rim_partials(): pl.pallas_call(rim_kernel, out_shape=(jax.ShapeDtypeStruct((cols // 2, ou...  1.59 us
    unnamed x8, local copies, waits for them, and re-layouts  0.66 us
    reshape x1, local copies, waits for them, and re-layouts, on_device(): return jnp.stack([flow_x, flow_y]).reshape(2, 1, row_width)  0.6 us
    pallas_call x1, Pallas kernels, own_partials(): pl.pallas_call(own_kernel, out_shape=(part, part), scratch_shapes=[pltpu....  0.54 us
  transfers between devices with their start and end apart: 11, of which 5 were waited for; matrix products, arithmetic and copies ran while one was open for 0% of the time, Pallas kernels for 8%

profile of v5, /device:TPU:0, one launch (start us, length us, event | category | flops | bytes accessed | tf_op | source)
XLA Modules:
  0.0 26.2 jit_solution(12530169283710996910)
XLA Ops:
  0.0 0.0 copy-start
  0.0 0.0 copy-start.1
  0.0 0.0 copy-start.2
  0.0 1.6 %rim_partials.1 = (bf16[480,128]{1,0:T(8,128)(2,1)S(1)}, bf16[480,128]{1,0:T(8,128)(2,1)S(1)}) custom-call(bf16[2,960,128]{2,1,0:T(8,128)(2,1)} %query_hbm.1, bf16[2,960,128]{2,1,0:T(8,128)(2,1)} %target_hbm.1, bf16[3,3,128,128]{3,2,1,0:T(8,128)(2,1)} %weight_hbm.1), custom_call_target="tpu_custom_call" | custom-call | tf_op jit(solution)/shard_map/rim_partials/pallas_call | solution.py:62
  1.6 0.5 %collective-permute-start = (bf16[480,128]{1,0:T(8,128)(2,1)S(1)}, bf16[480,128]{1,0:T(8,128)(2,1)S(1)}, u32[]{:S(2)}, u32[]{:S(2)}) collective-permute-start(bf16[480,128]{1,0:T(8,128)(2,1)S(1)} %get-tuple-element.13), channel_id=1, source_target_pairs={{0,1},{1,0},{2,3},{3,2},{4,5},{5,4},{6,7},{7,6},{8,9},{9,8},{10,11... | collective-permute-start | bytes 368648 | tf_op jit(solution)/shard_map/ppermute | solution.py:196
  2.1 2.6 %collective-permute-start.2 = (bf16[480,128]{1,0:T(8,128)(2,1)S(1)}, bf16[480,128]{1,0:T(8,128)(2,1)S(1)}, u32[]{:S(2)}, u32[]{:S(2)}) collective-permute-start(bf16[480,128]{1,0:T(8,128)(2,1)S(1)} %get-tuple-element.14), channel_id=1, source_target_pairs={{0,2},{1,3},{2,4},{3,5},{4,6},{5,7},{6,8},{7,9},{8,10},{9,11},{10,... | collective-permute-start | bytes 368648 | tf_op jit(solution)/shard_map/ppermute | solution.py:196
  4.7 0.0 copy-start.3
  4.7 0.0 copy-done
  4.7 0.0 copy-done.1
  4.7 0.0 copy-done.2
  4.7 0.6 %copy-done.3 = f32[128]{0:T(128)S(1)} copy-done((f32[128]{0:T(128)S(1)}, f32[128]{0:T(128)}, u32[]{:S(2)}) %copy-start.3) | copy-done | bytes 536
  5.4 0.5 %own_partials.1 = (f32[480,128]{1,0:T(8,128)S(1)}, f32[480,128]{1,0:T(8,128)S(1)}) custom-call(bf16[2,960,128]{2,1,0:T(8,128)(2,1)S(1)} %copy-done, bf16[2,960,128]{2,1,0:T(8,128)(2,1)S(1)} %copy-done.1, bf16[3,3,128,128]{3,2,1,0:T(8,128)(2,1)S(1)} %copy-done.2, f32[1,128]{1,0:T(1,128)S(1)} %bitcast.7), custom_call_target="tpu_custom_call" | custom-call | flops 188743680 | bytes 4194304 | tf_op jit(solution)/shard_map/own_partials/pallas_call | solution.py:96
  5.9 0.0 collective-permute-done
  6.0 0.2 collective-permute-start.1
  6.2 0.3 %collective-permute-start.6 = (bf16[480,128]{1,0:T(8,128)(2,1)S(1)}, bf16[480,128]{1,0:T(8,128)(2,1)S(1)}, u32[]{:S(2)}, u32[]{:S(2)}) collective-permute-start(bf16[480,128]{1,0:T(8,128)(2,1)S(1)} %add_convert_fusion.1.refs_5_), channel_id=1, source_target_pairs={{0,1},{1,8},{2,3},{3,10},{4,5},{5,12},{6,7},{7,14},{8,9},{9,0},{10... | collective-permute-start | bytes 368648 | tf_op jit(solution)/shard_map/ppermute | solution.py:196
  6.5 5.2 %collective-permute-done.2 = bf16[480,128]{1,0:T(8,128)(2,1)S(1)} collective-permute-done((bf16[480,128]{1,0:T(8,128)(2,1)S(1)}, bf16[480,128]{1,0:T(8,128)(2,1)S(1)}, u32[]{:S(2)}, u32[]{:S(2)}) %collective-permute-start.2) | collective-permute-done | bytes 122912 | tf_op jit(solution)/shard_map/ppermute | solution.py:196
  11.7 0.0 collective-permute-done.1.refs_4_
  11.7 0.1 add_convert_fusion.refs_0_.refs_3_
  11.8 0.1 collective-permute-start.4
  11.9 1.2 %collective-permute-start.3 = (bf16[480,128]{1,0:T(8,128)(2,1)S(1)}, bf16[480,128]{1,0:T(8,128)(2,1)S(1)}, u32[]{:S(2)}, u32[]{:S(2)}) collective-permute-start(bf16[480,128]{1,0:T(8,128)(2,1)S(1)} %add_convert_fusion.refs_0_.refs_3_), channel_id=1, source_target_pairs={{0,5},{1,0},{2,7},{3,2},{4,1},{5,4},{6,3},{7,6},{8,13},{9,8},{10,1... | collective-permute-start | bytes 368648 | tf_op jit(solution)/shard_map/ppermute | solution.py:196
  13.0 0.1 collective-permute-start.5
  13.1 0.0 collective-permute-done.6.refs_4_
  13.1 3.6 %collective-permute-done.4.refs_0_.refs_2_.refs_5_ = bf16[480,128]{1,0:T(8,128)(2,1)S(1)} collective-permute-done((bf16[480,128]{1,0:T(8,128)(2,1)S(1)}, bf16[480,128]{1,0:T(8,128)(2,1)S(1)}, u32[]{:S(2)}, u32[]{:S(2)}) %collective-permute-start.4) | collective-permute-done | bytes 122912 | tf_op jit(solution)/shard_map/ppermute | solution.py:196
  16.8 0.1 collective-permute-start.7
  16.8 0.0 collective-permute-done.3.refs_1_.refs_2_
  16.9 0.8 %match.3.refs_8_ = f32[4,480]{1,0:T(4,128)S(1)} custom-call(bf16[480,128]{1,0:T(8,128)(2,1)S(1)} %add_convert_fusion.refs_0_.refs_3_, bf16[480,128]{1,0:T(8,128)(2,1)S(1)} %collective-permute-done.3.refs_1_.refs_2_, bf16[480,128]{1,0:T(8,128)(2,1)S(1)} %collective-permute-done.3.refs_1_.refs_2_, bf16[480,128]{1,0:T(8,128)(2,1)S(1)} %add_convert_fusion.refs_0_.refs_3_, ...), custom_call_target="tpu_custom_call" | custom-call | flops 117964800 | bytes 4194304 | tf_op jit(solution)/shard_map/match/pallas_call | solution.py:164
  17.6 0.0 collective-permute-done.5.refs_1_.refs_3_
  17.6 0.8 %match.4.refs_9_ = f32[4,480]{1,0:T(4,128)S(1)} custom-call(bf16[480,128]{1,0:T(8,128)(2,1)S(1)} %collective-permute-done.4.refs_0_.refs_2_.refs_5_, bf16[480,128]{1,0:T(8,128)(2,1)S(1)} %collective-permute-done.5.refs_1_.refs_3_, bf16[480,128]{1,0:T(8,128)(2,1)S(1)} %collective-permute-done.3.refs_1_.refs_2_, ...), custom_call_target="tpu_custom_call" | custom-call | flops 117964800 | bytes 4194304 | tf_op jit(solution)/shard_map/match/pallas_call | solution.py:164
  18.4 0.0 collective-permute-done.7.refs_6_.refs_7_
  18.4 1.3 %match.5 = (f32[4,480]{1,0:T(4,128)S(1)}, f32[4,480]{1,0:T(4,128)S(1)}) custom-call(bf16[480,128]{1,0:T(8,128)(2,1)S(1)} %add_convert_fusion.refs_0_.refs_3_, bf16[480,128]{1,0:T(8,128)(2,1)S(1)} %collective-permute-done.3.refs_1_.refs_2_, bf16[480,128]{1,0:T(8,128)(2,1)S(1)} %collective-permute-done.4.refs_0_.refs_2_.refs_5_, ...), custom_call_target="tpu_custom_call" | custom-call | flops 235929600 | bytes 4194304 | tf_op jit(solution)/shard_map/match/pallas_call | solution.py:164
  19.7 0.7 %collective-permute-start.8 = (f32[4,480]{1,0:T(4,128)S(1)}, f32[4,480]{1,0:T(4,128)S(1)}, u32[]{:S(2)}, u32[]{:S(2)}) collective-permute-start(f32[4,480]{1,0:T(4,128)S(1)} %get-tuple-element.15), channel_id=1, source_target_pairs={{0,2},{1,5},{2,0},{3,7},{4,6},{5,1},{6,4},{7,3},{8,10},{9,13},{10,... | collective-permute-start | bytes 23048 | tf_op jit(solution)/shard_map/ppermute | solution.py:196
  20.4 1.4 %collective-permute-start.9 = (f32[4,480]{1,0:T(4,128)S(1)}, f32[4,480]{1,0:T(4,128)S(1)}, u32[]{:S(2)}, u32[]{:S(2)}) collective-permute-start(f32[4,480]{1,0:T(4,128)S(1)} %get-tuple-element.16), channel_id=1, source_target_pairs={{0,2},{1,7},{2,0},{3,5},{4,6},{5,3},{6,4},{7,1},{8,10},{9,15},{10,... | collective-permute-start | bytes 23048 | tf_op jit(solution)/shard_map/ppermute | solution.py:196
  21.8 1.6 %collective-permute-done.8 = f32[4,480]{1,0:T(4,128)S(1)} collective-permute-done((f32[4,480]{1,0:T(4,128)S(1)}, f32[4,480]{1,0:T(4,128)S(1)}, u32[]{:S(2)}, u32[]{:S(2)}) %collective-permute-start.8) | collective-permute-done | bytes 7712 | tf_op jit(solution)/shard_map/ppermute | solution.py:196
  23.4 0.7 %collective-permute-done.9 = f32[4,480]{1,0:T(4,128)S(1)} collective-permute-done((f32[4,480]{1,0:T(4,128)S(1)}, f32[4,480]{1,0:T(4,128)S(1)}, u32[]{:S(2)}, u32[]{:S(2)}) %collective-permute-start.9) | collective-permute-done | bytes 7712 | tf_op jit(solution)/shard_map/ppermute | solution.py:196
  24.1 0.6 %collective-permute-start.10 = (f32[4,480]{1,0:T(4,128)S(1)}, f32[4,480]{1,0:T(4,128)S(1)}, u32[]{:S(2)}, u32[]{:S(2)}) collective-permute-start(f32[4,480]{1,0:T(4,128)S(1)} %pad_maximum_fusion), channel_id=1, source_target_pairs={{0,1},{1,0},{2,3},{3,2},{4,5},{5,4},{6,7},{7,6},{8,9},{9,8},{10,11... | collective-permute-start | bytes 23048 | tf_op jit(solution)/shard_map/ppermute | solution.py:196
  24.7 0.8 %collective-permute-done.10 = f32[4,480]{1,0:T(4,128)S(1)} collective-permute-done((f32[4,480]{1,0:T(4,128)S(1)}, f32[4,480]{1,0:T(4,128)S(1)}, u32[]{:S(2)}, u32[]{:S(2)}) %collective-permute-start.10) | collective-permute-done | bytes 7712 | tf_op jit(solution)/shard_map/ppermute | solution.py:196
  25.6 0.6 %copy.5 = f32[2,1,480]{2,1,0:T(1,128)} copy(f32[2,1,480]{2,0,1:T(2,128)S(1)} %maximum_bitcast_fusion) | data formatting | bytes 7680 | tf_op jit(solution)/shard_map/reshape | solution.py:253
  (11 shorter events, 0.2 us)
Async XLA Ops:
  0.0 4.7 %copy-start = (bf16[2,960,128]{2,1,0:T(8,128)(2,1)S(1)}, bf16[2,960,128]{2,1,0:T(8,128)(2,1)}, u32[]{:S(2)}) copy-start(bf16[2,960,128]{2,1,0:T(8,128)(2,1)} %query_hbm.1) | copy-start | bytes 1474564
  0.0 4.7 %copy-start.1 = (bf16[2,960,128]{2,1,0:T(8,128)(2,1)S(1)}, bf16[2,960,128]{2,1,0:T(8,128)(2,1)}, u32[]{:S(2)}) copy-start(bf16[2,960,128]{2,1,0:T(8,128)(2,1)} %target_hbm.1) | copy-start | bytes 1474564
  0.0 4.7 %copy-start.2 = (bf16[3,3,128,128]{3,2,1,0:T(8,128)(2,1)S(1)}, bf16[3,3,128,128]{3,2,1,0:T(8,128)(2,1)}, u32[]{:S(2)}) copy-start(bf16[3,3,128,128]{3,2,1,0:T(8,128)(2,1)} %weight_hbm.1) | copy-start | bytes 884740
  1.6 4.3 %collective-permute-start = (bf16[480,128]{1,0:T(8,128)(2,1)S(1)}, bf16[480,128]{1,0:T(8,128)(2,1)S(1)}, u32[]{:S(2)}, u32[]{:S(2)}) collective-permute-start(bf16[480,128]{1,0:T(8,128)(2,1)S(1)} %get-tuple-element.13), channel_id=1, source_target_pairs={{0,1},{1,0},{2,3},{3,2},{4,5},{5,4},{6,7},{7,6},{8,9},{9,8},{10,11... | collective-permute-start | bytes 368648 | tf_op jit(solution)/shard_map/ppermute | solution.py:196
  2.1 9.6 %collective-permute-start.2 = (bf16[480,128]{1,0:T(8,128)(2,1)S(1)}, bf16[480,128]{1,0:T(8,128)(2,1)S(1)}, u32[]{:S(2)}, u32[]{:S(2)}) collective-permute-start(bf16[480,128]{1,0:T(8,128)(2,1)S(1)} %get-tuple-element.14), channel_id=1, source_target_pairs={{0,2},{1,3},{2,4},{3,5},{4,6},{5,7},{6,8},{7,9},{8,10},{9,11},{10,... | collective-permute-start | bytes 368648 | tf_op jit(solution)/shard_map/ppermute | solution.py:196
  4.7 0.7 %copy-start.3 = (f32[128]{0:T(128)S(1)}, f32[128]{0:T(128)}, u32[]{:S(2)}) copy-start(f32[128]{0:T(128)} %param.7) | copy-start | bytes 1540
  6.0 5.8 %collective-permute-start.1 = (bf16[480,128]{1,0:T(8,128)(2,1)S(1)}, bf16[480,128]{1,0:T(8,128)(2,1)S(1)}, u32[]{:S(2)}, u32[]{:S(2)}) collective-permute-start(bf16[480,128]{1,0:T(8,128)(2,1)S(1)} %add_convert_fusion.1.refs_5_), channel_id=1, source_target_pairs={{0,1},{1,0},{2,3},{3,2},{4,5},{5,4},{6,7},{7,6},{8,9},{9,8},{10,11... | collective-permute-start | bytes 368648 | tf_op jit(solution)/shard_map/ppermute | solution.py:196
  6.2 6.9 %collective-permute-start.6 = (bf16[480,128]{1,0:T(8,128)(2,1)S(1)}, bf16[480,128]{1,0:T(8,128)(2,1)S(1)}, u32[]{:S(2)}, u32[]{:S(2)}) collective-permute-start(bf16[480,128]{1,0:T(8,128)(2,1)S(1)} %add_convert_fusion.1.refs_5_), channel_id=1, source_target_pairs={{0,1},{1,8},{2,3},{3,10},{4,5},{5,12},{6,7},{7,14},{8,9},{9,0},{10... | collective-permute-start | bytes 368648 | tf_op jit(solution)/shard_map/ppermute | solution.py:196
  11.8 4.9 %collective-permute-start.4 = (bf16[480,128]{1,0:T(8,128)(2,1)S(1)}, bf16[480,128]{1,0:T(8,128)(2,1)S(1)}, u32[]{:S(2)}, u32[]{:S(2)}) collective-permute-start(bf16[480,128]{1,0:T(8,128)(2,1)S(1)} %add_convert_fusion.refs_0_.refs_3_), channel_id=1, source_target_pairs={{0,2},{1,9},{2,0},{3,11},{4,6},{5,13},{6,4},{7,15},{8,10},{9,1},{1... | collective-permute-start | bytes 368648 | tf_op jit(solution)/shard_map/ppermute | solution.py:196
  11.9 5.0 %collective-permute-start.3 = (bf16[480,128]{1,0:T(8,128)(2,1)S(1)}, bf16[480,128]{1,0:T(8,128)(2,1)S(1)}, u32[]{:S(2)}, u32[]{:S(2)}) collective-permute-start(bf16[480,128]{1,0:T(8,128)(2,1)S(1)} %add_convert_fusion.refs_0_.refs_3_), channel_id=1, source_target_pairs={{0,5},{1,0},{2,7},{3,2},{4,1},{5,4},{6,3},{7,6},{8,13},{9,8},{10,1... | collective-permute-start | bytes 368648 | tf_op jit(solution)/shard_map/ppermute | solution.py:196
  13.0 4.6 %collective-permute-start.5 = (bf16[480,128]{1,0:T(8,128)(2,1)S(1)}, bf16[480,128]{1,0:T(8,128)(2,1)S(1)}, u32[]{:S(2)}, u32[]{:S(2)}) collective-permute-start(bf16[480,128]{1,0:T(8,128)(2,1)S(1)} %add_convert_fusion.refs_0_.refs_3_), channel_id=1, source_target_pairs={{0,7},{1,0},{2,5},{3,2},{4,3},{5,4},{6,1},{7,6},{8,15},{9,8},{10,1... | collective-permute-start | bytes 368648 | tf_op jit(solution)/shard_map/ppermute | solution.py:196
  16.8 1.6 %collective-permute-start.7 = (bf16[480,128]{1,0:T(8,128)(2,1)S(1)}, bf16[480,128]{1,0:T(8,128)(2,1)S(1)}, u32[]{:S(2)}, u32[]{:S(2)}) collective-permute-start(bf16[480,128]{1,0:T(8,128)(2,1)S(1)} %broadcast_select_fusion), channel_id=1, source_target_pairs={{0,1},{1,0},{2,3},{3,2},{4,5},{5,4},{6,7},{7,6},{8,9},{9,8},{10,11... | collective-permute-start | bytes 368648 | tf_op jit(solution)/shard_map/ppermute | solution.py:196
  19.7 3.7 %collective-permute-start.8 = (f32[4,480]{1,0:T(4,128)S(1)}, f32[4,480]{1,0:T(4,128)S(1)}, u32[]{:S(2)}, u32[]{:S(2)}) collective-permute-start(f32[4,480]{1,0:T(4,128)S(1)} %get-tuple-element.15), channel_id=1, source_target_pairs={{0,2},{1,5},{2,0},{3,7},{4,6},{5,1},{6,4},{7,3},{8,10},{9,13},{10,... | collective-permute-start | bytes 23048 | tf_op jit(solution)/shard_map/ppermute | solution.py:196
  20.4 3.7 %collective-permute-start.9 = (f32[4,480]{1,0:T(4,128)S(1)}, f32[4,480]{1,0:T(4,128)S(1)}, u32[]{:S(2)}, u32[]{:S(2)}) collective-permute-start(f32[4,480]{1,0:T(4,128)S(1)} %get-tuple-element.16), channel_id=1, source_target_pairs={{0,2},{1,7},{2,0},{3,5},{4,6},{5,3},{6,4},{7,1},{8,10},{9,15},{10,... | collective-permute-start | bytes 23048 | tf_op jit(solution)/shard_map/ppermute | solution.py:196
  24.1 1.4 %collective-permute-start.10 = (f32[4,480]{1,0:T(4,128)S(1)}, f32[4,480]{1,0:T(4,128)S(1)}, u32[]{:S(2)}, u32[]{:S(2)}) collective-permute-start(f32[4,480]{1,0:T(4,128)S(1)} %pad_maximum_fusion), channel_id=1, source_target_pairs={{0,1},{1,0},{2,3},{3,2},{4,5},{5,4},{6,7},{7,6},{8,9},{9,8},{10,11... | collective-permute-start | bytes 23048 | tf_op jit(solution)/shard_map/ppermute | solution.py:196

commit v6 on v5

--- a/solution.py
+++ b/solution.py
@@ -230,8 +230,8 @@
     below = routed(whole, lambda s, c: (s ^ 2, 1) if c == 0 else (s, 0))
     corner = routed(whole, lambda s, c: (s ^ 3, 1) if c == 0 else (s, 0))
 
-    members = [(whole, below), (even_away[0], corner)]
-    rows = [(below, whole), (handed, odd)]
+    members = [(whole, corner), (even_away[0], below)]
+    rows = [(corner, whole), (handed, odd)]
     states = [match([member], rows, lambda s, c: (2 * s, 2 * s + 1))[0] for member in members]
     for hop in range(1, slots // 4):
         away = swapped(pick(odd_away[hop - 1], even_away[hop - 1]))
@@ -243,9 +243,9 @@
 
         states = match(members, rows, ids, states)
     state, other = states
-    other = routed(other, lambda s, c: (s ^ (1 if c == 0 else 3), c))
-    below_state = routed(state, lambda s, c: (s ^ (1 if c == 0 else 2), c))
-    own = combined(pick(state, below_state), other, scale)
+    corner_state = routed(state, lambda s, c: (s ^ (1 if c == 0 else 3), c))
+    near_state = routed(other, lambda s, c: (s ^ (1 if c == 0 else 2), c))
+    own = combined(pick(state, corner_state), near_state, scale)
     total = combined(own, swapped(own), scale)
     columns = jnp.arange(row_width, dtype=jnp.int32).astype(jnp.float32) * CELL
     flow_x = total[2] / total[1] - columns

time: 26.4 us -> 26.2 us (level)
  no operation moved by 1% of the time
where the time goes in v6:
time: 26.2 us; the launch traced here: 26 us
  waiting for transfers between devices  12 us (46%)
  starting transfers between devices  7.52 us (29%)
  Pallas kernels  4.91 us (19%)
  local copies, waits for them, and re-layouts  1.25 us (5%)
    ppermute x11, waiting for transfers between devices, routed(): return lax.ppermute(value, ('query', 'target'), pairs)  12 us
    ppermute x11, starting transfers between devices, routed(): return lax.ppermute(value, ('query', 'target'), pairs)  7.52 us
    pallas_call x3, Pallas kernels, match(): pl.pallas_call(functools.partial(match_kernel, count, bool(states), row_i...  2.78 us
    pallas_call x1, Pallas kernels, rim_partials(): pl.pallas_call(rim_kernel, out_shape=(jax.ShapeDtypeStruct((cols // 2, ou...  1.59 us
    unnamed x8, local copies, waits for them, and re-layouts  0.66 us
    reshape x1, local copies, waits for them, and re-layouts, on_device(): return jnp.stack([flow_x, flow_y]).reshape(2, 1, row_width)  0.6 us
    pallas_call x1, Pallas kernels, own_partials(): pl.pallas_call(own_kernel, out_shape=(part, part), scratch_shapes=[pltpu....  0.54 us
  transfers between devices with their start and end apart: 11, of which 5 were waited for; matrix products, arithmetic and copies ran while one was open for 0% of the time, Pallas kernels for 8%

profile of v6, /device:TPU:0, one launch (start us, length us, event | category | flops | bytes accessed | tf_op | source)
XLA Modules:
  0.0 26.0 jit_solution(5471906982963808273)
XLA Ops:
  0.0 0.0 copy-start
  0.0 0.0 copy-start.1
  0.0 0.0 copy-start.2
  0.0 1.6 %rim_partials.1 = (bf16[480,128]{1,0:T(8,128)(2,1)S(1)}, bf16[480,128]{1,0:T(8,128)(2,1)S(1)}) custom-call(bf16[2,960,128]{2,1,0:T(8,128)(2,1)} %query_hbm.1, bf16[2,960,128]{2,1,0:T(8,128)(2,1)} %target_hbm.1, bf16[3,3,128,128]{3,2,1,0:T(8,128)(2,1)} %weight_hbm.1), custom_call_target="tpu_custom_call" | custom-call | tf_op jit(solution)/shard_map/rim_partials/pallas_call | solution.py:62
  1.6 0.5 %collective-permute-start = (bf16[480,128]{1,0:T(8,128)(2,1)S(1)}, bf16[480,128]{1,0:T(8,128)(2,1)S(1)}, u32[]{:S(2)}, u32[]{:S(2)}) collective-permute-start(bf16[480,128]{1,0:T(8,128)(2,1)S(1)} %get-tuple-element.13), channel_id=1, source_target_pairs={{0,1},{1,0},{2,3},{3,2},{4,5},{5,4},{6,7},{7,6},{8,9},{9,8},{10,11... | collective-permute-start | bytes 368648 | tf_op jit(solution)/shard_map/ppermute | solution.py:196
  2.1 2.6 %collective-permute-start.2 = (bf16[480,128]{1,0:T(8,128)(2,1)S(1)}, bf16[480,128]{1,0:T(8,128)(2,1)S(1)}, u32[]{:S(2)}, u32[]{:S(2)}) collective-permute-start(bf16[480,128]{1,0:T(8,128)(2,1)S(1)} %get-tuple-element.14), channel_id=1, source_target_pairs={{0,2},{1,3},{2,4},{3,5},{4,6},{5,7},{6,8},{7,9},{8,10},{9,11},{10,... | collective-permute-start | bytes 368648 | tf_op jit(solution)/shard_map/ppermute | solution.py:196
  4.7 0.0 copy-start.3
  4.7 0.0 copy-done
  4.7 0.0 copy-done.1
  4.7 0.0 copy-done.2
  4.7 0.6 %copy-done.3 = f32[128]{0:T(128)S(1)} copy-done((f32[128]{0:T(128)S(1)}, f32[128]{0:T(128)}, u32[]{:S(2)}) %copy-start.3) | copy-done | bytes 536
  5.4 0.5 %own_partials.1 = (f32[480,128]{1,0:T(8,128)S(1)}, f32[480,128]{1,0:T(8,128)S(1)}) custom-call(bf16[2,960,128]{2,1,0:T(8,128)(2,1)S(1)} %copy-done, bf16[2,960,128]{2,1,0:T(8,128)(2,1)S(1)} %copy-done.1, bf16[3,3,128,128]{3,2,1,0:T(8,128)(2,1)S(1)} %copy-done.2, f32[1,128]{1,0:T(1,128)S(1)} %bitcast.7), custom_call_target="tpu_custom_call" | custom-call | flops 188743680 | bytes 4194304 | tf_op jit(solution)/shard_map/own_partials/pallas_call | solution.py:96
  5.9 0.0 collective-permute-done
  6.0 0.2 collective-permute-start.1
  6.2 0.3 %collective-permute-start.6 = (bf16[480,128]{1,0:T(8,128)(2,1)S(1)}, bf16[480,128]{1,0:T(8,128)(2,1)S(1)}, u32[]{:S(2)}, u32[]{:S(2)}) collective-permute-start(bf16[480,128]{1,0:T(8,128)(2,1)S(1)} %add_convert_fusion.1.refs_5_), channel_id=1, source_target_pairs={{0,1},{1,8},{2,3},{3,10},{4,5},{5,12},{6,7},{7,14},{8,9},{9,0},{10... | collective-permute-start | bytes 368648 | tf_op jit(solution)/shard_map/ppermute | solution.py:196
  6.5 5.2 %collective-permute-done.2 = bf16[480,128]{1,0:T(8,128)(2,1)S(1)} collective-permute-done((bf16[480,128]{1,0:T(8,128)(2,1)S(1)}, bf16[480,128]{1,0:T(8,128)(2,1)S(1)}, u32[]{:S(2)}, u32[]{:S(2)}) %collective-permute-start.2) | collective-permute-done | bytes 122912 | tf_op jit(solution)/shard_map/ppermute | solution.py:196
  11.7 0.0 collective-permute-done.1.refs_4_
  11.7 0.1 add_convert_fusion.refs_0_.refs_3_
  11.8 0.1 collective-permute-start.4
  11.9 1.2 %collective-permute-start.3 = (bf16[480,128]{1,0:T(8,128)(2,1)S(1)}, bf16[480,128]{1,0:T(8,128)(2,1)S(1)}, u32[]{:S(2)}, u32[]{:S(2)}) collective-permute-start(bf16[480,128]{1,0:T(8,128)(2,1)S(1)} %add_convert_fusion.refs_0_.refs_3_), channel_id=1, source_target_pairs={{0,7},{1,0},{2,5},{3,2},{4,3},{5,4},{6,1},{7,6},{8,15},{9,8},{10,1... | collective-permute-start | bytes 368648 | tf_op jit(solution)/shard_map/ppermute | solution.py:196
  13.1 0.0 collective-permute-start.5
  13.1 0.0 collective-permute-done.6.refs_4_
  13.1 3.7 %collective-permute-done.4.refs_0_.refs_2_.refs_5_ = bf16[480,128]{1,0:T(8,128)(2,1)S(1)} collective-permute-done((bf16[480,128]{1,0:T(8,128)(2,1)S(1)}, bf16[480,128]{1,0:T(8,128)(2,1)S(1)}, u32[]{:S(2)}, u32[]{:S(2)}) %collective-permute-start.4) | collective-permute-done | bytes 122912 | tf_op jit(solution)/shard_map/ppermute | solution.py:196
  16.8 0.1 collective-permute-start.7
  16.9 0.0 collective-permute-done.3.refs_1_.refs_2_
  16.9 0.8 %match.3.refs_8_ = f32[4,480]{1,0:T(4,128)S(1)} custom-call(bf16[480,128]{1,0:T(8,128)(2,1)S(1)} %add_convert_fusion.refs_0_.refs_3_, bf16[480,128]{1,0:T(8,128)(2,1)S(1)} %collective-permute-done.3.refs_1_.refs_2_, bf16[480,128]{1,0:T(8,128)(2,1)S(1)} %collective-permute-done.3.refs_1_.refs_2_, bf16[480,128]{1,0:T(8,128)(2,1)S(1)} %add_convert_fusion.refs_0_.refs_3_, ...), custom_call_target="tpu_custom_call" | custom-call | flops 117964800 | bytes 4194304 | tf_op jit(solution)/shard_map/match/pallas_call | solution.py:164
  17.7 0.0 collective-permute-done.5.refs_1_.refs_3_
  17.7 0.8 %match.4.refs_9_ = f32[4,480]{1,0:T(4,128)S(1)} custom-call(bf16[480,128]{1,0:T(8,128)(2,1)S(1)} %collective-permute-done.4.refs_0_.refs_2_.refs_5_, bf16[480,128]{1,0:T(8,128)(2,1)S(1)} %collective-permute-done.5.refs_1_.refs_3_, bf16[480,128]{1,0:T(8,128)(2,1)S(1)} %collective-permute-done.3.refs_1_.refs_2_, ...), custom_call_target="tpu_custom_call" | custom-call | flops 117964800 | bytes 4194304 | tf_op jit(solution)/shard_map/match/pallas_call | solution.py:164
  18.5 0.0 collective-permute-done.7.refs_6_.refs_7_
  18.5 1.3 %match.5 = (f32[4,480]{1,0:T(4,128)S(1)}, f32[4,480]{1,0:T(4,128)S(1)}) custom-call(bf16[480,128]{1,0:T(8,128)(2,1)S(1)} %add_convert_fusion.refs_0_.refs_3_, bf16[480,128]{1,0:T(8,128)(2,1)S(1)} %collective-permute-done.3.refs_1_.refs_2_, bf16[480,128]{1,0:T(8,128)(2,1)S(1)} %collective-permute-done.4.refs_0_.refs_2_.refs_5_, ...), custom_call_target="tpu_custom_call" | custom-call | flops 235929600 | bytes 4194304 | tf_op jit(solution)/shard_map/match/pallas_call | solution.py:164
  19.8 0.6 %collective-permute-start.8 = (f32[4,480]{1,0:T(4,128)S(1)}, f32[4,480]{1,0:T(4,128)S(1)}, u32[]{:S(2)}, u32[]{:S(2)}) collective-permute-start(f32[4,480]{1,0:T(4,128)S(1)} %get-tuple-element.15), channel_id=1, source_target_pairs={{0,2},{1,7},{2,0},{3,5},{4,6},{5,3},{6,4},{7,1},{8,10},{9,15},{10,... | collective-permute-start | bytes 23048 | tf_op jit(solution)/shard_map/ppermute | solution.py:196
  20.4 1.5 %collective-permute-start.9 = (f32[4,480]{1,0:T(4,128)S(1)}, f32[4,480]{1,0:T(4,128)S(1)}, u32[]{:S(2)}, u32[]{:S(2)}) collective-permute-start(f32[4,480]{1,0:T(4,128)S(1)} %get-tuple-element.16), channel_id=1, source_target_pairs={{0,2},{1,5},{2,0},{3,7},{4,6},{5,1},{6,4},{7,3},{8,10},{9,13},{10,... | collective-permute-start | bytes 23048 | tf_op jit(solution)/shard_map/ppermute | solution.py:196
  21.8 1.6 %collective-permute-done.8 = f32[4,480]{1,0:T(4,128)S(1)} collective-permute-done((f32[4,480]{1,0:T(4,128)S(1)}, f32[4,480]{1,0:T(4,128)S(1)}, u32[]{:S(2)}, u32[]{:S(2)}) %collective-permute-start.8) | collective-permute-done | bytes 7712 | tf_op jit(solution)/shard_map/ppermute | solution.py:196
  23.5 0.6 %collective-permute-done.9 = f32[4,480]{1,0:T(4,128)S(1)} collective-permute-done((f32[4,480]{1,0:T(4,128)S(1)}, f32[4,480]{1,0:T(4,128)S(1)}, u32[]{:S(2)}, u32[]{:S(2)}) %collective-permute-start.9) | collective-permute-done | bytes 7712 | tf_op jit(solution)/shard_map/ppermute | solution.py:196
  24.1 0.4 %collective-permute-start.10 = (f32[4,480]{1,0:T(4,128)S(1)}, f32[4,480]{1,0:T(4,128)S(1)}, u32[]{:S(2)}, u32[]{:S(2)}) collective-permute-start(f32[4,480]{1,0:T(4,128)S(1)} %pad_maximum_fusion), channel_id=1, source_target_pairs={{0,1},{1,0},{2,3},{3,2},{4,5},{5,4},{6,7},{7,6},{8,9},{9,8},{10,11... | collective-permute-start | bytes 23048 | tf_op jit(solution)/shard_map/ppermute | solution.py:196
  24.5 0.8 %collective-permute-done.10 = f32[4,480]{1,0:T(4,128)S(1)} collective-permute-done((f32[4,480]{1,0:T(4,128)S(1)}, f32[4,480]{1,0:T(4,128)S(1)}, u32[]{:S(2)}, u32[]{:S(2)}) %collective-permute-start.10) | collective-permute-done | bytes 7712 | tf_op jit(solution)/shard_map/ppermute | solution.py:196
  25.4 0.6 %copy.5 = f32[2,1,480]{2,1,0:T(1,128)} copy(f32[2,1,480]{2,0,1:T(2,128)S(1)} %maximum_bitcast_fusion) | data formatting | bytes 7680 | tf_op jit(solution)/shard_map/reshape | solution.py:253
  (11 shorter events, 0.2 us)
Async XLA Ops:
  0.0 4.7 %copy-start = (bf16[2,960,128]{2,1,0:T(8,128)(2,1)S(1)}, bf16[2,960,128]{2,1,0:T(8,128)(2,1)}, u32[]{:S(2)}) copy-start(bf16[2,960,128]{2,1,0:T(8,128)(2,1)} %query_hbm.1) | copy-start | bytes 1474564
  0.0 4.7 %copy-start.1 = (bf16[2,960,128]{2,1,0:T(8,128)(2,1)S(1)}, bf16[2,960,128]{2,1,0:T(8,128)(2,1)}, u32[]{:S(2)}) copy-start(bf16[2,960,128]{2,1,0:T(8,128)(2,1)} %target_hbm.1) | copy-start | bytes 1474564
  0.0 4.7 %copy-start.2 = (bf16[3,3,128,128]{3,2,1,0:T(8,128)(2,1)S(1)}, bf16[3,3,128,128]{3,2,1,0:T(8,128)(2,1)}, u32[]{:S(2)}) copy-start(bf16[3,3,128,128]{3,2,1,0:T(8,128)(2,1)} %weight_hbm.1) | copy-start | bytes 884740
  1.6 4.3 %collective-permute-start = (bf16[480,128]{1,0:T(8,128)(2,1)S(1)}, bf16[480,128]{1,0:T(8,128)(2,1)S(1)}, u32[]{:S(2)}, u32[]{:S(2)}) collective-permute-start(bf16[480,128]{1,0:T(8,128)(2,1)S(1)} %get-tuple-element.13), channel_id=1, source_target_pairs={{0,1},{1,0},{2,3},{3,2},{4,5},{5,4},{6,7},{7,6},{8,9},{9,8},{10,11... | collective-permute-start | bytes 368648 | tf_op jit(solution)/shard_map/ppermute | solution.py:196
  2.1 9.6 %collective-permute-start.2 = (bf16[480,128]{1,0:T(8,128)(2,1)S(1)}, bf16[480,128]{1,0:T(8,128)(2,1)S(1)}, u32[]{:S(2)}, u32[]{:S(2)}) collective-permute-start(bf16[480,128]{1,0:T(8,128)(2,1)S(1)} %get-tuple-element.14), channel_id=1, source_target_pairs={{0,2},{1,3},{2,4},{3,5},{4,6},{5,7},{6,8},{7,9},{8,10},{9,11},{10,... | collective-permute-start | bytes 368648 | tf_op jit(solution)/shard_map/ppermute | solution.py:196
  4.7 0.7 %copy-start.3 = (f32[128]{0:T(128)S(1)}, f32[128]{0:T(128)}, u32[]{:S(2)}) copy-start(f32[128]{0:T(128)} %param.7) | copy-start | bytes 1540
  6.0 5.8 %collective-permute-start.1 = (bf16[480,128]{1,0:T(8,128)(2,1)S(1)}, bf16[480,128]{1,0:T(8,128)(2,1)S(1)}, u32[]{:S(2)}, u32[]{:S(2)}) collective-permute-start(bf16[480,128]{1,0:T(8,128)(2,1)S(1)} %add_convert_fusion.1.refs_5_), channel_id=1, source_target_pairs={{0,1},{1,0},{2,3},{3,2},{4,5},{5,4},{6,7},{7,6},{8,9},{9,8},{10,11... | collective-permute-start | bytes 368648 | tf_op jit(solution)/shard_map/ppermute | solution.py:196
  6.2 6.9 %collective-permute-start.6 = (bf16[480,128]{1,0:T(8,128)(2,1)S(1)}, bf16[480,128]{1,0:T(8,128)(2,1)S(1)}, u32[]{:S(2)}, u32[]{:S(2)}) collective-permute-start(bf16[480,128]{1,0:T(8,128)(2,1)S(1)} %add_convert_fusion.1.refs_5_), channel_id=1, source_target_pairs={{0,1},{1,8},{2,3},{3,10},{4,5},{5,12},{6,7},{7,14},{8,9},{9,0},{10... | collective-permute-start | bytes 368648 | tf_op jit(solution)/shard_map/ppermute | solution.py:196
  11.8 5.0 %collective-permute-start.4 = (bf16[480,128]{1,0:T(8,128)(2,1)S(1)}, bf16[480,128]{1,0:T(8,128)(2,1)S(1)}, u32[]{:S(2)}, u32[]{:S(2)}) collective-permute-start(bf16[480,128]{1,0:T(8,128)(2,1)S(1)} %add_convert_fusion.refs_0_.refs_3_), channel_id=1, source_target_pairs={{0,2},{1,9},{2,0},{3,11},{4,6},{5,13},{6,4},{7,15},{8,10},{9,1},{1... | collective-permute-start | bytes 368648 | tf_op jit(solution)/shard_map/ppermute | solution.py:196
  11.9 5.1 %collective-permute-start.3 = (bf16[480,128]{1,0:T(8,128)(2,1)S(1)}, bf16[480,128]{1,0:T(8,128)(2,1)S(1)}, u32[]{:S(2)}, u32[]{:S(2)}) collective-permute-start(bf16[480,128]{1,0:T(8,128)(2,1)S(1)} %add_convert_fusion.refs_0_.refs_3_), channel_id=1, source_target_pairs={{0,7},{1,0},{2,5},{3,2},{4,3},{5,4},{6,1},{7,6},{8,15},{9,8},{10,1... | collective-permute-start | bytes 368648 | tf_op jit(solution)/shard_map/ppermute | solution.py:196
  13.1 4.6 %collective-permute-start.5 = (bf16[480,128]{1,0:T(8,128)(2,1)S(1)}, bf16[480,128]{1,0:T(8,128)(2,1)S(1)}, u32[]{:S(2)}, u32[]{:S(2)}) collective-permute-start(bf16[480,128]{1,0:T(8,128)(2,1)S(1)} %add_convert_fusion.refs_0_.refs_3_), channel_id=1, source_target_pairs={{0,5},{1,0},{2,7},{3,2},{4,1},{5,4},{6,3},{7,6},{8,13},{9,8},{10,1... | collective-permute-start | bytes 368648 | tf_op jit(solution)/shard_map/ppermute | solution.py:196
  16.8 1.6 %collective-permute-start.7 = (bf16[480,128]{1,0:T(8,128)(2,1)S(1)}, bf16[480,128]{1,0:T(8,128)(2,1)S(1)}, u32[]{:S(2)}, u32[]{:S(2)}) collective-permute-start(bf16[480,128]{1,0:T(8,128)(2,1)S(1)} %broadcast_select_fusion), channel_id=1, source_target_pairs={{0,1},{1,0},{2,3},{3,2},{4,5},{5,4},{6,7},{7,6},{8,9},{9,8},{10,11... | collective-permute-start | bytes 368648 | tf_op jit(solution)/shard_map/ppermute | solution.py:196
  19.8 3.7 %collective-permute-start.8 = (f32[4,480]{1,0:T(4,128)S(1)}, f32[4,480]{1,0:T(4,128)S(1)}, u32[]{:S(2)}, u32[]{:S(2)}) collective-permute-start(f32[4,480]{1,0:T(4,128)S(1)} %get-tuple-element.15), channel_id=1, source_target_pairs={{0,2},{1,7},{2,0},{3,5},{4,6},{5,3},{6,4},{7,1},{8,10},{9,15},{10,... | collective-permute-start | bytes 23048 | tf_op jit(solution)/shard_map/ppermute | solution.py:196
  20.4 3.7 %collective-permute-start.9 = (f32[4,480]{1,0:T(4,128)S(1)}, f32[4,480]{1,0:T(4,128)S(1)}, u32[]{:S(2)}, u32[]{:S(2)}) collective-permute-start(f32[4,480]{1,0:T(4,128)S(1)} %get-tuple-element.16), channel_id=1, source_target_pairs={{0,2},{1,5},{2,0},{3,7},{4,6},{5,1},{6,4},{7,3},{8,10},{9,13},{10,... | collective-permute-start | bytes 23048 | tf_op jit(solution)/shard_map/ppermute | solution.py:196
  24.1 1.2 %collective-permute-start.10 = (f32[4,480]{1,0:T(4,128)S(1)}, f32[4,480]{1,0:T(4,128)S(1)}, u32[]{:S(2)}, u32[]{:S(2)}) collective-permute-start(f32[4,480]{1,0:T(4,128)S(1)} %pad_maximum_fusion), channel_id=1, source_target_pairs={{0,1},{1,0},{2,3},{3,2},{4,5},{5,4},{6,7},{7,6},{8,9},{9,8},{10,11... | collective-permute-start | bytes 23048 | tf_op jit(solution)/shard_map/ppermute | solution.py:196

commit v7 on v6

--- a/solution.py
+++ b/solution.py
@@ -11,7 +11,7 @@
 CELL = 0.0625
 LOG2E = math.log2(math.e)
 VMEM_LIMIT = 32 * 1024 * 1024
-RIM_VMEM = (64 * 1024 - 10752) * 1024
+RIM_VMEM = (64 * 1024 - 10944) * 1024
 
 
 def column_taps(row, stage):
@@ -61,7 +61,7 @@
     hbm = pl.BlockSpec(memory_space=pltpu.HBM)
     return pl.pallas_call(
         rim_kernel,
-        out_shape=(jax.ShapeDtypeStruct((cols // 2, out_channels), jnp.bfloat16),) * 2,
+        out_shape=(jax.ShapeDtypeStruct((cols // 2, out_channels), jnp.float32),) * 2,
         in_specs=[hbm] * 3,
         out_specs=(pl.BlockSpec(memory_space=pltpu.VMEM),) * 2,
         scratch_shapes=[
@@ -213,16 +213,17 @@
 
     far_rim, near_rim = rim_partials(query_input, target_input, conv_weight)
     near_rim = swapped(near_rim)
-    far_rim = routed(far_rim, lambda s, c: ((s + 1) % slots, c)).astype(jnp.float32)
+    far_rim = routed(far_rim, lambda s, c: ((s + 1) % slots, c))
     far_rim = jnp.where(slot == 0, 0.0, far_rim)
     query_part, target_part = own_partials(query_input, target_input, conv_weight, conv_bias)
-    odd = (target_part + pick(0.0, near_rim.astype(jnp.float32))).astype(jnp.bfloat16)
-    handed = swapped(odd)
+    odd = (target_part + near_rim).astype(jnp.bfloat16)
+    handed = swapped(pick(target_part, odd.astype(jnp.float32)))
     odd_away = [
         routed(odd, lambda s, c: (s, 1) if c == 0 else ((s + 4 * hop) % slots, 0))
         for hop in range(1, max(2, slots // 4))
     ]
-    whole = (pick(query_part, handed.astype(jnp.float32)) + far_rim).astype(jnp.bfloat16)
+    whole = (pick(query_part, handed) + far_rim).astype(jnp.bfloat16)
+    handed = handed.astype(jnp.bfloat16)
     even_away = [
         routed(whole, lambda s, c: (s ^ 1, 0) if c == 0 else ((s + 4 * hop) % slots, 1))
         for hop in range(1, max(2, slots // 4))

time: 26.2 us -> 29.2 us (1.11); the launches traced: 26 us -> 28.7 us
  waiting for transfers between devices: 12 us -> 14.9 us
    ppermute x11, waiting for transfers between devices: 12 us -> 14.9 us  [routed(): return lax.ppermute(value, ('query', 'target'), pairs)]
  transfers between devices with their start and end apart: 11 -> 11, of which waited for: 5 -> 5; matrix products, arithmetic and copies ran while one was open for 0% -> 0% of each run, Pallas kernels for 8% -> 7%
where the time goes in v7:
time: 29.2 us; the launch traced here: 28.7 us
  waiting for transfers between devices  14.9 us (51%)
  starting transfers between devices  7.31 us (25%)
  Pallas kernels  4.92 us (17%)
  local copies, waits for them, and re-layouts  1.25 us (4%)
    ppermute x11, waiting for transfers between devices, routed(): return lax.ppermute(value, ('query', 'target'), pairs)  14.9 us
    ppermute x11, starting transfers between devices, routed(): return lax.ppermute(value, ('query', 'target'), pairs)  7.31 us
    pallas_call x3, Pallas kernels, match(): pl.pallas_call(functools.partial(match_kernel, count, bool(states), row_i...  2.79 us
    pallas_call x1, Pallas kernels, rim_partials(): pl.pallas_call(rim_kernel, out_shape=(jax.ShapeDtypeStruct((cols // 2, ou...  1.59 us
    unnamed x8, local copies, waits for them, and re-layouts  0.66 us
    reshape x1, local copies, waits for them, and re-layouts, on_device(): return jnp.stack([flow_x, flow_y]).reshape(2, 1, row_width)  0.6 us
  transfers between devices with their start and end apart: 11, of which 5 were waited for; matrix products, arithmetic and copies ran while one was open for 0% of the time, Pallas kernels for 7%

profile of v7, /device:TPU:0, one launch (start us, length us, event | category | flops | bytes accessed | tf_op | source)
XLA Modules:
  0.0 28.7 jit_solution(2598110936679864342)
XLA Ops:
  0.0 0.0 copy-start
  0.0 0.0 copy-start.1
  0.0 0.0 copy-start.2
  0.0 1.6 %rim_partials.1 = (f32[480,128]{1,0:T(8,128)S(1)}, f32[480,128]{1,0:T(8,128)S(1)}) custom-call(bf16[2,960,128]{2,1,0:T(8,128)(2,1)} %query_hbm.1, bf16[2,960,128]{2,1,0:T(8,128)(2,1)} %target_hbm.1, bf16[3,3,128,128]{3,2,1,0:T(8,128)(2,1)} %weight_hbm.1), custom_call_target="tpu_custom_call" | custom-call | tf_op jit(solution)/shard_map/rim_partials/pallas_call | solution.py:62
  1.6 0.5 %collective-permute-start = (f32[480,128]{1,0:T(8,128)S(1)}, f32[480,128]{1,0:T(8,128)S(1)}, u32[]{:S(2)}, u32[]{:S(2)}) collective-permute-start(f32[480,128]{1,0:T(8,128)S(1)} %get-tuple-element.13), channel_id=1, source_target_pairs={{0,1},{1,0},{2,3},{3,2},{4,5},{5,4},{6,7},{7,6},{8,9},{9,8},{10,11... | collective-permute-start | bytes 737288 | tf_op jit(solution)/shard_map/ppermute | solution.py:196
  2.1 2.6 %collective-permute-start.2 = (f32[480,128]{1,0:T(8,128)S(1)}, f32[480,128]{1,0:T(8,128)S(1)}, u32[]{:S(2)}, u32[]{:S(2)}) collective-permute-start(f32[480,128]{1,0:T(8,128)S(1)} %get-tuple-element.14), channel_id=1, source_target_pairs={{0,2},{1,3},{2,4},{3,5},{4,6},{5,7},{6,8},{7,9},{8,10},{9,11},{10,... | collective-permute-start | bytes 737288 | tf_op jit(solution)/shard_map/ppermute | solution.py:196
  4.7 0.0 copy-start.3
  4.7 0.0 copy-done
  4.7 0.0 copy-done.1
  4.7 0.0 copy-done.2
  4.7 0.6 %copy-done.3 = f32[128]{0:T(128)S(1)} copy-done((f32[128]{0:T(128)S(1)}, f32[128]{0:T(128)}, u32[]{:S(2)}) %copy-start.3) | copy-done | bytes 536
  5.4 0.5 %own_partials.1 = (f32[480,128]{1,0:T(8,128)S(1)}, f32[480,128]{1,0:T(8,128)S(1)}) custom-call(bf16[2,960,128]{2,1,0:T(8,128)(2,1)S(1)} %copy-done, bf16[2,960,128]{2,1,0:T(8,128)(2,1)S(1)} %copy-done.1, bf16[3,3,128,128]{3,2,1,0:T(8,128)(2,1)S(1)} %copy-done.2, f32[1,128]{1,0:T(1,128)S(1)} %bitcast.7), custom_call_target="tpu_custom_call" | custom-call | flops 188743680 | bytes 4194304 | tf_op jit(solution)/shard_map/own_partials/pallas_call | solution.py:96
  5.9 0.0 collective-permute-done
  6.0 0.2 collective-permute-start.1
  6.2 0.3 %collective-permute-start.6 = (bf16[480,128]{1,0:T(8,128)(2,1)S(1)}, bf16[480,128]{1,0:T(8,128)(2,1)S(1)}, u32[]{:S(2)}, u32[]{:S(2)}) collective-permute-start(bf16[480,128]{1,0:T(8,128)(2,1)S(1)} %get-tuple-element.20.refs_5_), channel_id=1, source_target_pairs={{0,1},{1,8},{2,3},{3,10},{4,5},{5,12},{6,7},{7,14},{8,9},{9,0},{10... | collective-permute-start | bytes 368648 | tf_op jit(solution)/shard_map/ppermute | solution.py:196
  6.5 8.1 %collective-permute-done.2 = f32[480,128]{1,0:T(8,128)S(1)} collective-permute-done((f32[480,128]{1,0:T(8,128)S(1)}, f32[480,128]{1,0:T(8,128)S(1)}, u32[]{:S(2)}, u32[]{:S(2)}) %collective-permute-start.2) | collective-permute-done | bytes 245792 | tf_op jit(solution)/shard_map/ppermute | solution.py:196
  14.6 0.0 collective-permute-done.1
  14.7 0.1 collective-permute-start.4
  14.8 0.9 %collective-permute-start.3 = (bf16[480,128]{1,0:T(8,128)(2,1)S(1)}, bf16[480,128]{1,0:T(8,128)(2,1)S(1)}, u32[]{:S(2)}, u32[]{:S(2)}) collective-permute-start(bf16[480,128]{1,0:T(8,128)(2,1)S(1)} %get-tuple-element.22.refs_0_.refs_3_), channel_id=1, source_target_pairs={{0,7},{1,0},{2,5},{3,2},{4,3},{5,4},{6,1},{7,6},{8,15},{9,8},{10,1... | collective-permute-start | bytes 368648 | tf_op jit(solution)/shard_map/ppermute | solution.py:196
  15.7 0.0 collective-permute-start.5
  15.7 0.0 collective-permute-done.6.refs_4_
  15.7 4.0 %collective-permute-done.4.refs_0_.refs_2_.refs_5_ = bf16[480,128]{1,0:T(8,128)(2,1)S(1)} collective-permute-done((bf16[480,128]{1,0:T(8,128)(2,1)S(1)}, bf16[480,128]{1,0:T(8,128)(2,1)S(1)}, u32[]{:S(2)}, u32[]{:S(2)}) %collective-permute-start.4) | collective-permute-done | bytes 122912 | tf_op jit(solution)/shard_map/ppermute | solution.py:196
  19.8 0.1 collective-permute-start.7
  19.9 0.0 collective-permute-done.3.refs_1_.refs_2_
  19.9 0.8 %match.3.refs_8_ = f32[4,480]{1,0:T(4,128)S(1)} custom-call(bf16[480,128]{1,0:T(8,128)(2,1)S(1)} %get-tuple-element.22.refs_0_.refs_3_, bf16[480,128]{1,0:T(8,128)(2,1)S(1)} %collective-permute-done.3.refs_1_.refs_2_, bf16[480,128]{1,0:T(8,128)(2,1)S(1)} %collective-permute-done.3.refs_1_.refs_2_, bf16[480,128]{1,0:T(8,128)(2,1)S(1)} %get-tuple-element.22.refs_0_.refs_3_, ...), custom_call_target="tpu_custom_call" | custom-call | flops 117964800 | bytes 4194304 | tf_op jit(solution)/shard_map/match/pallas_call | solution.py:164
  20.6 0.0 collective-permute-done.5.refs_1_.refs_3_
  20.6 0.8 %match.4.refs_9_ = f32[4,480]{1,0:T(4,128)S(1)} custom-call(bf16[480,128]{1,0:T(8,128)(2,1)S(1)} %collective-permute-done.4.refs_0_.refs_2_.refs_5_, bf16[480,128]{1,0:T(8,128)(2,1)S(1)} %collective-permute-done.5.refs_1_.refs_3_, bf16[480,128]{1,0:T(8,128)(2,1)S(1)} %collective-permute-done.3.refs_1_.refs_2_, ...), custom_call_target="tpu_custom_call" | custom-call | flops 117964800 | bytes 4194304 | tf_op jit(solution)/shard_map/match/pallas_call | solution.py:164
  21.4 0.0 collective-permute-done.7.refs_6_.refs_7_
  21.4 1.3 %match.5 = (f32[4,480]{1,0:T(4,128)S(1)}, f32[4,480]{1,0:T(4,128)S(1)}) custom-call(bf16[480,128]{1,0:T(8,128)(2,1)S(1)} %get-tuple-element.22.refs_0_.refs_3_, bf16[480,128]{1,0:T(8,128)(2,1)S(1)} %collective-permute-done.3.refs_1_.refs_2_, bf16[480,128]{1,0:T(8,128)(2,1)S(1)} %collective-permute-done.4.refs_0_.refs_2_.refs_5_, ...), custom_call_target="tpu_custom_call" | custom-call | flops 235929600 | bytes 4194304 | tf_op jit(solution)/shard_map/match/pallas_call | solution.py:164
  22.7 0.4 %collective-permute-start.8 = (f32[4,480]{1,0:T(4,128)S(1)}, f32[4,480]{1,0:T(4,128)S(1)}, u32[]{:S(2)}, u32[]{:S(2)}) collective-permute-start(f32[4,480]{1,0:T(4,128)S(1)} %get-tuple-element.15), channel_id=1, source_target_pairs={{0,2},{1,7},{2,0},{3,5},{4,6},{5,3},{6,4},{7,1},{8,10},{9,15},{10,... | collective-permute-start | bytes 23048 | tf_op jit(solution)/shard_map/ppermute | solution.py:196
  23.0 1.7 %collective-permute-start.9 = (f32[4,480]{1,0:T(4,128)S(1)}, f32[4,480]{1,0:T(4,128)S(1)}, u32[]{:S(2)}, u32[]{:S(2)}) collective-permute-start(f32[4,480]{1,0:T(4,128)S(1)} %get-tuple-element.16), channel_id=1, source_target_pairs={{0,2},{1,5},{2,0},{3,7},{4,6},{5,1},{6,4},{7,3},{8,10},{9,13},{10,... | collective-permute-start | bytes 23048 | tf_op jit(solution)/shard_map/ppermute | solution.py:196
  24.8 1.6 %collective-permute-done.8 = f32[4,480]{1,0:T(4,128)S(1)} collective-permute-done((f32[4,480]{1,0:T(4,128)S(1)}, f32[4,480]{1,0:T(4,128)S(1)}, u32[]{:S(2)}, u32[]{:S(2)}) %collective-permute-start.8) | collective-permute-done | bytes 7712 | tf_op jit(solution)/shard_map/ppermute | solution.py:196
  26.4 0.3 collective-permute-done.9
  26.8 0.5 %collective-permute-start.10 = (f32[4,480]{1,0:T(4,128)S(1)}, f32[4,480]{1,0:T(4,128)S(1)}, u32[]{:S(2)}, u32[]{:S(2)}) collective-permute-start(f32[4,480]{1,0:T(4,128)S(1)} %pad_maximum_fusion), channel_id=1, source_target_pairs={{0,1},{1,0},{2,3},{3,2},{4,5},{5,4},{6,7},{7,6},{8,9},{9,8},{10,11... | collective-permute-start | bytes 23048 | tf_op jit(solution)/shard_map/ppermute | solution.py:196
  27.2 0.8 %collective-permute-done.10 = f32[4,480]{1,0:T(4,128)S(1)} collective-permute-done((f32[4,480]{1,0:T(4,128)S(1)}, f32[4,480]{1,0:T(4,128)S(1)}, u32[]{:S(2)}, u32[]{:S(2)}) %collective-permute-start.10) | collective-permute-done | bytes 7712 | tf_op jit(solution)/shard_map/ppermute | solution.py:196
  28.1 0.6 %copy.5 = f32[2,1,480]{2,1,0:T(1,128)} copy(f32[2,1,480]{2,0,1:T(2,128)S(1)} %maximum_bitcast_fusion) | data formatting | bytes 7680 | tf_op jit(solution)/shard_map/reshape | solution.py:254
  (12 shorter events, 0.2 us)
Async XLA Ops:
  0.0 4.7 %copy-start = (bf16[2,960,128]{2,1,0:T(8,128)(2,1)S(1)}, bf16[2,960,128]{2,1,0:T(8,128)(2,1)}, u32[]{:S(2)}) copy-start(bf16[2,960,128]{2,1,0:T(8,128)(2,1)} %query_hbm.1) | copy-start | bytes 1474564
  0.0 4.7 %copy-start.1 = (bf16[2,960,128]{2,1,0:T(8,128)(2,1)S(1)}, bf16[2,960,128]{2,1,0:T(8,128)(2,1)}, u32[]{:S(2)}) copy-start(bf16[2,960,128]{2,1,0:T(8,128)(2,1)} %target_hbm.1) | copy-start | bytes 1474564
  0.0 4.7 %copy-start.2 = (bf16[3,3,128,128]{3,2,1,0:T(8,128)(2,1)S(1)}, bf16[3,3,128,128]{3,2,1,0:T(8,128)(2,1)}, u32[]{:S(2)}) copy-start(bf16[3,3,128,128]{3,2,1,0:T(8,128)(2,1)} %weight_hbm.1) | copy-start | bytes 884740
  1.6 4.3 %collective-permute-start = (f32[480,128]{1,0:T(8,128)S(1)}, f32[480,128]{1,0:T(8,128)S(1)}, u32[]{:S(2)}, u32[]{:S(2)}) collective-permute-start(f32[480,128]{1,0:T(8,128)S(1)} %get-tuple-element.13), channel_id=1, source_target_pairs={{0,1},{1,0},{2,3},{3,2},{4,5},{5,4},{6,7},{7,6},{8,9},{9,8},{10,11... | collective-permute-start | bytes 737288 | tf_op jit(solution)/shard_map/ppermute | solution.py:196
  2.1 12.5 %collective-permute-start.2 = (f32[480,128]{1,0:T(8,128)S(1)}, f32[480,128]{1,0:T(8,128)S(1)}, u32[]{:S(2)}, u32[]{:S(2)}) collective-permute-start(f32[480,128]{1,0:T(8,128)S(1)} %get-tuple-element.14), channel_id=1, source_target_pairs={{0,2},{1,3},{2,4},{3,5},{4,6},{5,7},{6,8},{7,9},{8,10},{9,11},{10,... | collective-permute-start | bytes 737288 | tf_op jit(solution)/shard_map/ppermute | solution.py:196
  4.7 0.7 %copy-start.3 = (f32[128]{0:T(128)S(1)}, f32[128]{0:T(128)}, u32[]{:S(2)}) copy-start(f32[128]{0:T(128)} %param.7) | copy-start | bytes 1540
  6.0 8.7 %collective-permute-start.1 = (f32[480,128]{1,0:T(8,128)S(1)}, f32[480,128]{1,0:T(8,128)S(1)}, u32[]{:S(2)}, u32[]{:S(2)}) collective-permute-start(f32[480,128]{1,0:T(8,128)S(1)} %get-tuple-element.19), channel_id=1, source_target_pairs={{0,1},{1,0},{2,3},{3,2},{4,5},{5,4},{6,7},{7,6},{8,9},{9,8},{10,11... | collective-permute-start | bytes 737288 | tf_op jit(solution)/shard_map/ppermute | solution.py:196
  6.2 9.5 %collective-permute-start.6 = (bf16[480,128]{1,0:T(8,128)(2,1)S(1)}, bf16[480,128]{1,0:T(8,128)(2,1)S(1)}, u32[]{:S(2)}, u32[]{:S(2)}) collective-permute-start(bf16[480,128]{1,0:T(8,128)(2,1)S(1)} %get-tuple-element.20.refs_5_), channel_id=1, source_target_pairs={{0,1},{1,8},{2,3},{3,10},{4,5},{5,12},{6,7},{7,14},{8,9},{9,0},{10... | collective-permute-start | bytes 368648 | tf_op jit(solution)/shard_map/ppermute | solution.py:196
  14.7 5.1 %collective-permute-start.4 = (bf16[480,128]{1,0:T(8,128)(2,1)S(1)}, bf16[480,128]{1,0:T(8,128)(2,1)S(1)}, u32[]{:S(2)}, u32[]{:S(2)}) collective-permute-start(bf16[480,128]{1,0:T(8,128)(2,1)S(1)} %get-tuple-element.22.refs_0_.refs_3_), channel_id=1, source_target_pairs={{0,2},{1,9},{2,0},{3,11},{4,6},{5,13},{6,4},{7,15},{8,10},{9,1},{1... | collective-permute-start | bytes 368648 | tf_op jit(solution)/shard_map/ppermute | solution.py:196
  14.8 5.1 %collective-permute-start.3 = (bf16[480,128]{1,0:T(8,128)(2,1)S(1)}, bf16[480,128]{1,0:T(8,128)(2,1)S(1)}, u32[]{:S(2)}, u32[]{:S(2)}) collective-permute-start(bf16[480,128]{1,0:T(8,128)(2,1)S(1)} %get-tuple-element.22.refs_0_.refs_3_), channel_id=1, source_target_pairs={{0,7},{1,0},{2,5},{3,2},{4,3},{5,4},{6,1},{7,6},{8,15},{9,8},{10,1... | collective-permute-start | bytes 368648 | tf_op jit(solution)/shard_map/ppermute | solution.py:196
  15.7 4.9 %collective-permute-start.5 = (bf16[480,128]{1,0:T(8,128)(2,1)S(1)}, bf16[480,128]{1,0:T(8,128)(2,1)S(1)}, u32[]{:S(2)}, u32[]{:S(2)}) collective-permute-start(bf16[480,128]{1,0:T(8,128)(2,1)S(1)} %get-tuple-element.22.refs_0_.refs_3_), channel_id=1, source_target_pairs={{0,5},{1,0},{2,7},{3,2},{4,1},{5,4},{6,3},{7,6},{8,13},{9,8},{10,1... | collective-permute-start | bytes 368648 | tf_op jit(solution)/shard_map/ppermute | solution.py:196
  19.8 1.6 %collective-permute-start.7 = (bf16[480,128]{1,0:T(8,128)(2,1)S(1)}, bf16[480,128]{1,0:T(8,128)(2,1)S(1)}, u32[]{:S(2)}, u32[]{:S(2)}) collective-permute-start(bf16[480,128]{1,0:T(8,128)(2,1)S(1)} %broadcast_select_fusion), channel_id=1, source_target_pairs={{0,1},{1,0},{2,3},{3,2},{4,5},{5,4},{6,7},{7,6},{8,9},{9,8},{10,11... | collective-permute-start | bytes 368648 | tf_op jit(solution)/shard_map/ppermute | solution.py:196
  22.7 3.7 %collective-permute-start.8 = (f32[4,480]{1,0:T(4,128)S(1)}, f32[4,480]{1,0:T(4,128)S(1)}, u32[]{:S(2)}, u32[]{:S(2)}) collective-permute-start(f32[4,480]{1,0:T(4,128)S(1)} %get-tuple-element.15), channel_id=1, source_target_pairs={{0,2},{1,7},{2,0},{3,5},{4,6},{5,3},{6,4},{7,1},{8,10},{9,15},{10,... | collective-permute-start | bytes 23048 | tf_op jit(solution)/shard_map/ppermute | solution.py:196
  23.0 3.7 %collective-permute-start.9 = (f32[4,480]{1,0:T(4,128)S(1)}, f32[4,480]{1,0:T(4,128)S(1)}, u32[]{:S(2)}, u32[]{:S(2)}) collective-permute-start(f32[4,480]{1,0:T(4,128)S(1)} %get-tuple-element.16), channel_id=1, source_target_pairs={{0,2},{1,5},{2,0},{3,7},{4,6},{5,1},{6,4},{7,3},{8,10},{9,13},{10,... | collective-permute-start | bytes 23048 | tf_op jit(solution)/shard_map/ppermute | solution.py:196
  26.8 1.3 %collective-permute-start.10 = (f32[4,480]{1,0:T(4,128)S(1)}, f32[4,480]{1,0:T(4,128)S(1)}, u32[]{:S(2)}, u32[]{:S(2)}) collective-permute-start(f32[4,480]{1,0:T(4,128)S(1)} %pad_maximum_fusion), channel_id=1, source_target_pairs={{0,1},{1,0},{2,3},{3,2},{4,5},{5,4},{6,7},{7,6},{8,9},{9,8},{10,11... | collective-permute-start | bytes 23048 | tf_op jit(solution)/shard_map/ppermute | solution.py:196

commit v8 on v7

--- a/solution.py
+++ b/solution.py
@@ -11,6 +11,7 @@
 CELL = 0.0625
 LOG2E = math.log2(math.e)
 VMEM_LIMIT = 32 * 1024 * 1024
+ROOT_SCALE = 0.1875
 RIM_VMEM = (64 * 1024 - 10944) * 1024
 
 
@@ -75,7 +76,9 @@
     )(query_input, target_input, conv_weight)
 
 
-def own_kernel(query_ref, target_ref, weight_ref, bias_ref, query_out, target_out, *stages):
+def own_kernel(
+    query_ref, target_ref, weight_ref, bias_ref, query_out, target_out, upper_ref, lower_ref, *stages
+):
     for stage in stages:
         stage[pl.ds(0, 8), :] = jnp.zeros((8, stage.shape[1]), jnp.float32)
     pairs = ((target_ref, target_out), (query_ref, query_out))
@@ -86,16 +89,21 @@
                 frame_ref[tap_row - 1], weight_ref, tap_row, stages[2 * which + tap_row - 1]
             )
         out_ref[...] = total
+        if which == 0:
+            upper = total.astype(jnp.bfloat16)
+            upper_ref[...] = upper
+            lower_ref[...] = (total - upper.astype(jnp.float32)).astype(jnp.bfloat16)
 
 
 def own_partials(query_input, target_input, conv_weight, conv_bias):
     _, cols, channels = query_input.shape
     out_channels = conv_weight.shape[3]
     part = jax.ShapeDtypeStruct((cols // 2, out_channels), jnp.float32)
+    half = jax.ShapeDtypeStruct((cols // 2, out_channels), jnp.bfloat16)
     flops = 2 * 2 * 6 * (cols // 2) * channels * out_channels
     return pl.pallas_call(
         own_kernel,
-        out_shape=(part, part),
+        out_shape=(part, part, half, half),
         scratch_shapes=[pltpu.VMEM((cols + 8, channels), jnp.float32)] * 4,
         compiler_params=pltpu.CompilerParams(vmem_limit_bytes=VMEM_LIMIT),
         cost_estimate=pl.CostEstimate(flops=flops, bytes_accessed=1 << 22, transcendentals=0),
@@ -196,6 +204,16 @@
     return lax.ppermute(value, ("query", "target"), pairs)
 
 
+def squared(value):
+    return (value * jnp.abs(value) * (ROOT_SCALE * ROOT_SCALE)).astype(jnp.float16)
+
+
+def rooted(square):
+    square = square.astype(jnp.float32)
+    root = jnp.sqrt(jnp.abs(square)) * (1.0 / ROOT_SCALE)
+    return jnp.where(square < 0, -root, root)
+
+
 def on_device(query_input, target_input, conv_weight, conv_bias):
     slot = lax.axis_index("query")
     core = lax.axis_index("target")
@@ -213,17 +231,22 @@
 
     far_rim, near_rim = rim_partials(query_input, target_input, conv_weight)
     near_rim = swapped(near_rim)
+    far_rim, conv_bias = lax.optimization_barrier((squared(far_rim), conv_bias))
     far_rim = routed(far_rim, lambda s, c: ((s + 1) % slots, c))
-    far_rim = jnp.where(slot == 0, 0.0, far_rim)
-    query_part, target_part = own_partials(query_input, target_input, conv_weight, conv_bias)
+    far_rim = jnp.where(slot == 0, 0.0, rooted(far_rim))
+    near_rim, conv_bias = lax.optimization_barrier((near_rim, conv_bias))
+    query_part, target_part, upper, lower = own_partials(
+        query_input, target_input, conv_weight, conv_bias
+    )
     odd = (target_part + near_rim).astype(jnp.bfloat16)
-    handed = swapped(pick(target_part, odd.astype(jnp.float32)))
+    handed = swapped(pick(upper, odd))
+    rest = swapped(lower)
     odd_away = [
         routed(odd, lambda s, c: (s, 1) if c == 0 else ((s + 4 * hop) % slots, 0))
         for hop in range(1, max(2, slots // 4))
     ]
-    whole = (pick(query_part, handed) + far_rim).astype(jnp.bfloat16)
-    handed = handed.astype(jnp.bfloat16)
+    unfinished = handed.astype(jnp.float32) + rest.astype(jnp.float32)
+    whole = (pick(query_part, unfinished) + far_rim).astype(jnp.bfloat16)
     even_away = [
         routed(whole, lambda s, c: (s ^ 1, 0) if c == 0 else ((s + 4 * hop) % slots, 1))
         for hop in range(1, max(2, slots // 4))

time: 29.2 us -> 26.4 us (0.904); the launches traced: 28.7 us -> 26.3 us
  waiting for transfers between devices: 14.9 us -> 11.6 us
  starting transfers between devices: 7.31 us -> 7.95 us
    ppermute x11 -> x12, waiting for transfers between devices: 14.9 us -> 11.6 us  [routed(): return lax.ppermute(value, ('query', 'target'), pairs)]
    ppermute x11 -> x12, starting transfers between devices: 7.31 us -> 7.95 us  [routed(): return lax.ppermute(value, ('query', 'target'), pairs)]
  transfers between devices with their start and end apart: 11 -> 12, of which waited for: 5 -> 5; matrix products, arithmetic and copies ran while one was open for 0% -> 1% of each run, Pallas kernels for 7% -> 8%
where the time goes in v8:
time: 26.4 us; the launch traced here: 26.3 us
  waiting for transfers between devices  11.6 us (44%)
  starting transfers between devices  7.95 us (30%)
  Pallas kernels  4.9 us (19%)
  local copies, waits for them, and re-layouts  1.25 us (5%)
  other arithmetic  0.39 us (1%)
    ppermute x12, waiting for transfers between devices, routed(): return lax.ppermute(value, ('query', 'target'), pairs)  11.6 us
    ppermute x12, starting transfers between devices, routed(): return lax.ppermute(value, ('query', 'target'), pairs)  7.95 us
    pallas_call x3, Pallas kernels, match(): pl.pallas_call(functools.partial(match_kernel, count, bool(states), row_i...  2.78 us
    pallas_call x1, Pallas kernels, rim_partials(): pl.pallas_call(rim_kernel, out_shape=(jax.ShapeDtypeStruct((cols // 2, ou...  1.57 us
    unnamed x8, local copies, waits for them, and re-layouts  0.65 us
    reshape x1, local copies, waits for them, and re-layouts, on_device(): return jnp.stack([flow_x, flow_y]).reshape(2, 1, row_width)  0.6 us
    pallas_call x1, Pallas kernels, own_partials(): pl.pallas_call(own_kernel, out_shape=(part, part, half, half), scratch_sh...  0.55 us
  transfers between devices with their start and end apart: 12, of which 5 were waited for; matrix products, arithmetic and copies ran while one was open for 1% of the time, Pallas kernels for 8%

profile of v8, /device:TPU:0, one launch (start us, length us, event | category | flops | bytes accessed | tf_op | source)
XLA Modules:
  0.0 26.3 jit_solution(6512965293937541984)
XLA Ops:
  0.0 0.0 copy-start
  0.0 0.0 copy-start.1
  0.0 1.6 %rim_partials.1 = (f32[480,128]{1,0:T(8,128)S(1)}, f32[480,128]{1,0:T(8,128)S(1)}) custom-call(bf16[2,960,128]{2,1,0:T(8,128)(2,1)} %query_ref.1, bf16[2,960,128]{2,1,0:T(8,128)(2,1)} %target_ref.1, bf16[3,3,128,128]{3,2,1,0:T(8,128)(2,1)} %weight_ref.1), custom_call_target="tpu_custom_call" | custom-call | tf_op jit(solution)/shard_map/rim_partials/pallas_call | solution.py:63
  1.6 0.0 copy-start.2
  1.6 0.5 %collective-permute-start = (f32[480,128]{1,0:T(8,128)S(1)}, f32[480,128]{1,0:T(8,128)S(1)}, u32[]{:S(2)}, u32[]{:S(2)}) collective-permute-start(f32[480,128]{1,0:T(8,128)S(1)} %get-tuple-element.17), channel_id=1, source_target_pairs={{0,1},{1,0},{2,3},{3,2},{4,5},{5,4},{6,7},{7,6},{8,9},{9,8},{10,11... | collective-permute-start | bytes 737288 | tf_op jit(solution)/shard_map/ppermute | solution.py:204
  2.2 2.6 %collective-permute-start.3 = (f16[480,128]{1,0:T(8,128)(2,1)S(1)}, f16[480,128]{1,0:T(8,128)(2,1)S(1)}, u32[]{:S(2)}, u32[]{:S(2)}) collective-permute-start(f16[480,128]{1,0:T(8,128)(2,1)S(1)} %fusion.3), channel_id=1, source_target_pairs={{0,2},{1,3},{2,4},{3,5},{4,6},{5,7},{6,8},{7,9},{8,10},{9,11},{10,... | collective-permute-start | bytes 368648 | tf_op jit(solution)/shard_map/ppermute | solution.py:204
  4.7 0.0 copy-start.3
  4.8 0.0 collective-permute-done
  4.8 0.0 copy-done
  4.8 0.0 copy-done.1
  4.8 0.0 copy-done.2
  4.8 0.6 %copy-done.3 = f32[128]{0:T(128)S(1)} copy-done((f32[128]{0:T(128)S(1)}, f32[128]{0:T(128)}, u32[]{:S(2)}) %copy-start.3) | copy-done | bytes 536
  5.4 0.5 %own_partials.1 = (f32[480,128]{1,0:T(8,128)S(1)}, f32[480,128]{1,0:T(8,128)S(1)}, bf16[480,128]{1,0:T(8,128)(2,1)S(1)}, bf16[480,128]{1,0:T(8,128)(2,1)S(1)}) custom-call(bf16[2,960,128]{2,1,0:T(8,128)(2,1)S(1)} %copy-done, bf16[2,960,128]{2,1,0:T(8,128)(2,1)S(1)} %copy-done.1, bf16[3,3,128,128]{3,2,1,0:T(8,128)(2,1)S(1)} %copy-done.2, f32[1,128]{1,0:T(1,128)S(1)} %bitcast.7), custom_call_target="tpu_custom_call" | custom-call | flops 188743680 | bytes 4194304 | tf_op jit(solution)/shard_map/own_partials/pallas_call | solution.py:104
  6.0 0.3 %collective-permute-start.2 = (bf16[480,128]{1,0:T(8,128)(2,1)S(1)}, bf16[480,128]{1,0:T(8,128)(2,1)S(1)}, u32[]{:S(2)}, u32[]{:S(2)}) collective-permute-start(bf16[480,128]{1,0:T(8,128)(2,1)S(1)} %get-tuple-element.25), channel_id=1, source_target_pairs={{0,1},{1,0},{2,3},{3,2},{4,5},{5,4},{6,7},{7,6},{8,9},{9,8},{10,11... | collective-permute-start | bytes 368648 | tf_op jit(solution)/shard_map/ppermute | solution.py:204
  6.2 0.1 broadcast_select_fusion.1
  6.3 0.4 %collective-permute-start.1 = (bf16[480,128]{1,0:T(8,128)(2,1)S(1)}, bf16[480,128]{1,0:T(8,128)(2,1)S(1)}, u32[]{:S(2)}, u32[]{:S(2)}) collective-permute-start(bf16[480,128]{1,0:T(8,128)(2,1)S(1)} %get-tuple-element.31), channel_id=1, source_target_pairs={{0,1},{1,0},{2,3},{3,2},{4,5},{5,4},{6,7},{7,6},{8,9},{9,8},{10,11... | collective-permute-start | bytes 368648 | tf_op jit(solution)/shard_map/ppermute | solution.py:204
  6.7 0.2 collective-permute-start.7
  6.9 4.9 %collective-permute-done.3 = f16[480,128]{1,0:T(8,128)(2,1)S(1)} collective-permute-done((f16[480,128]{1,0:T(8,128)(2,1)S(1)}, f16[480,128]{1,0:T(8,128)(2,1)S(1)}, u32[]{:S(2)}, u32[]{:S(2)}) %collective-permute-start.3) | collective-permute-done | bytes 122912 | tf_op jit(solution)/shard_map/ppermute | solution.py:204
  11.8 0.0 collective-permute-done.2
  11.8 0.0 collective-permute-done.1.refs_4_
  11.8 0.2 fusion.6.refs_0_.refs_3_
  12.0 0.1 collective-permute-start.5
  12.1 1.3 %collective-permute-start.4 = (bf16[480,128]{1,0:T(8,128)(2,1)S(1)}, bf16[480,128]{1,0:T(8,128)(2,1)S(1)}, u32[]{:S(2)}, u32[]{:S(2)}) collective-permute-start(bf16[480,128]{1,0:T(8,128)(2,1)S(1)} %fusion.6.refs_0_.refs_3_), channel_id=1, source_target_pairs={{0,7},{1,0},{2,5},{3,2},{4,3},{5,4},{6,1},{7,6},{8,15},{9,8},{10,1... | collective-permute-start | bytes 368648 | tf_op jit(solution)/shard_map/ppermute | solution.py:204
  13.4 0.0 collective-permute-start.6
  13.4 0.0 collective-permute-done.7.refs_4_
  13.4 3.6 %collective-permute-done.5.refs_0_.refs_2_.refs_5_ = bf16[480,128]{1,0:T(8,128)(2,1)S(1)} collective-permute-done((bf16[480,128]{1,0:T(8,128)(2,1)S(1)}, bf16[480,128]{1,0:T(8,128)(2,1)S(1)}, u32[]{:S(2)}, u32[]{:S(2)}) %collective-permute-start.5) | collective-permute-done | bytes 122912 | tf_op jit(solution)/shard_map/ppermute | solution.py:204
  17.0 0.1 collective-permute-start.8
  17.1 0.0 collective-permute-done.4.refs_1_.refs_2_
  17.1 0.8 %match.3.refs_8_ = f32[4,480]{1,0:T(4,128)S(1)} custom-call(bf16[480,128]{1,0:T(8,128)(2,1)S(1)} %fusion.6.refs_0_.refs_3_, bf16[480,128]{1,0:T(8,128)(2,1)S(1)} %collective-permute-done.4.refs_1_.refs_2_, bf16[480,128]{1,0:T(8,128)(2,1)S(1)} %collective-permute-done.4.refs_1_.refs_2_, bf16[480,128]{1,0:T(8,128)(2,1)S(1)} %fusion.6.refs_0_.refs_3_, ...), custom_call_target="tpu_custom_call" | custom-call | flops 117964800 | bytes 4194304 | tf_op jit(solution)/shard_map/match/pallas_call | solution.py:172
  17.9 0.0 collective-permute-done.6.refs_1_.refs_3_
  17.9 0.8 %match.4.refs_9_ = f32[4,480]{1,0:T(4,128)S(1)} custom-call(bf16[480,128]{1,0:T(8,128)(2,1)S(1)} %collective-permute-done.5.refs_0_.refs_2_.refs_5_, bf16[480,128]{1,0:T(8,128)(2,1)S(1)} %collective-permute-done.6.refs_1_.refs_3_, bf16[480,128]{1,0:T(8,128)(2,1)S(1)} %collective-permute-done.4.refs_1_.refs_2_, bf16[480,128]{1,0:T(8,128)(2,1)S(1)} %fusion.6.refs_0_.refs_3_, ...), custom_call_target="tpu_custom_call" | custom-call | flops 117964800 | bytes 4194304 | tf_op jit(solution)/shard_map/match/pallas_call | solution.py:172
  18.6 0.0 collective-permute-done.8.refs_6_.refs_7_
  18.7 1.3 %match.5 = (f32[4,480]{1,0:T(4,128)S(1)}, f32[4,480]{1,0:T(4,128)S(1)}) custom-call(bf16[480,128]{1,0:T(8,128)(2,1)S(1)} %fusion.6.refs_0_.refs_3_, bf16[480,128]{1,0:T(8,128)(2,1)S(1)} %collective-permute-done.4.refs_1_.refs_2_, bf16[480,128]{1,0:T(8,128)(2,1)S(1)} %collective-permute-done.5.refs_0_.refs_2_.refs_5_, ...), custom_call_target="tpu_custom_call" | custom-call | flops 235929600 | bytes 4194304 | tf_op jit(solution)/shard_map/match/pallas_call | solution.py:172
  19.9 0.7 %collective-permute-start.9 = (f32[4,480]{1,0:T(4,128)S(1)}, f32[4,480]{1,0:T(4,128)S(1)}, u32[]{:S(2)}, u32[]{:S(2)}) collective-permute-start(f32[4,480]{1,0:T(4,128)S(1)} %get-tuple-element.27), channel_id=1, source_target_pairs={{0,2},{1,7},{2,0},{3,5},{4,6},{5,3},{6,4},{7,1},{8,10},{9,15},{10,... | collective-permute-start | bytes 23048 | tf_op jit(solution)/shard_map/ppermute | solution.py:204
  20.6 1.4 %collective-permute-start.10 = (f32[4,480]{1,0:T(4,128)S(1)}, f32[4,480]{1,0:T(4,128)S(1)}, u32[]{:S(2)}, u32[]{:S(2)}) collective-permute-start(f32[4,480]{1,0:T(4,128)S(1)} %get-tuple-element.28), channel_id=1, source_target_pairs={{0,2},{1,5},{2,0},{3,7},{4,6},{5,1},{6,4},{7,3},{8,10},{9,13},{10,... | collective-permute-start | bytes 23048 | tf_op jit(solution)/shard_map/ppermute | solution.py:204
  22.0 1.6 %collective-permute-done.9 = f32[4,480]{1,0:T(4,128)S(1)} collective-permute-done((f32[4,480]{1,0:T(4,128)S(1)}, f32[4,480]{1,0:T(4,128)S(1)}, u32[]{:S(2)}, u32[]{:S(2)}) %collective-permute-start.9) | collective-permute-done | bytes 7712 | tf_op jit(solution)/shard_map/ppermute | solution.py:204
  23.6 0.6 %collective-permute-done.10 = f32[4,480]{1,0:T(4,128)S(1)} collective-permute-done((f32[4,480]{1,0:T(4,128)S(1)}, f32[4,480]{1,0:T(4,128)S(1)}, u32[]{:S(2)}, u32[]{:S(2)}) %collective-permute-start.10) | collective-permute-done | bytes 7712 | tf_op jit(solution)/shard_map/ppermute | solution.py:204
  24.3 0.5 %collective-permute-start.11 = (f32[4,480]{1,0:T(4,128)S(1)}, f32[4,480]{1,0:T(4,128)S(1)}, u32[]{:S(2)}, u32[]{:S(2)}) collective-permute-start(f32[4,480]{1,0:T(4,128)S(1)} %pad_maximum_fusion), channel_id=1, source_target_pairs={{0,1},{1,0},{2,3},{3,2},{4,5},{5,4},{6,7},{7,6},{8,9},{9,8},{10,11... | collective-permute-start | bytes 23048 | tf_op jit(solution)/shard_map/ppermute | solution.py:204
  24.8 0.8 %collective-permute-done.11 = f32[4,480]{1,0:T(4,128)S(1)} collective-permute-done((f32[4,480]{1,0:T(4,128)S(1)}, f32[4,480]{1,0:T(4,128)S(1)}, u32[]{:S(2)}, u32[]{:S(2)}) %collective-permute-start.11) | collective-permute-done | bytes 7712 | tf_op jit(solution)/shard_map/ppermute | solution.py:204
  25.7 0.6 %copy.5 = f32[2,1,480]{2,1,0:T(1,128)} copy(f32[2,1,480]{2,0,1:T(2,128)S(1)} %maximum_bitcast_fusion) | data formatting | bytes 7680 | tf_op jit(solution)/shard_map/reshape | solution.py:277
  (11 shorter events, 0.2 us)
Async XLA Ops:
  0.0 4.8 %copy-start = (bf16[2,960,128]{2,1,0:T(8,128)(2,1)S(1)}, bf16[2,960,128]{2,1,0:T(8,128)(2,1)}, u32[]{:S(2)}) copy-start(bf16[2,960,128]{2,1,0:T(8,128)(2,1)} %query_ref.1) | copy-start | bytes 1474564
  0.0 4.8 %copy-start.1 = (bf16[2,960,128]{2,1,0:T(8,128)(2,1)S(1)}, bf16[2,960,128]{2,1,0:T(8,128)(2,1)}, u32[]{:S(2)}) copy-start(bf16[2,960,128]{2,1,0:T(8,128)(2,1)} %target_ref.1) | copy-start | bytes 1474564
  1.6 3.2 %copy-start.2 = (bf16[3,3,128,128]{3,2,1,0:T(8,128)(2,1)S(1)}, bf16[3,3,128,128]{3,2,1,0:T(8,128)(2,1)}, u32[]{:S(2)}) copy-start(bf16[3,3,128,128]{3,2,1,0:T(8,128)(2,1)} %weight_ref.1) | copy-start | bytes 884740
  1.6 3.2 %collective-permute-start = (f32[480,128]{1,0:T(8,128)S(1)}, f32[480,128]{1,0:T(8,128)S(1)}, u32[]{:S(2)}, u32[]{:S(2)}) collective-permute-start(f32[480,128]{1,0:T(8,128)S(1)} %get-tuple-element.17), channel_id=1, source_target_pairs={{0,1},{1,0},{2,3},{3,2},{4,5},{5,4},{6,7},{7,6},{8,9},{9,8},{10,11... | collective-permute-start | bytes 737288 | tf_op jit(solution)/shard_map/ppermute | solution.py:204
  2.2 9.6 %collective-permute-start.3 = (f16[480,128]{1,0:T(8,128)(2,1)S(1)}, f16[480,128]{1,0:T(8,128)(2,1)S(1)}, u32[]{:S(2)}, u32[]{:S(2)}) collective-permute-start(f16[480,128]{1,0:T(8,128)(2,1)S(1)} %fusion.3), channel_id=1, source_target_pairs={{0,2},{1,3},{2,4},{3,5},{4,6},{5,7},{6,8},{7,9},{8,10},{9,11},{10,... | collective-permute-start | bytes 368648 | tf_op jit(solution)/shard_map/ppermute | solution.py:204
  4.7 0.7 %copy-start.3 = (f32[128]{0:T(128)S(1)}, f32[128]{0:T(128)}, u32[]{:S(2)}) copy-start(f32[128]{0:T(128)} %param.7) | copy-start | bytes 1540
  6.0 5.8 %collective-permute-start.2 = (bf16[480,128]{1,0:T(8,128)(2,1)S(1)}, bf16[480,128]{1,0:T(8,128)(2,1)S(1)}, u32[]{:S(2)}, u32[]{:S(2)}) collective-permute-start(bf16[480,128]{1,0:T(8,128)(2,1)S(1)} %get-tuple-element.25), channel_id=1, source_target_pairs={{0,1},{1,0},{2,3},{3,2},{4,5},{5,4},{6,7},{7,6},{8,9},{9,8},{10,11... | collective-permute-start | bytes 368648 | tf_op jit(solution)/shard_map/ppermute | solution.py:204
  6.3 5.5 %collective-permute-start.1 = (bf16[480,128]{1,0:T(8,128)(2,1)S(1)}, bf16[480,128]{1,0:T(8,128)(2,1)S(1)}, u32[]{:S(2)}, u32[]{:S(2)}) collective-permute-start(bf16[480,128]{1,0:T(8,128)(2,1)S(1)} %get-tuple-element.31), channel_id=1, source_target_pairs={{0,1},{1,0},{2,3},{3,2},{4,5},{5,4},{6,7},{7,6},{8,9},{9,8},{10,11... | collective-permute-start | bytes 368648 | tf_op jit(solution)/shard_map/ppermute | solution.py:204
  6.7 6.7 %collective-permute-start.7 = (bf16[480,128]{1,0:T(8,128)(2,1)S(1)}, bf16[480,128]{1,0:T(8,128)(2,1)S(1)}, u32[]{:S(2)}, u32[]{:S(2)}) collective-permute-start(bf16[480,128]{1,0:T(8,128)(2,1)S(1)} %get-tuple-element.32.refs_5_), channel_id=1, source_target_pairs={{0,1},{1,8},{2,3},{3,10},{4,5},{5,12},{6,7},{7,14},{8,9},{9,0},{10... | collective-permute-start | bytes 368648 | tf_op jit(solution)/shard_map/ppermute | solution.py:204
  12.0 5.0 %collective-permute-start.5 = (bf16[480,128]{1,0:T(8,128)(2,1)S(1)}, bf16[480,128]{1,0:T(8,128)(2,1)S(1)}, u32[]{:S(2)}, u32[]{:S(2)}) collective-permute-start(bf16[480,128]{1,0:T(8,128)(2,1)S(1)} %fusion.6.refs_0_.refs_3_), channel_id=1, source_target_pairs={{0,2},{1,9},{2,0},{3,11},{4,6},{5,13},{6,4},{7,15},{8,10},{9,1},{1... | collective-permute-start | bytes 368648 | tf_op jit(solution)/shard_map/ppermute | solution.py:204
  12.1 5.0 %collective-permute-start.4 = (bf16[480,128]{1,0:T(8,128)(2,1)S(1)}, bf16[480,128]{1,0:T(8,128)(2,1)S(1)}, u32[]{:S(2)}, u32[]{:S(2)}) collective-permute-start(bf16[480,128]{1,0:T(8,128)(2,1)S(1)} %fusion.6.refs_0_.refs_3_), channel_id=1, source_target_pairs={{0,7},{1,0},{2,5},{3,2},{4,3},{5,4},{6,1},{7,6},{8,15},{9,8},{10,1... | collective-permute-start | bytes 368648 | tf_op jit(solution)/shard_map/ppermute | solution.py:204
  13.4 4.5 %collective-permute-start.6 = (bf16[480,128]{1,0:T(8,128)(2,1)S(1)}, bf16[480,128]{1,0:T(8,128)(2,1)S(1)}, u32[]{:S(2)}, u32[]{:S(2)}) collective-permute-start(bf16[480,128]{1,0:T(8,128)(2,1)S(1)} %fusion.6.refs_0_.refs_3_), channel_id=1, source_target_pairs={{0,5},{1,0},{2,7},{3,2},{4,1},{5,4},{6,3},{7,6},{8,13},{9,8},{10,1... | collective-permute-start | bytes 368648 | tf_op jit(solution)/shard_map/ppermute | solution.py:204
  17.0 1.6 %collective-permute-start.8 = (bf16[480,128]{1,0:T(8,128)(2,1)S(1)}, bf16[480,128]{1,0:T(8,128)(2,1)S(1)}, u32[]{:S(2)}, u32[]{:S(2)}) collective-permute-start(bf16[480,128]{1,0:T(8,128)(2,1)S(1)} %broadcast_select_fusion), channel_id=1, source_target_pairs={{0,1},{1,0},{2,3},{3,2},{4,5},{5,4},{6,7},{7,6},{8,9},{9,8},{10,11... | collective-permute-start | bytes 368648 | tf_op jit(solution)/shard_map/ppermute | solution.py:204
  19.9 3.7 %collective-permute-start.9 = (f32[4,480]{1,0:T(4,128)S(1)}, f32[4,480]{1,0:T(4,128)S(1)}, u32[]{:S(2)}, u32[]{:S(2)}) collective-permute-start(f32[4,480]{1,0:T(4,128)S(1)} %get-tuple-element.27), channel_id=1, source_target_pairs={{0,2},{1,7},{2,0},{3,5},{4,6},{5,3},{6,4},{7,1},{8,10},{9,15},{10,... | collective-permute-start | bytes 23048 | tf_op jit(solution)/shard_map/ppermute | solution.py:204
  20.6 3.7 %collective-permute-start.10 = (f32[4,480]{1,0:T(4,128)S(1)}, f32[4,480]{1,0:T(4,128)S(1)}, u32[]{:S(2)}, u32[]{:S(2)}) collective-permute-start(f32[4,480]{1,0:T(4,128)S(1)} %get-tuple-element.28), channel_id=1, source_target_pairs={{0,2},{1,5},{2,0},{3,7},{4,6},{5,1},{6,4},{7,3},{8,10},{9,13},{10,... | collective-permute-start | bytes 23048 | tf_op jit(solution)/shard_map/ppermute | solution.py:204
  24.3 1.3 %collective-permute-start.11 = (f32[4,480]{1,0:T(4,128)S(1)}, f32[4,480]{1,0:T(4,128)S(1)}, u32[]{:S(2)}, u32[]{:S(2)}) collective-permute-start(f32[4,480]{1,0:T(4,128)S(1)} %pad_maximum_fusion), channel_id=1, source_target_pairs={{0,1},{1,0},{2,3},{3,2},{4,5},{5,4},{6,7},{7,6},{8,9},{9,8},{10,11... | collective-permute-start | bytes 23048 | tf_op jit(solution)/shard_map/ppermute | solution.py:204

commit v9 on v7

--- a/solution.py
+++ b/solution.py
@@ -33,46 +33,66 @@
     return total
 
 
-def rim_kernel(
-    query_hbm, target_hbm, weight_hbm, far_rim_ref, near_rim_ref, rows_ref, taps_ref, sems, *stages
-):
+def rim_kernel(query_hbm, target_hbm, weight_hbm, rim_ref, near_ref, row_ref, taps_ref, sems, stage):
     first = lax.axis_index("target") == 0
     last = query_hbm.shape[0] - 1
-    copies = [
-        pltpu.make_async_copy(weight_hbm.at[pl.ds(0, 1)], taps_ref, sems.at[2]),
-        pltpu.make_async_copy(target_hbm.at[last], rows_ref.at[0], sems.at[0]),
-        pltpu.make_async_copy(query_hbm.at[last], rows_ref.at[1], sems.at[1]),
-    ]
-    for copy in copies:
-        copy.start()
-    for stage in stages:
-        stage[pl.ds(0, 8), :] = jnp.zeros((8, stage.shape[1]), jnp.float32)
-    for copy in copies:
-        copy.wait()
-    target_rim = tap_row_sum(rows_ref[0], taps_ref, 0, stages[0])
-    query_rim = tap_row_sum(rows_ref[1], taps_ref, 0, stages[1])
-    near_rim_ref[...] = target_rim.astype(near_rim_ref.dtype)
-    far_rim_ref[...] = jnp.where(first, query_rim, target_rim).astype(far_rim_ref.dtype)
+    taps_copy = pltpu.make_async_copy(weight_hbm.at[pl.ds(0, 1)], taps_ref, sems.at[0])
+    near_copy = pltpu.make_async_copy(target_hbm.at[last], near_ref, sems.at[2])
+
+    @pl.when(first)
+    def _():
+        pltpu.make_async_copy(query_hbm.at[last], row_ref, sems.at[1]).start()
+
+    @pl.when(jnp.logical_not(first))
+    def _():
+        pltpu.make_async_copy(target_hbm.at[last], row_ref, sems.at[1]).start()
+
+    taps_copy.start()
+    near_copy.start()
+    stage[pl.ds(0, 8), :] = jnp.zeros((8, stage.shape[1]), jnp.float32)
+    pltpu.make_async_copy(query_hbm.at[last], row_ref, sems.at[1]).wait()
+    taps_copy.wait()
+    rim_ref[...] = tap_row_sum(row_ref[...], taps_ref, 0, stage)
+    near_copy.wait()
 
 
 def rim_partials(query_input, target_input, conv_weight):
     _, cols, channels = query_input.shape
     out_channels = conv_weight.shape[3]
-    hbm = pl.BlockSpec(memory_space=pltpu.HBM)
     return pl.pallas_call(
         rim_kernel,
-        out_shape=(jax.ShapeDtypeStruct((cols // 2, out_channels), jnp.float32),) * 2,
-        in_specs=[hbm] * 3,
+        out_shape=(
+            jax.ShapeDtypeStruct((cols // 2, out_channels), jnp.float32),
+            jax.ShapeDtypeStruct((cols, channels), target_input.dtype),
+        ),
+        in_specs=[pl.BlockSpec(memory_space=pltpu.HBM)] * 3,
         out_specs=(pl.BlockSpec(memory_space=pltpu.VMEM),) * 2,
         scratch_shapes=[
-            pltpu.VMEM((2, cols, channels), jnp.bfloat16),
+            pltpu.VMEM((cols, channels), jnp.bfloat16),
             pltpu.VMEM((1,) + conv_weight.shape[1:], jnp.bfloat16),
             pltpu.SemaphoreType.DMA((3,)),
-        ]
-        + [pltpu.VMEM((cols + 8, channels), jnp.float32)] * 2,
+            pltpu.VMEM((cols + 8, channels), jnp.float32),
+        ],
         compiler_params=pltpu.CompilerParams(vmem_limit_bytes=RIM_VMEM),
         name="rim_partials",
     )(query_input, target_input, conv_weight)
+
+
+def odd_kernel(row_ref, weight_ref, part_ref, odd_ref, stage):
+    stage[pl.ds(0, 8), :] = jnp.zeros((8, stage.shape[1]), jnp.float32)
+    rim = tap_row_sum(row_ref[...], weight_ref, 0, stage)
+    odd_ref[...] = (part_ref[...] + rim).astype(odd_ref.dtype)
+
+
+def odd_row(row, conv_weight, part):
+    cols, channels = row.shape
+    return pl.pallas_call(
+        odd_kernel,
+        out_shape=jax.ShapeDtypeStruct(part.shape, jnp.bfloat16),
+        scratch_shapes=[pltpu.VMEM((cols + 8, channels), jnp.float32)],
+        compiler_params=pltpu.CompilerParams(vmem_limit_bytes=VMEM_LIMIT),
+        name="odd_row",
+    )(row, conv_weight, part)
 
 
 def own_kernel(query_ref, target_ref, weight_ref, bias_ref, query_out, target_out, *stages):
@@ -211,12 +231,12 @@
     def swapped(value):
         return routed(value, lambda s, c: (s, 1 - c))
 
-    far_rim, near_rim = rim_partials(query_input, target_input, conv_weight)
-    near_rim = swapped(near_rim)
+    far_rim, near_row = rim_partials(query_input, target_input, conv_weight)
+    near_row = swapped(near_row)
     far_rim = routed(far_rim, lambda s, c: ((s + 1) % slots, c))
     far_rim = jnp.where(slot == 0, 0.0, far_rim)
     query_part, target_part = own_partials(query_input, target_input, conv_weight, conv_bias)
-    odd = (target_part + near_rim).astype(jnp.bfloat16)
+    odd = odd_row(near_row, conv_weight, target_part)
     handed = swapped(pick(target_part, odd.astype(jnp.float32)))
     odd_away = [
         routed(odd, lambda s, c: (s, 1) if c == 0 else ((s + 4 * hop) % slots, 0))

time: 29.2 us -> 29 us (level)
  waiting for transfers between devices: 14.9 us -> 14.6 us
  transfers between devices with their start and end apart: 11 -> 11, of which waited for: 5 -> 5; matrix products, arithmetic and copies ran while one was open for 0% -> 0% of each run, Pallas kernels for 7% -> 8%
where the time goes in v9:
time: 29 us; the launch traced here: 28.5 us
  waiting for transfers between devices  14.6 us (50%)
  starting transfers between devices  7.31 us (25%)
  Pallas kernels  4.98 us (17%)
  local copies, waits for them, and re-layouts  1.25 us (4%)
    ppermute x11, waiting for transfers between devices, routed(): return lax.ppermute(value, ('query', 'target'), pairs)  14.6 us
    ppermute x11, starting transfers between devices, routed(): return lax.ppermute(value, ('query', 'target'), pairs)  7.31 us
    pallas_call x3, Pallas kernels, match(): pl.pallas_call(functools.partial(match_kernel, count, bool(states), row_i...  2.79 us
    pallas_call x1, Pallas kernels, rim_partials(): pl.pallas_call(rim_kernel, out_shape=(jax.ShapeDtypeStruct((cols // 2, ou...  1.39 us
    unnamed x8, local copies, waits for them, and re-layouts  0.66 us
    reshape x1, local copies, waits for them, and re-layouts, on_device(): return jnp.stack([flow_x, flow_y]).reshape(2, 1, row_width)  0.6 us
  transfers between devices with their start and end apart: 11, of which 5 were waited for; matrix products, arithmetic and copies ran while one was open for 0% of the time, Pallas kernels for 8%

profile of v9, /device:TPU:0, one launch (start us, length us, event | category | flops | bytes accessed | tf_op | source)
XLA Modules:
  0.0 28.5 jit_solution(8556318187812856076)
XLA Ops:
  0.0 0.0 copy-start.1
  0.0 0.0 copy-start.2
  0.0 0.0 copy-start
  0.0 1.4 %rim_partials.1 = (f32[480,128]{1,0:T(8,128)S(1)}, bf16[960,128]{1,0:T(8,128)(2,1)S(1)}) custom-call(bf16[2,960,128]{2,1,0:T(8,128)(2,1)} %query_hbm.1, bf16[2,960,128]{2,1,0:T(8,128)(2,1)} %target_hbm.1, bf16[3,3,128,128]{3,2,1,0:T(8,128)(2,1)} %weight_ref.3), custom_call_target="tpu_custom_call" | custom-call | tf_op jit(solution)/shard_map/rim_partials/pallas_call | solution.py:62
  1.4 0.5 %collective-permute-start = (bf16[960,128]{1,0:T(8,128)(2,1)S(1)}, bf16[960,128]{1,0:T(8,128)(2,1)S(1)}, u32[]{:S(2)}, u32[]{:S(2)}) collective-permute-start(bf16[960,128]{1,0:T(8,128)(2,1)S(1)} %get-tuple-element.13), channel_id=1, source_target_pairs={{0,1},{1,0},{2,3},{3,2},{4,5},{5,4},{6,7},{7,6},{8,9},{9,8},{10,11... | collective-permute-start | bytes 737288 | tf_op jit(solution)/shard_map/ppermute | solution.py:216
  1.9 2.6 %collective-permute-start.2 = (f32[480,128]{1,0:T(8,128)S(1)}, f32[480,128]{1,0:T(8,128)S(1)}, u32[]{:S(2)}, u32[]{:S(2)}) collective-permute-start(f32[480,128]{1,0:T(8,128)S(1)} %get-tuple-element.14), channel_id=1, source_target_pairs={{0,2},{1,3},{2,4},{3,5},{4,6},{5,7},{6,8},{7,9},{8,10},{9,11},{10,... | collective-permute-start | bytes 737288 | tf_op jit(solution)/shard_map/ppermute | solution.py:216
  4.5 0.0 copy-start.3
  4.5 0.0 copy-done.1
  4.5 0.0 copy-done.2
  4.5 0.0 copy-done
  4.5 0.6 %copy-done.3 = f32[128]{0:T(128)S(1)} copy-done((f32[128]{0:T(128)S(1)}, f32[128]{0:T(128)}, u32[]{:S(2)}) %copy-start.3) | copy-done | bytes 536
  5.2 0.5 %own_partials.1 = (f32[480,128]{1,0:T(8,128)S(1)}, f32[480,128]{1,0:T(8,128)S(1)}) custom-call(bf16[2,960,128]{2,1,0:T(8,128)(2,1)S(1)} %copy-done.1, bf16[2,960,128]{2,1,0:T(8,128)(2,1)S(1)} %copy-done.2, bf16[3,3,128,128]{3,2,1,0:T(8,128)(2,1)S(1)} %copy-done, f32[1,128]{1,0:T(1,128)S(1)} %bitcast.7), custom_call_target="tpu_custom_call" | custom-call | flops 188743680 | bytes 4194304 | tf_op jit(solution)/shard_map/own_partials/pallas_call | solution.py:116
  5.7 0.0 collective-permute-done.row_ref
  5.7 0.3 odd_row.1.refs_5_
  6.0 0.2 collective-permute-start.1
  6.3 0.3 %collective-permute-start.6 = (bf16[480,128]{1,0:T(8,128)(2,1)S(1)}, bf16[480,128]{1,0:T(8,128)(2,1)S(1)}, u32[]{:S(2)}, u32[]{:S(2)}) collective-permute-start(bf16[480,128]{1,0:T(8,128)(2,1)S(1)} %odd_row.1.refs_5_), channel_id=1, source_target_pairs={{0,1},{1,8},{2,3},{3,10},{4,5},{5,12},{6,7},{7,14},{8,9},{9,0},{10... | collective-permute-start | bytes 368648 | tf_op jit(solution)/shard_map/ppermute | solution.py:216
  6.6 7.9 %collective-permute-done.2 = f32[480,128]{1,0:T(8,128)S(1)} collective-permute-done((f32[480,128]{1,0:T(8,128)S(1)}, f32[480,128]{1,0:T(8,128)S(1)}, u32[]{:S(2)}, u32[]{:S(2)}) %collective-permute-start.2) | collective-permute-done | bytes 245792 | tf_op jit(solution)/shard_map/ppermute | solution.py:216
  14.5 0.0 collective-permute-done.1
  14.5 0.1 collective-permute-start.4
  14.6 0.9 %collective-permute-start.3 = (bf16[480,128]{1,0:T(8,128)(2,1)S(1)}, bf16[480,128]{1,0:T(8,128)(2,1)S(1)}, u32[]{:S(2)}, u32[]{:S(2)}) collective-permute-start(bf16[480,128]{1,0:T(8,128)(2,1)S(1)} %get-tuple-element.20.refs_0_.refs_3_), channel_id=1, source_target_pairs={{0,7},{1,0},{2,5},{3,2},{4,3},{5,4},{6,1},{7,6},{8,15},{9,8},{10,1... | collective-permute-start | bytes 368648 | tf_op jit(solution)/shard_map/ppermute | solution.py:216
  15.5 0.0 collective-permute-start.5
  15.5 0.0 collective-permute-done.6.refs_4_
  15.5 4.0 %collective-permute-done.4.refs_0_.refs_2_.refs_5_ = bf16[480,128]{1,0:T(8,128)(2,1)S(1)} collective-permute-done((bf16[480,128]{1,0:T(8,128)(2,1)S(1)}, bf16[480,128]{1,0:T(8,128)(2,1)S(1)}, u32[]{:S(2)}, u32[]{:S(2)}) %collective-permute-start.4) | collective-permute-done | bytes 122912 | tf_op jit(solution)/shard_map/ppermute | solution.py:216
  19.6 0.1 collective-permute-start.7
  19.7 0.0 collective-permute-done.3.refs_1_.refs_2_
  19.7 0.8 %match.3.refs_8_ = f32[4,480]{1,0:T(4,128)S(1)} custom-call(bf16[480,128]{1,0:T(8,128)(2,1)S(1)} %get-tuple-element.20.refs_0_.refs_3_, bf16[480,128]{1,0:T(8,128)(2,1)S(1)} %collective-permute-done.3.refs_1_.refs_2_, bf16[480,128]{1,0:T(8,128)(2,1)S(1)} %collective-permute-done.3.refs_1_.refs_2_, bf16[480,128]{1,0:T(8,128)(2,1)S(1)} %get-tuple-element.20.refs_0_.refs_3_, ...), custom_call_target="tpu_custom_call" | custom-call | flops 117964800 | bytes 4194304 | tf_op jit(solution)/shard_map/match/pallas_call | solution.py:184
  20.4 0.0 collective-permute-done.5.refs_1_.refs_3_
  20.5 0.8 %match.4.refs_9_ = f32[4,480]{1,0:T(4,128)S(1)} custom-call(bf16[480,128]{1,0:T(8,128)(2,1)S(1)} %collective-permute-done.4.refs_0_.refs_2_.refs_5_, bf16[480,128]{1,0:T(8,128)(2,1)S(1)} %collective-permute-done.5.refs_1_.refs_3_, bf16[480,128]{1,0:T(8,128)(2,1)S(1)} %collective-permute-done.3.refs_1_.refs_2_, ...), custom_call_target="tpu_custom_call" | custom-call | flops 117964800 | bytes 4194304 | tf_op jit(solution)/shard_map/match/pallas_call | solution.py:184
  21.2 0.0 collective-permute-done.7.refs_6_.refs_7_
  21.2 1.3 %match.5 = (f32[4,480]{1,0:T(4,128)S(1)}, f32[4,480]{1,0:T(4,128)S(1)}) custom-call(bf16[480,128]{1,0:T(8,128)(2,1)S(1)} %get-tuple-element.20.refs_0_.refs_3_, bf16[480,128]{1,0:T(8,128)(2,1)S(1)} %collective-permute-done.3.refs_1_.refs_2_, bf16[480,128]{1,0:T(8,128)(2,1)S(1)} %collective-permute-done.4.refs_0_.refs_2_.refs_5_, ...), custom_call_target="tpu_custom_call" | custom-call | flops 235929600 | bytes 4194304 | tf_op jit(solution)/shard_map/match/pallas_call | solution.py:184
  22.5 0.3 %collective-permute-start.8 = (f32[4,480]{1,0:T(4,128)S(1)}, f32[4,480]{1,0:T(4,128)S(1)}, u32[]{:S(2)}, u32[]{:S(2)}) collective-permute-start(f32[4,480]{1,0:T(4,128)S(1)} %get-tuple-element.15), channel_id=1, source_target_pairs={{0,2},{1,7},{2,0},{3,5},{4,6},{5,3},{6,4},{7,1},{8,10},{9,15},{10,... | collective-permute-start | bytes 23048 | tf_op jit(solution)/shard_map/ppermute | solution.py:216
  22.8 1.7 %collective-permute-start.9 = (f32[4,480]{1,0:T(4,128)S(1)}, f32[4,480]{1,0:T(4,128)S(1)}, u32[]{:S(2)}, u32[]{:S(2)}) collective-permute-start(f32[4,480]{1,0:T(4,128)S(1)} %get-tuple-element.16), channel_id=1, source_target_pairs={{0,2},{1,5},{2,0},{3,7},{4,6},{5,1},{6,4},{7,3},{8,10},{9,13},{10,... | collective-permute-start | bytes 23048 | tf_op jit(solution)/shard_map/ppermute | solution.py:216
  24.6 1.6 %collective-permute-done.8 = f32[4,480]{1,0:T(4,128)S(1)} collective-permute-done((f32[4,480]{1,0:T(4,128)S(1)}, f32[4,480]{1,0:T(4,128)S(1)}, u32[]{:S(2)}, u32[]{:S(2)}) %collective-permute-start.8) | collective-permute-done | bytes 7712 | tf_op jit(solution)/shard_map/ppermute | solution.py:216
  26.2 0.3 collective-permute-done.9
  26.6 0.5 %collective-permute-start.10 = (f32[4,480]{1,0:T(4,128)S(1)}, f32[4,480]{1,0:T(4,128)S(1)}, u32[]{:S(2)}, u32[]{:S(2)}) collective-permute-start(f32[4,480]{1,0:T(4,128)S(1)} %pad_maximum_fusion), channel_id=1, source_target_pairs={{0,1},{1,0},{2,3},{3,2},{4,5},{5,4},{6,7},{7,6},{8,9},{9,8},{10,11... | collective-permute-start | bytes 23048 | tf_op jit(solution)/shard_map/ppermute | solution.py:216
  27.0 0.8 %collective-permute-done.10 = f32[4,480]{1,0:T(4,128)S(1)} collective-permute-done((f32[4,480]{1,0:T(4,128)S(1)}, f32[4,480]{1,0:T(4,128)S(1)}, u32[]{:S(2)}, u32[]{:S(2)}) %collective-permute-start.10) | collective-permute-done | bytes 7712 | tf_op jit(solution)/shard_map/ppermute | solution.py:216
  27.9 0.6 %copy.5 = f32[2,1,480]{2,1,0:T(1,128)} copy(f32[2,1,480]{2,0,1:T(2,128)S(1)} %maximum_bitcast_fusion) | data formatting | bytes 7680 | tf_op jit(solution)/shard_map/reshape | solution.py:274
  (12 shorter events, 0.2 us)
Async XLA Ops:
  0.0 4.5 %copy-start.1 = (bf16[2,960,128]{2,1,0:T(8,128)(2,1)S(1)}, bf16[2,960,128]{2,1,0:T(8,128)(2,1)}, u32[]{:S(2)}) copy-start(bf16[2,960,128]{2,1,0:T(8,128)(2,1)} %query_hbm.1) | copy-start | bytes 1474564
  0.0 4.5 %copy-start.2 = (bf16[2,960,128]{2,1,0:T(8,128)(2,1)S(1)}, bf16[2,960,128]{2,1,0:T(8,128)(2,1)}, u32[]{:S(2)}) copy-start(bf16[2,960,128]{2,1,0:T(8,128)(2,1)} %target_hbm.1) | copy-start | bytes 1474564
  0.0 4.5 %copy-start = (bf16[3,3,128,128]{3,2,1,0:T(8,128)(2,1)S(1)}, bf16[3,3,128,128]{3,2,1,0:T(8,128)(2,1)}, u32[]{:S(2)}) copy-start(bf16[3,3,128,128]{3,2,1,0:T(8,128)(2,1)} %weight_ref.3) | copy-start | bytes 884740
  1.4 4.3 %collective-permute-start = (bf16[960,128]{1,0:T(8,128)(2,1)S(1)}, bf16[960,128]{1,0:T(8,128)(2,1)S(1)}, u32[]{:S(2)}, u32[]{:S(2)}) collective-permute-start(bf16[960,128]{1,0:T(8,128)(2,1)S(1)} %get-tuple-element.13), channel_id=1, source_target_pairs={{0,1},{1,0},{2,3},{3,2},{4,5},{5,4},{6,7},{7,6},{8,9},{9,8},{10,11... | collective-permute-start | bytes 737288 | tf_op jit(solution)/shard_map/ppermute | solution.py:216
  1.9 12.5 %collective-permute-start.2 = (f32[480,128]{1,0:T(8,128)S(1)}, f32[480,128]{1,0:T(8,128)S(1)}, u32[]{:S(2)}, u32[]{:S(2)}) collective-permute-start(f32[480,128]{1,0:T(8,128)S(1)} %get-tuple-element.14), channel_id=1, source_target_pairs={{0,2},{1,3},{2,4},{3,5},{4,6},{5,7},{6,8},{7,9},{8,10},{9,11},{10,... | collective-permute-start | bytes 737288 | tf_op jit(solution)/shard_map/ppermute | solution.py:216
  4.5 0.7 %copy-start.3 = (f32[128]{0:T(128)S(1)}, f32[128]{0:T(128)}, u32[]{:S(2)}) copy-start(f32[128]{0:T(128)} %param.7) | copy-start | bytes 1540
  6.0 8.4 %collective-permute-start.1 = (f32[480,128]{1,0:T(8,128)S(1)}, f32[480,128]{1,0:T(8,128)S(1)}, u32[]{:S(2)}, u32[]{:S(2)}) collective-permute-start(f32[480,128]{1,0:T(8,128)S(1)} %convert_select_fusion), channel_id=1, source_target_pairs={{0,1},{1,0},{2,3},{3,2},{4,5},{5,4},{6,7},{7,6},{8,9},{9,8},{10,11... | collective-permute-start | bytes 737288 | tf_op jit(solution)/shard_map/ppermute | solution.py:216
  6.3 9.3 %collective-permute-start.6 = (bf16[480,128]{1,0:T(8,128)(2,1)S(1)}, bf16[480,128]{1,0:T(8,128)(2,1)S(1)}, u32[]{:S(2)}, u32[]{:S(2)}) collective-permute-start(bf16[480,128]{1,0:T(8,128)(2,1)S(1)} %odd_row.1.refs_5_), channel_id=1, source_target_pairs={{0,1},{1,8},{2,3},{3,10},{4,5},{5,12},{6,7},{7,14},{8,9},{9,0},{10... | collective-permute-start | bytes 368648 | tf_op jit(solution)/shard_map/ppermute | solution.py:216
  14.5 5.1 %collective-permute-start.4 = (bf16[480,128]{1,0:T(8,128)(2,1)S(1)}, bf16[480,128]{1,0:T(8,128)(2,1)S(1)}, u32[]{:S(2)}, u32[]{:S(2)}) collective-permute-start(bf16[480,128]{1,0:T(8,128)(2,1)S(1)} %get-tuple-element.20.refs_0_.refs_3_), channel_id=1, source_target_pairs={{0,2},{1,9},{2,0},{3,11},{4,6},{5,13},{6,4},{7,15},{8,10},{9,1},{1... | collective-permute-start | bytes 368648 | tf_op jit(solution)/shard_map/ppermute | solution.py:216
  14.6 5.1 %collective-permute-start.3 = (bf16[480,128]{1,0:T(8,128)(2,1)S(1)}, bf16[480,128]{1,0:T(8,128)(2,1)S(1)}, u32[]{:S(2)}, u32[]{:S(2)}) collective-permute-start(bf16[480,128]{1,0:T(8,128)(2,1)S(1)} %get-tuple-element.20.refs_0_.refs_3_), channel_id=1, source_target_pairs={{0,7},{1,0},{2,5},{3,2},{4,3},{5,4},{6,1},{7,6},{8,15},{9,8},{10,1... | collective-permute-start | bytes 368648 | tf_op jit(solution)/shard_map/ppermute | solution.py:216
  15.5 4.9 %collective-permute-start.5 = (bf16[480,128]{1,0:T(8,128)(2,1)S(1)}, bf16[480,128]{1,0:T(8,128)(2,1)S(1)}, u32[]{:S(2)}, u32[]{:S(2)}) collective-permute-start(bf16[480,128]{1,0:T(8,128)(2,1)S(1)} %get-tuple-element.20.refs_0_.refs_3_), channel_id=1, source_target_pairs={{0,5},{1,0},{2,7},{3,2},{4,1},{5,4},{6,3},{7,6},{8,13},{9,8},{10,1... | collective-permute-start | bytes 368648 | tf_op jit(solution)/shard_map/ppermute | solution.py:216
  19.6 1.6 %collective-permute-start.7 = (bf16[480,128]{1,0:T(8,128)(2,1)S(1)}, bf16[480,128]{1,0:T(8,128)(2,1)S(1)}, u32[]{:S(2)}, u32[]{:S(2)}) collective-permute-start(bf16[480,128]{1,0:T(8,128)(2,1)S(1)} %broadcast_select_fusion), channel_id=1, source_target_pairs={{0,1},{1,0},{2,3},{3,2},{4,5},{5,4},{6,7},{7,6},{8,9},{9,8},{10,11... | collective-permute-start | bytes 368648 | tf_op jit(solution)/shard_map/ppermute | solution.py:216
  22.5 3.7 %collective-permute-start.8 = (f32[4,480]{1,0:T(4,128)S(1)}, f32[4,480]{1,0:T(4,128)S(1)}, u32[]{:S(2)}, u32[]{:S(2)}) collective-permute-start(f32[4,480]{1,0:T(4,128)S(1)} %get-tuple-element.15), channel_id=1, source_target_pairs={{0,2},{1,7},{2,0},{3,5},{4,6},{5,3},{6,4},{7,1},{8,10},{9,15},{10,... | collective-permute-start | bytes 23048 | tf_op jit(solution)/shard_map/ppermute | solution.py:216
  22.8 3.7 %collective-permute-start.9 = (f32[4,480]{1,0:T(4,128)S(1)}, f32[4,480]{1,0:T(4,128)S(1)}, u32[]{:S(2)}, u32[]{:S(2)}) collective-permute-start(f32[4,480]{1,0:T(4,128)S(1)} %get-tuple-element.16), channel_id=1, source_target_pairs={{0,2},{1,5},{2,0},{3,7},{4,6},{5,1},{6,4},{7,3},{8,10},{9,13},{10,... | collective-permute-start | bytes 23048 | tf_op jit(solution)/shard_map/ppermute | solution.py:216
  26.6 1.3 %collective-permute-start.10 = (f32[4,480]{1,0:T(4,128)S(1)}, f32[4,480]{1,0:T(4,128)S(1)}, u32[]{:S(2)}, u32[]{:S(2)}) collective-permute-start(f32[4,480]{1,0:T(4,128)S(1)} %pad_maximum_fusion), channel_id=1, source_target_pairs={{0,1},{1,0},{2,3},{3,2},{4,5},{5,4},{6,7},{7,6},{8,9},{9,8},{10,11... | collective-permute-start | bytes 23048 | tf_op jit(solution)/shard_map/ppermute | solution.py:216

commit v10 on v9

--- a/solution.py
+++ b/solution.py
@@ -252,7 +252,7 @@
     corner = routed(whole, lambda s, c: (s ^ 3, 1) if c == 0 else (s, 0))
 
     members = [(whole, corner), (even_away[0], below)]
-    rows = [(corner, whole), (handed, odd)]
+    rows = [(below, whole), (handed, odd)]
     states = [match([member], rows, lambda s, c: (2 * s, 2 * s + 1))[0] for member in members]
     for hop in range(1, slots // 4):
         away = swapped(pick(odd_away[hop - 1], even_away[hop - 1]))

time: 29 us -> 28.7 us (0.990); the launches traced: 28.5 us -> 28.6 us
  starting transfers between devices: 7.31 us -> 7.74 us
  waiting for transfers between devices: 14.6 us -> 14.2 us
    ppermute x11, starting transfers between devices: 7.31 us -> 7.74 us  [routed(): return lax.ppermute(value, ('query', 'target'), pairs)]
    ppermute x11, waiting for transfers between devices: 14.6 us -> 14.2 us  [routed(): return lax.ppermute(value, ('query', 'target'), pairs)]
where the time goes in v10:
time: 28.7 us; the launch traced here: 28.6 us
  waiting for transfers between devices  14.2 us (49%)
  starting transfers between devices  7.74 us (27%)
  Pallas kernels  4.98 us (17%)
  local copies, waits for them, and re-layouts  1.25 us (4%)
    ppermute x11, waiting for transfers between devices, routed(): return lax.ppermute(value, ('query', 'target'), pairs)  14.2 us
    ppermute x11, starting transfers between devices, routed(): return lax.ppermute(value, ('query', 'target'), pairs)  7.74 us
    pallas_call x3, Pallas kernels, match(): pl.pallas_call(functools.partial(match_kernel, count, bool(states), row_i...  2.78 us
    pallas_call x1, Pallas kernels, rim_partials(): pl.pallas_call(rim_kernel, out_shape=(jax.ShapeDtypeStruct((cols // 2, ou...  1.39 us
    unnamed x8, local copies, waits for them, and re-layouts  0.66 us
    reshape x1, local copies, waits for them, and re-layouts, on_device(): return jnp.stack([flow_x, flow_y]).reshape(2, 1, row_width)  0.6 us
  transfers between devices with their start and end apart: 11, of which 5 were waited for; matrix products, arithmetic and copies ran while one was open for 0% of the time, Pallas kernels for 8%

profile of v10, /device:TPU:0, one launch (start us, length us, event | category | flops | bytes accessed | tf_op | source)
XLA Modules:
  0.0 28.6 jit_solution(818154721365017123)
XLA Ops:
  0.0 0.0 copy-start.1
  0.0 0.0 copy-start.2
  0.0 0.0 copy-start
  0.0 1.4 %rim_partials.1 = (f32[480,128]{1,0:T(8,128)S(1)}, bf16[960,128]{1,0:T(8,128)(2,1)S(1)}) custom-call(bf16[2,960,128]{2,1,0:T(8,128)(2,1)} %query_hbm.1, bf16[2,960,128]{2,1,0:T(8,128)(2,1)} %target_hbm.1, bf16[3,3,128,128]{3,2,1,0:T(8,128)(2,1)} %weight_ref.3), custom_call_target="tpu_custom_call" | custom-call | tf_op jit(solution)/shard_map/rim_partials/pallas_call | solution.py:62
  1.4 0.5 %collective-permute-start = (bf16[960,128]{1,0:T(8,128)(2,1)S(1)}, bf16[960,128]{1,0:T(8,128)(2,1)S(1)}, u32[]{:S(2)}, u32[]{:S(2)}) collective-permute-start(bf16[960,128]{1,0:T(8,128)(2,1)S(1)} %get-tuple-element.13), channel_id=1, source_target_pairs={{0,1},{1,0},{2,3},{3,2},{4,5},{5,4},{6,7},{7,6},{8,9},{9,8},{10,11... | collective-permute-start | bytes 737288 | tf_op jit(solution)/shard_map/ppermute | solution.py:216
  1.9 2.6 %collective-permute-start.2 = (f32[480,128]{1,0:T(8,128)S(1)}, f32[480,128]{1,0:T(8,128)S(1)}, u32[]{:S(2)}, u32[]{:S(2)}) collective-permute-start(f32[480,128]{1,0:T(8,128)S(1)} %get-tuple-element.14), channel_id=1, source_target_pairs={{0,2},{1,3},{2,4},{3,5},{4,6},{5,7},{6,8},{7,9},{8,10},{9,11},{10,... | collective-permute-start | bytes 737288 | tf_op jit(solution)/shard_map/ppermute | solution.py:216
  4.5 0.0 copy-start.3
  4.5 0.0 copy-done.1
  4.5 0.0 copy-done.2
  4.5 0.0 copy-done
  4.5 0.6 %copy-done.3 = f32[128]{0:T(128)S(1)} copy-done((f32[128]{0:T(128)S(1)}, f32[128]{0:T(128)}, u32[]{:S(2)}) %copy-start.3) | copy-done | bytes 536
  5.2 0.5 %own_partials.1 = (f32[480,128]{1,0:T(8,128)S(1)}, f32[480,128]{1,0:T(8,128)S(1)}) custom-call(bf16[2,960,128]{2,1,0:T(8,128)(2,1)S(1)} %copy-done.1, bf16[2,960,128]{2,1,0:T(8,128)(2,1)S(1)} %copy-done.2, bf16[3,3,128,128]{3,2,1,0:T(8,128)(2,1)S(1)} %copy-done, f32[1,128]{1,0:T(1,128)S(1)} %bitcast.7), custom_call_target="tpu_custom_call" | custom-call | flops 188743680 | bytes 4194304 | tf_op jit(solution)/shard_map/own_partials/pallas_call | solution.py:116
  5.7 0.0 collective-permute-done.row_ref
  5.7 0.3 odd_row.1.refs_5_
  6.0 0.2 collective-permute-start.1
  6.3 0.3 %collective-permute-start.6 = (bf16[480,128]{1,0:T(8,128)(2,1)S(1)}, bf16[480,128]{1,0:T(8,128)(2,1)S(1)}, u32[]{:S(2)}, u32[]{:S(2)}) collective-permute-start(bf16[480,128]{1,0:T(8,128)(2,1)S(1)} %odd_row.1.refs_5_), channel_id=1, source_target_pairs={{0,1},{1,8},{2,3},{3,10},{4,5},{5,12},{6,7},{7,14},{8,9},{9,0},{10... | collective-permute-start | bytes 368648 | tf_op jit(solution)/shard_map/ppermute | solution.py:216
  6.6 7.9 %collective-permute-done.2 = f32[480,128]{1,0:T(8,128)S(1)} collective-permute-done((f32[480,128]{1,0:T(8,128)S(1)}, f32[480,128]{1,0:T(8,128)S(1)}, u32[]{:S(2)}, u32[]{:S(2)}) %collective-permute-start.2) | collective-permute-done | bytes 245792 | tf_op jit(solution)/shard_map/ppermute | solution.py:216
  14.5 0.0 collective-permute-done.1
  14.5 0.1 collective-permute-start.4
  14.6 0.9 %collective-permute-start.5 = (bf16[480,128]{1,0:T(8,128)(2,1)S(1)}, bf16[480,128]{1,0:T(8,128)(2,1)S(1)}, u32[]{:S(2)}, u32[]{:S(2)}) collective-permute-start(bf16[480,128]{1,0:T(8,128)(2,1)S(1)} %get-tuple-element.20.refs_0_.refs_3_), channel_id=1, source_target_pairs={{0,5},{1,0},{2,7},{3,2},{4,1},{5,4},{6,3},{7,6},{8,13},{9,8},{10,1... | collective-permute-start | bytes 368648 | tf_op jit(solution)/shard_map/ppermute | solution.py:216
  15.5 0.5 %collective-permute-start.3 = (bf16[480,128]{1,0:T(8,128)(2,1)S(1)}, bf16[480,128]{1,0:T(8,128)(2,1)S(1)}, u32[]{:S(2)}, u32[]{:S(2)}) collective-permute-start(bf16[480,128]{1,0:T(8,128)(2,1)S(1)} %get-tuple-element.20.refs_0_.refs_3_), channel_id=1, source_target_pairs={{0,7},{1,0},{2,5},{3,2},{4,3},{5,4},{6,1},{7,6},{8,15},{9,8},{10,1... | collective-permute-start | bytes 368648 | tf_op jit(solution)/shard_map/ppermute | solution.py:216
  15.9 0.0 collective-permute-done.6.refs_4_
  15.9 3.5 %collective-permute-done.4.refs_0_.refs_2_.refs_5_ = bf16[480,128]{1,0:T(8,128)(2,1)S(1)} collective-permute-done((bf16[480,128]{1,0:T(8,128)(2,1)S(1)}, bf16[480,128]{1,0:T(8,128)(2,1)S(1)}, u32[]{:S(2)}, u32[]{:S(2)}) %collective-permute-start.4) | collective-permute-done | bytes 122912 | tf_op jit(solution)/shard_map/ppermute | solution.py:216
  19.5 0.1 collective-permute-start.7
  19.6 0.0 collective-permute-done.5.refs_2_.refs_1_.refs_3_
  19.6 0.8 %match.4.refs_9_ = f32[4,480]{1,0:T(4,128)S(1)} custom-call(bf16[480,128]{1,0:T(8,128)(2,1)S(1)} %collective-permute-done.4.refs_0_.refs_2_.refs_5_, bf16[480,128]{1,0:T(8,128)(2,1)S(1)} %collective-permute-done.5.refs_2_.refs_1_.refs_3_, bf16[480,128]{1,0:T(8,128)(2,1)S(1)} %collective-permute-done.5.refs_2_.refs_1_.refs_3_, ...), custom_call_target="tpu_custom_call" | custom-call | flops 117964800 | bytes 4194304 | tf_op jit(solution)/shard_map/match/pallas_call | solution.py:184
  20.3 0.0 collective-permute-done.3.refs_1_
  20.3 0.8 %match.3.refs_8_ = f32[4,480]{1,0:T(4,128)S(1)} custom-call(bf16[480,128]{1,0:T(8,128)(2,1)S(1)} %get-tuple-element.20.refs_0_.refs_3_, bf16[480,128]{1,0:T(8,128)(2,1)S(1)} %collective-permute-done.3.refs_1_, bf16[480,128]{1,0:T(8,128)(2,1)S(1)} %collective-permute-done.5.refs_2_.refs_1_.refs_3_, bf16[480,128]{1,0:T(8,128)(2,1)S(1)} %get-tuple-element.20.refs_0_.refs_3_, ...), custom_call_target="tpu_custom_call" | custom-call | flops 117964800 | bytes 4194304 | tf_op jit(solution)/shard_map/match/pallas_call | solution.py:184
  21.1 0.0 collective-permute-done.7.refs_6_.refs_7_
  21.1 1.3 %match.5 = (f32[4,480]{1,0:T(4,128)S(1)}, f32[4,480]{1,0:T(4,128)S(1)}) custom-call(bf16[480,128]{1,0:T(8,128)(2,1)S(1)} %get-tuple-element.20.refs_0_.refs_3_, bf16[480,128]{1,0:T(8,128)(2,1)S(1)} %collective-permute-done.3.refs_1_, bf16[480,128]{1,0:T(8,128)(2,1)S(1)} %collective-permute-done.4.refs_0_.refs_2_.refs_5_, ...), custom_call_target="tpu_custom_call" | custom-call | flops 235929600 | bytes 4194304 | tf_op jit(solution)/shard_map/match/pallas_call | solution.py:184
  22.4 0.5 %collective-permute-start.8 = (f32[4,480]{1,0:T(4,128)S(1)}, f32[4,480]{1,0:T(4,128)S(1)}, u32[]{:S(2)}, u32[]{:S(2)}) collective-permute-start(f32[4,480]{1,0:T(4,128)S(1)} %get-tuple-element.15), channel_id=1, source_target_pairs={{0,2},{1,7},{2,0},{3,5},{4,6},{5,3},{6,4},{7,1},{8,10},{9,15},{10,... | collective-permute-start | bytes 23048 | tf_op jit(solution)/shard_map/ppermute | solution.py:216
  22.8 1.6 %collective-permute-start.9 = (f32[4,480]{1,0:T(4,128)S(1)}, f32[4,480]{1,0:T(4,128)S(1)}, u32[]{:S(2)}, u32[]{:S(2)}) collective-permute-start(f32[4,480]{1,0:T(4,128)S(1)} %get-tuple-element.16), channel_id=1, source_target_pairs={{0,2},{1,5},{2,0},{3,7},{4,6},{5,1},{6,4},{7,3},{8,10},{9,13},{10,... | collective-permute-start | bytes 23048 | tf_op jit(solution)/shard_map/ppermute | solution.py:216
  24.5 1.6 %collective-permute-done.8 = f32[4,480]{1,0:T(4,128)S(1)} collective-permute-done((f32[4,480]{1,0:T(4,128)S(1)}, f32[4,480]{1,0:T(4,128)S(1)}, u32[]{:S(2)}, u32[]{:S(2)}) %collective-permute-start.8) | collective-permute-done | bytes 7712 | tf_op jit(solution)/shard_map/ppermute | solution.py:216
  26.1 0.4 %collective-permute-done.9 = f32[4,480]{1,0:T(4,128)S(1)} collective-permute-done((f32[4,480]{1,0:T(4,128)S(1)}, f32[4,480]{1,0:T(4,128)S(1)}, u32[]{:S(2)}, u32[]{:S(2)}) %collective-permute-start.9) | collective-permute-done | bytes 7712 | tf_op jit(solution)/shard_map/ppermute | solution.py:216
  26.6 0.5 %collective-permute-start.10 = (f32[4,480]{1,0:T(4,128)S(1)}, f32[4,480]{1,0:T(4,128)S(1)}, u32[]{:S(2)}, u32[]{:S(2)}) collective-permute-start(f32[4,480]{1,0:T(4,128)S(1)} %pad_maximum_fusion), channel_id=1, source_target_pairs={{0,1},{1,0},{2,3},{3,2},{4,5},{5,4},{6,7},{7,6},{8,9},{9,8},{10,11... | collective-permute-start | bytes 23048 | tf_op jit(solution)/shard_map/ppermute | solution.py:216
  27.1 0.8 %collective-permute-done.10 = f32[4,480]{1,0:T(4,128)S(1)} collective-permute-done((f32[4,480]{1,0:T(4,128)S(1)}, f32[4,480]{1,0:T(4,128)S(1)}, u32[]{:S(2)}, u32[]{:S(2)}) %collective-permute-start.10) | collective-permute-done | bytes 7712 | tf_op jit(solution)/shard_map/ppermute | solution.py:216
  28.0 0.6 %copy.5 = f32[2,1,480]{2,1,0:T(1,128)} copy(f32[2,1,480]{2,0,1:T(2,128)S(1)} %maximum_bitcast_fusion) | data formatting | bytes 7680 | tf_op jit(solution)/shard_map/reshape | solution.py:274
  (12 shorter events, 0.2 us)
Async XLA Ops:
  0.0 4.5 %copy-start.1 = (bf16[2,960,128]{2,1,0:T(8,128)(2,1)S(1)}, bf16[2,960,128]{2,1,0:T(8,128)(2,1)}, u32[]{:S(2)}) copy-start(bf16[2,960,128]{2,1,0:T(8,128)(2,1)} %query_hbm.1) | copy-start | bytes 1474564
  0.0 4.5 %copy-start.2 = (bf16[2,960,128]{2,1,0:T(8,128)(2,1)S(1)}, bf16[2,960,128]{2,1,0:T(8,128)(2,1)}, u32[]{:S(2)}) copy-start(bf16[2,960,128]{2,1,0:T(8,128)(2,1)} %target_hbm.1) | copy-start | bytes 1474564
  0.0 4.5 %copy-start = (bf16[3,3,128,128]{3,2,1,0:T(8,128)(2,1)S(1)}, bf16[3,3,128,128]{3,2,1,0:T(8,128)(2,1)}, u32[]{:S(2)}) copy-start(bf16[3,3,128,128]{3,2,1,0:T(8,128)(2,1)} %weight_ref.3) | copy-start | bytes 884740
  1.4 4.3 %collective-permute-start = (bf16[960,128]{1,0:T(8,128)(2,1)S(1)}, bf16[960,128]{1,0:T(8,128)(2,1)S(1)}, u32[]{:S(2)}, u32[]{:S(2)}) collective-permute-start(bf16[960,128]{1,0:T(8,128)(2,1)S(1)} %get-tuple-element.13), channel_id=1, source_target_pairs={{0,1},{1,0},{2,3},{3,2},{4,5},{5,4},{6,7},{7,6},{8,9},{9,8},{10,11... | collective-permute-start | bytes 737288 | tf_op jit(solution)/shard_map/ppermute | solution.py:216
  1.9 12.5 %collective-permute-start.2 = (f32[480,128]{1,0:T(8,128)S(1)}, f32[480,128]{1,0:T(8,128)S(1)}, u32[]{:S(2)}, u32[]{:S(2)}) collective-permute-start(f32[480,128]{1,0:T(8,128)S(1)} %get-tuple-element.14), channel_id=1, source_target_pairs={{0,2},{1,3},{2,4},{3,5},{4,6},{5,7},{6,8},{7,9},{8,10},{9,11},{10,... | collective-permute-start | bytes 737288 | tf_op jit(solution)/shard_map/ppermute | solution.py:216
  4.5 0.7 %copy-start.3 = (f32[128]{0:T(128)S(1)}, f32[128]{0:T(128)}, u32[]{:S(2)}) copy-start(f32[128]{0:T(128)} %param.7) | copy-start | bytes 1540
  6.0 8.4 %collective-permute-start.1 = (f32[480,128]{1,0:T(8,128)S(1)}, f32[480,128]{1,0:T(8,128)S(1)}, u32[]{:S(2)}, u32[]{:S(2)}) collective-permute-start(f32[480,128]{1,0:T(8,128)S(1)} %convert_select_fusion), channel_id=1, source_target_pairs={{0,1},{1,0},{2,3},{3,2},{4,5},{5,4},{6,7},{7,6},{8,9},{9,8},{10,11... | collective-permute-start | bytes 737288 | tf_op jit(solution)/shard_map/ppermute | solution.py:216
  6.3 9.7 %collective-permute-start.6 = (bf16[480,128]{1,0:T(8,128)(2,1)S(1)}, bf16[480,128]{1,0:T(8,128)(2,1)S(1)}, u32[]{:S(2)}, u32[]{:S(2)}) collective-permute-start(bf16[480,128]{1,0:T(8,128)(2,1)S(1)} %odd_row.1.refs_5_), channel_id=1, source_target_pairs={{0,1},{1,8},{2,3},{3,10},{4,5},{5,12},{6,7},{7,14},{8,9},{9,0},{10... | collective-permute-start | bytes 368648 | tf_op jit(solution)/shard_map/ppermute | solution.py:216
  14.5 4.9 %collective-permute-start.4 = (bf16[480,128]{1,0:T(8,128)(2,1)S(1)}, bf16[480,128]{1,0:T(8,128)(2,1)S(1)}, u32[]{:S(2)}, u32[]{:S(2)}) collective-permute-start(bf16[480,128]{1,0:T(8,128)(2,1)S(1)} %get-tuple-element.20.refs_0_.refs_3_), channel_id=1, source_target_pairs={{0,2},{1,9},{2,0},{3,11},{4,6},{5,13},{6,4},{7,15},{8,10},{9,1},{1... | collective-permute-start | bytes 368648 | tf_op jit(solution)/shard_map/ppermute | solution.py:216
  14.6 5.0 %collective-permute-start.5 = (bf16[480,128]{1,0:T(8,128)(2,1)S(1)}, bf16[480,128]{1,0:T(8,128)(2,1)S(1)}, u32[]{:S(2)}, u32[]{:S(2)}) collective-permute-start(bf16[480,128]{1,0:T(8,128)(2,1)S(1)} %get-tuple-element.20.refs_0_.refs_3_), channel_id=1, source_target_pairs={{0,5},{1,0},{2,7},{3,2},{4,1},{5,4},{6,3},{7,6},{8,13},{9,8},{10,1... | collective-permute-start | bytes 368648 | tf_op jit(solution)/shard_map/ppermute | solution.py:216
  15.5 4.9 %collective-permute-start.3 = (bf16[480,128]{1,0:T(8,128)(2,1)S(1)}, bf16[480,128]{1,0:T(8,128)(2,1)S(1)}, u32[]{:S(2)}, u32[]{:S(2)}) collective-permute-start(bf16[480,128]{1,0:T(8,128)(2,1)S(1)} %get-tuple-element.20.refs_0_.refs_3_), channel_id=1, source_target_pairs={{0,7},{1,0},{2,5},{3,2},{4,3},{5,4},{6,1},{7,6},{8,15},{9,8},{10,1... | collective-permute-start | bytes 368648 | tf_op jit(solution)/shard_map/ppermute | solution.py:216
  19.5 1.6 %collective-permute-start.7 = (bf16[480,128]{1,0:T(8,128)(2,1)S(1)}, bf16[480,128]{1,0:T(8,128)(2,1)S(1)}, u32[]{:S(2)}, u32[]{:S(2)}) collective-permute-start(bf16[480,128]{1,0:T(8,128)(2,1)S(1)} %broadcast_select_fusion), channel_id=1, source_target_pairs={{0,1},{1,0},{2,3},{3,2},{4,5},{5,4},{6,7},{7,6},{8,9},{9,8},{10,11... | collective-permute-start | bytes 368648 | tf_op jit(solution)/shard_map/ppermute | solution.py:216
  22.4 3.7 %collective-permute-start.8 = (f32[4,480]{1,0:T(4,128)S(1)}, f32[4,480]{1,0:T(4,128)S(1)}, u32[]{:S(2)}, u32[]{:S(2)}) collective-permute-start(f32[4,480]{1,0:T(4,128)S(1)} %get-tuple-element.15), channel_id=1, source_target_pairs={{0,2},{1,7},{2,0},{3,5},{4,6},{5,3},{6,4},{7,1},{8,10},{9,15},{10,... | collective-permute-start | bytes 23048 | tf_op jit(solution)/shard_map/ppermute | solution.py:216
  22.8 3.7 %collective-permute-start.9 = (f32[4,480]{1,0:T(4,128)S(1)}, f32[4,480]{1,0:T(4,128)S(1)}, u32[]{:S(2)}, u32[]{:S(2)}) collective-permute-start(f32[4,480]{1,0:T(4,128)S(1)} %get-tuple-element.16), channel_id=1, source_target_pairs={{0,2},{1,5},{2,0},{3,7},{4,6},{5,1},{6,4},{7,3},{8,10},{9,13},{10,... | collective-permute-start | bytes 23048 | tf_op jit(solution)/shard_map/ppermute | solution.py:216
  26.6 1.3 %collective-permute-start.10 = (f32[4,480]{1,0:T(4,128)S(1)}, f32[4,480]{1,0:T(4,128)S(1)}, u32[]{:S(2)}, u32[]{:S(2)}) collective-permute-start(f32[4,480]{1,0:T(4,128)S(1)} %pad_maximum_fusion), channel_id=1, source_target_pairs={{0,1},{1,0},{2,3},{3,2},{4,5},{5,4},{6,7},{7,6},{8,9},{9,8},{10,11... | collective-permute-start | bytes 23048 | tf_op jit(solution)/shard_map/ppermute | solution.py:216

commit v11 on v10

--- a/solution.py
+++ b/solution.py
@@ -205,6 +205,31 @@
     return jnp.concatenate([highest, sums], axis=-2)
 
 
+def finish_kernel(scale, own_ref, other_ref, flow_ref):
+    slot = lax.axis_index("query")
+    state = merged(
+        tuple(own_ref[pl.ds(i, 1), :] for i in range(4)),
+        tuple(other_ref[pl.ds(i, 1), :] for i in range(4)),
+        scale,
+    )
+    columns = lax.broadcasted_iota(jnp.int32, state[0].shape, 1).astype(jnp.float32) * CELL
+    flow_ref[0] = state[2] / state[1] - columns
+    flow_ref[1] = state[3] / state[1] - slot.astype(jnp.float32) * CELL
+
+
+def finished(own, other, scale):
+    lanes = own.shape[1]
+    vmem = pl.BlockSpec(memory_space=pltpu.VMEM)
+    return pl.pallas_call(
+        functools.partial(finish_kernel, scale),
+        out_shape=jax.ShapeDtypeStruct((2, 1, lanes), jnp.float32),
+        in_specs=[vmem, vmem],
+        out_specs=vmem,
+        compiler_params=pltpu.CompilerParams(vmem_limit_bytes=VMEM_LIMIT),
+        name="finish",
+    )(own, other)
+
+
 def routed(value, route):
     slots, cores = lax.axis_size("query"), lax.axis_size("target")
     pairs = []
@@ -220,7 +245,6 @@
     slot = lax.axis_index("query")
     core = lax.axis_index("target")
     slots = lax.axis_size("query")
-    row_width = query_input.shape[1] // 2
     channels = conv_weight.shape[3]
     scale = LOG2E / math.sqrt(channels)
     first = core == 0
@@ -267,11 +291,7 @@
     corner_state = routed(state, lambda s, c: (s ^ (1 if c == 0 else 3), c))
     near_state = routed(other, lambda s, c: (s ^ (1 if c == 0 else 2), c))
     own = combined(pick(state, corner_state), near_state, scale)
-    total = combined(own, swapped(own), scale)
-    columns = jnp.arange(row_width, dtype=jnp.int32).astype(jnp.float32) * CELL
-    flow_x = total[2] / total[1] - columns
-    flow_y = total[3] / total[1] - slot.astype(jnp.float32) * CELL
-    return jnp.stack([flow_x, flow_y]).reshape(2, 1, row_width)
+    return finished(own, swapped(own), scale)
 
 
 def solution(mesh):

time: 28.7 us -> 28.6 us (level)
  Pallas kernels: 4.98 us -> 5.59 us
  local copies, waits for them, and re-layouts: 1.25 us -> 0.66 us
    pallas_call x0 -> x1, Pallas kernels: none -> 0.61 us  [finished(): pl.pallas_call(functools.partial(finish_kernel, scale), out_shape=jax.Sha...]
    reshape x1 -> x0, local copies, waits for them, and re-layouts: 0.6 us -> none  [on_device(): return jnp.stack([flow_x, flow_y]).reshape(2, 1, row_width)]
where the time goes in v11:
time: 28.6 us; the launch traced here: 28.5 us
  waiting for transfers between devices  14.2 us (50%)
  starting transfers between devices  7.74 us (27%)
  Pallas kernels  5.59 us (20%)
  local copies, waits for them, and re-layouts  0.66 us (2%)
    ppermute x11, waiting for transfers between devices, routed(): return lax.ppermute(value, ('query', 'target'), pairs)  14.2 us
    ppermute x11, starting transfers between devices, routed(): return lax.ppermute(value, ('query', 'target'), pairs)  7.74 us
    pallas_call x3, Pallas kernels, match(): pl.pallas_call(functools.partial(match_kernel, count, bool(states), row_i...  2.78 us
    pallas_call x1, Pallas kernels, rim_partials(): pl.pallas_call(rim_kernel, out_shape=(jax.ShapeDtypeStruct((cols // 2, ou...  1.39 us
    unnamed x8, local copies, waits for them, and re-layouts  0.66 us
    pallas_call x1, Pallas kernels, finished(): pl.pallas_call(functools.partial(finish_kernel, scale), out_shape=jax.Sha...  0.61 us
  transfers between devices with their start and end apart: 11, of which 5 were waited for; matrix products, arithmetic and copies ran while one was open for 0% of the time, Pallas kernels for 8%

profile of v11, /device:TPU:0, one launch (start us, length us, event | category | flops | bytes accessed | tf_op | source)
XLA Modules:
  0.0 28.5 jit_solution(15630047907496284632)
XLA Ops:
  0.0 0.0 copy-start.1
  0.0 0.0 copy-start.2
  0.0 0.0 copy-start
  0.0 1.4 %rim_partials.1 = (f32[480,128]{1,0:T(8,128)S(1)}, bf16[960,128]{1,0:T(8,128)(2,1)S(1)}) custom-call(bf16[2,960,128]{2,1,0:T(8,128)(2,1)} %query_hbm.1, bf16[2,960,128]{2,1,0:T(8,128)(2,1)} %target_hbm.1, bf16[3,3,128,128]{3,2,1,0:T(8,128)(2,1)} %weight_ref.3), custom_call_target="tpu_custom_call" | custom-call | tf_op jit(solution)/shard_map/rim_partials/pallas_call | solution.py:62
  1.4 0.5 %collective-permute-start = (bf16[960,128]{1,0:T(8,128)(2,1)S(1)}, bf16[960,128]{1,0:T(8,128)(2,1)S(1)}, u32[]{:S(2)}, u32[]{:S(2)}) collective-permute-start(bf16[960,128]{1,0:T(8,128)(2,1)S(1)} %get-tuple-element.13), channel_id=1, source_target_pairs={{0,1},{1,0},{2,3},{3,2},{4,5},{5,4},{6,7},{7,6},{8,9},{9,8},{10,11... | collective-permute-start | bytes 737288 | tf_op jit(solution)/shard_map/ppermute | solution.py:241
  1.9 2.6 %collective-permute-start.2 = (f32[480,128]{1,0:T(8,128)S(1)}, f32[480,128]{1,0:T(8,128)S(1)}, u32[]{:S(2)}, u32[]{:S(2)}) collective-permute-start(f32[480,128]{1,0:T(8,128)S(1)} %get-tuple-element.14), channel_id=1, source_target_pairs={{0,2},{1,3},{2,4},{3,5},{4,6},{5,7},{6,8},{7,9},{8,10},{9,11},{10,... | collective-permute-start | bytes 737288 | tf_op jit(solution)/shard_map/ppermute | solution.py:241
  4.5 0.0 copy-start.3
  4.5 0.0 copy-done.1
  4.5 0.0 copy-done.2
  4.5 0.0 copy-done
  4.5 0.6 %copy-done.3 = f32[128]{0:T(128)S(1)} copy-done((f32[128]{0:T(128)S(1)}, f32[128]{0:T(128)}, u32[]{:S(2)}) %copy-start.3) | copy-done | bytes 536
  5.2 0.5 %own_partials.1 = (f32[480,128]{1,0:T(8,128)S(1)}, f32[480,128]{1,0:T(8,128)S(1)}) custom-call(bf16[2,960,128]{2,1,0:T(8,128)(2,1)S(1)} %copy-done.1, bf16[2,960,128]{2,1,0:T(8,128)(2,1)S(1)} %copy-done.2, bf16[3,3,128,128]{3,2,1,0:T(8,128)(2,1)S(1)} %copy-done, f32[1,128]{1,0:T(1,128)S(1)} %bitcast.3), custom_call_target="tpu_custom_call" | custom-call | flops 188743680 | bytes 4194304 | tf_op jit(solution)/shard_map/own_partials/pallas_call | solution.py:116
  5.7 0.0 collective-permute-done.row_ref
  5.7 0.3 odd_row.1.refs_5_
  6.0 0.2 collective-permute-start.1
  6.3 0.3 %collective-permute-start.6 = (bf16[480,128]{1,0:T(8,128)(2,1)S(1)}, bf16[480,128]{1,0:T(8,128)(2,1)S(1)}, u32[]{:S(2)}, u32[]{:S(2)}) collective-permute-start(bf16[480,128]{1,0:T(8,128)(2,1)S(1)} %odd_row.1.refs_5_), channel_id=1, source_target_pairs={{0,1},{1,8},{2,3},{3,10},{4,5},{5,12},{6,7},{7,14},{8,9},{9,0},{10... | collective-permute-start | bytes 368648 | tf_op jit(solution)/shard_map/ppermute | solution.py:241
  6.6 7.9 %collective-permute-done.2 = f32[480,128]{1,0:T(8,128)S(1)} collective-permute-done((f32[480,128]{1,0:T(8,128)S(1)}, f32[480,128]{1,0:T(8,128)S(1)}, u32[]{:S(2)}, u32[]{:S(2)}) %collective-permute-start.2) | collective-permute-done | bytes 245792 | tf_op jit(solution)/shard_map/ppermute | solution.py:241
  14.5 0.0 collective-permute-done.1
  14.5 0.1 collective-permute-start.4
  14.6 0.9 %collective-permute-start.5 = (bf16[480,128]{1,0:T(8,128)(2,1)S(1)}, bf16[480,128]{1,0:T(8,128)(2,1)S(1)}, u32[]{:S(2)}, u32[]{:S(2)}) collective-permute-start(bf16[480,128]{1,0:T(8,128)(2,1)S(1)} %get-tuple-element.20.refs_0_.refs_3_), channel_id=1, source_target_pairs={{0,5},{1,0},{2,7},{3,2},{4,1},{5,4},{6,3},{7,6},{8,13},{9,8},{10,1... | collective-permute-start | bytes 368648 | tf_op jit(solution)/shard_map/ppermute | solution.py:241
  15.5 0.5 %collective-permute-start.3 = (bf16[480,128]{1,0:T(8,128)(2,1)S(1)}, bf16[480,128]{1,0:T(8,128)(2,1)S(1)}, u32[]{:S(2)}, u32[]{:S(2)}) collective-permute-start(bf16[480,128]{1,0:T(8,128)(2,1)S(1)} %get-tuple-element.20.refs_0_.refs_3_), channel_id=1, source_target_pairs={{0,7},{1,0},{2,5},{3,2},{4,3},{5,4},{6,1},{7,6},{8,15},{9,8},{10,1... | collective-permute-start | bytes 368648 | tf_op jit(solution)/shard_map/ppermute | solution.py:241
  15.9 0.0 collective-permute-done.6.refs_4_
  15.9 3.5 %collective-permute-done.4.refs_0_.refs_2_.refs_5_ = bf16[480,128]{1,0:T(8,128)(2,1)S(1)} collective-permute-done((bf16[480,128]{1,0:T(8,128)(2,1)S(1)}, bf16[480,128]{1,0:T(8,128)(2,1)S(1)}, u32[]{:S(2)}, u32[]{:S(2)}) %collective-permute-start.4) | collective-permute-done | bytes 122912 | tf_op jit(solution)/shard_map/ppermute | solution.py:241
  19.5 0.1 collective-permute-start.7
  19.6 0.0 collective-permute-done.5.refs_2_.refs_1_.refs_3_
  19.6 0.8 %match.4.refs_9_ = f32[4,480]{1,0:T(4,128)S(1)} custom-call(bf16[480,128]{1,0:T(8,128)(2,1)S(1)} %collective-permute-done.4.refs_0_.refs_2_.refs_5_, bf16[480,128]{1,0:T(8,128)(2,1)S(1)} %collective-permute-done.5.refs_2_.refs_1_.refs_3_, bf16[480,128]{1,0:T(8,128)(2,1)S(1)} %collective-permute-done.5.refs_2_.refs_1_.refs_3_, ...), custom_call_target="tpu_custom_call" | custom-call | flops 117964800 | bytes 4194304 | tf_op jit(solution)/shard_map/match/pallas_call | solution.py:184
  20.3 0.0 collective-permute-done.3.refs_1_
  20.3 0.8 %match.3.refs_8_ = f32[4,480]{1,0:T(4,128)S(1)} custom-call(bf16[480,128]{1,0:T(8,128)(2,1)S(1)} %get-tuple-element.20.refs_0_.refs_3_, bf16[480,128]{1,0:T(8,128)(2,1)S(1)} %collective-permute-done.3.refs_1_, bf16[480,128]{1,0:T(8,128)(2,1)S(1)} %collective-permute-done.5.refs_2_.refs_1_.refs_3_, bf16[480,128]{1,0:T(8,128)(2,1)S(1)} %get-tuple-element.20.refs_0_.refs_3_, ...), custom_call_target="tpu_custom_call" | custom-call | flops 117964800 | bytes 4194304 | tf_op jit(solution)/shard_map/match/pallas_call | solution.py:184
  21.1 0.0 collective-permute-done.7.refs_6_.refs_7_
  21.1 1.3 %match.5 = (f32[4,480]{1,0:T(4,128)S(1)}, f32[4,480]{1,0:T(4,128)S(1)}) custom-call(bf16[480,128]{1,0:T(8,128)(2,1)S(1)} %get-tuple-element.20.refs_0_.refs_3_, bf16[480,128]{1,0:T(8,128)(2,1)S(1)} %collective-permute-done.3.refs_1_, bf16[480,128]{1,0:T(8,128)(2,1)S(1)} %collective-permute-done.4.refs_0_.refs_2_.refs_5_, ...), custom_call_target="tpu_custom_call" | custom-call | flops 235929600 | bytes 4194304 | tf_op jit(solution)/shard_map/match/pallas_call | solution.py:184
  22.4 0.5 %collective-permute-start.8 = (f32[4,480]{1,0:T(4,128)S(1)}, f32[4,480]{1,0:T(4,128)S(1)}, u32[]{:S(2)}, u32[]{:S(2)}) collective-permute-start(f32[4,480]{1,0:T(4,128)S(1)} %get-tuple-element.15), channel_id=1, source_target_pairs={{0,2},{1,7},{2,0},{3,5},{4,6},{5,3},{6,4},{7,1},{8,10},{9,15},{10,... | collective-permute-start | bytes 23048 | tf_op jit(solution)/shard_map/ppermute | solution.py:241
  22.8 1.6 %collective-permute-start.9 = (f32[4,480]{1,0:T(4,128)S(1)}, f32[4,480]{1,0:T(4,128)S(1)}, u32[]{:S(2)}, u32[]{:S(2)}) collective-permute-start(f32[4,480]{1,0:T(4,128)S(1)} %get-tuple-element.16), channel_id=1, source_target_pairs={{0,2},{1,5},{2,0},{3,7},{4,6},{5,1},{6,4},{7,3},{8,10},{9,13},{10,... | collective-permute-start | bytes 23048 | tf_op jit(solution)/shard_map/ppermute | solution.py:241
  24.5 1.6 %collective-permute-done.8 = f32[4,480]{1,0:T(4,128)S(1)} collective-permute-done((f32[4,480]{1,0:T(4,128)S(1)}, f32[4,480]{1,0:T(4,128)S(1)}, u32[]{:S(2)}, u32[]{:S(2)}) %collective-permute-start.8) | collective-permute-done | bytes 7712 | tf_op jit(solution)/shard_map/ppermute | solution.py:241
  26.1 0.4 %collective-permute-done.9 = f32[4,480]{1,0:T(4,128)S(1)} collective-permute-done((f32[4,480]{1,0:T(4,128)S(1)}, f32[4,480]{1,0:T(4,128)S(1)}, u32[]{:S(2)}, u32[]{:S(2)}) %collective-permute-start.9) | collective-permute-done | bytes 7712 | tf_op jit(solution)/shard_map/ppermute | solution.py:241
  26.6 0.5 %collective-permute-start.10 = (f32[4,480]{1,0:T(4,128)S(1)}, f32[4,480]{1,0:T(4,128)S(1)}, u32[]{:S(2)}, u32[]{:S(2)}) collective-permute-start(f32[4,480]{1,0:T(4,128)S(1)} %pad_maximum_fusion.own_ref), channel_id=1, source_target_pairs={{0,1},{1,0},{2,3},{3,2},{4,5},{5,4},{6,7},{7,6},{8,9},{9,8},{10,11... | collective-permute-start | bytes 23048 | tf_op jit(solution)/shard_map/ppermute | solution.py:241
  27.1 0.8 %collective-permute-done.10.other_ref = f32[4,480]{1,0:T(4,128)S(1)} collective-permute-done((f32[4,480]{1,0:T(4,128)S(1)}, f32[4,480]{1,0:T(4,128)S(1)}, u32[]{:S(2)}, u32[]{:S(2)}) %collective-permute-start.10) | collective-permute-done | bytes 7712 | tf_op jit(solution)/shard_map/ppermute | solution.py:241
  27.9 0.6 %finish.1 = f32[2,1,480]{2,1,0:T(1,128)} custom-call(f32[4,480]{1,0:T(4,128)S(1)} %pad_maximum_fusion.own_ref, f32[4,480]{1,0:T(4,128)S(1)} %collective-permute-done.10.other_ref), custom_call_target="tpu_custom_call" | custom-call | tf_op jit(solution)/shard_map/finish/pallas_call | solution.py:223
  (8 shorter events, 0.1 us)
Async XLA Ops:
  0.0 4.5 %copy-start.1 = (bf16[2,960,128]{2,1,0:T(8,128)(2,1)S(1)}, bf16[2,960,128]{2,1,0:T(8,128)(2,1)}, u32[]{:S(2)}) copy-start(bf16[2,960,128]{2,1,0:T(8,128)(2,1)} %query_hbm.1) | copy-start | bytes 1474564
  0.0 4.5 %copy-start.2 = (bf16[2,960,128]{2,1,0:T(8,128)(2,1)S(1)}, bf16[2,960,128]{2,1,0:T(8,128)(2,1)}, u32[]{:S(2)}) copy-start(bf16[2,960,128]{2,1,0:T(8,128)(2,1)} %target_hbm.1) | copy-start | bytes 1474564
  0.0 4.5 %copy-start = (bf16[3,3,128,128]{3,2,1,0:T(8,128)(2,1)S(1)}, bf16[3,3,128,128]{3,2,1,0:T(8,128)(2,1)}, u32[]{:S(2)}) copy-start(bf16[3,3,128,128]{3,2,1,0:T(8,128)(2,1)} %weight_ref.3) | copy-start | bytes 884740
  1.4 4.3 %collective-permute-start = (bf16[960,128]{1,0:T(8,128)(2,1)S(1)}, bf16[960,128]{1,0:T(8,128)(2,1)S(1)}, u32[]{:S(2)}, u32[]{:S(2)}) collective-permute-start(bf16[960,128]{1,0:T(8,128)(2,1)S(1)} %get-tuple-element.13), channel_id=1, source_target_pairs={{0,1},{1,0},{2,3},{3,2},{4,5},{5,4},{6,7},{7,6},{8,9},{9,8},{10,11... | collective-permute-start | bytes 737288 | tf_op jit(solution)/shard_map/ppermute | solution.py:241
  1.9 12.5 %collective-permute-start.2 = (f32[480,128]{1,0:T(8,128)S(1)}, f32[480,128]{1,0:T(8,128)S(1)}, u32[]{:S(2)}, u32[]{:S(2)}) collective-permute-start(f32[480,128]{1,0:T(8,128)S(1)} %get-tuple-element.14), channel_id=1, source_target_pairs={{0,2},{1,3},{2,4},{3,5},{4,6},{5,7},{6,8},{7,9},{8,10},{9,11},{10,... | collective-permute-start | bytes 737288 | tf_op jit(solution)/shard_map/ppermute | solution.py:241
  4.5 0.7 %copy-start.3 = (f32[128]{0:T(128)S(1)}, f32[128]{0:T(128)}, u32[]{:S(2)}) copy-start(f32[128]{0:T(128)} %param.7) | copy-start | bytes 1540
  6.0 8.4 %collective-permute-start.1 = (f32[480,128]{1,0:T(8,128)S(1)}, f32[480,128]{1,0:T(8,128)S(1)}, u32[]{:S(2)}, u32[]{:S(2)}) collective-permute-start(f32[480,128]{1,0:T(8,128)S(1)} %convert_select_fusion), channel_id=1, source_target_pairs={{0,1},{1,0},{2,3},{3,2},{4,5},{5,4},{6,7},{7,6},{8,9},{9,8},{10,11... | collective-permute-start | bytes 737288 | tf_op jit(solution)/shard_map/ppermute | solution.py:241
  6.3 9.7 %collective-permute-start.6 = (bf16[480,128]{1,0:T(8,128)(2,1)S(1)}, bf16[480,128]{1,0:T(8,128)(2,1)S(1)}, u32[]{:S(2)}, u32[]{:S(2)}) collective-permute-start(bf16[480,128]{1,0:T(8,128)(2,1)S(1)} %odd_row.1.refs_5_), channel_id=1, source_target_pairs={{0,1},{1,8},{2,3},{3,10},{4,5},{5,12},{6,7},{7,14},{8,9},{9,0},{10... | collective-permute-start | bytes 368648 | tf_op jit(solution)/shard_map/ppermute | solution.py:241
  14.5 4.9 %collective-permute-start.4 = (bf16[480,128]{1,0:T(8,128)(2,1)S(1)}, bf16[480,128]{1,0:T(8,128)(2,1)S(1)}, u32[]{:S(2)}, u32[]{:S(2)}) collective-permute-start(bf16[480,128]{1,0:T(8,128)(2,1)S(1)} %get-tuple-element.20.refs_0_.refs_3_), channel_id=1, source_target_pairs={{0,2},{1,9},{2,0},{3,11},{4,6},{5,13},{6,4},{7,15},{8,10},{9,1},{1... | collective-permute-start | bytes 368648 | tf_op jit(solution)/shard_map/ppermute | solution.py:241
  14.6 5.0 %collective-permute-start.5 = (bf16[480,128]{1,0:T(8,128)(2,1)S(1)}, bf16[480,128]{1,0:T(8,128)(2,1)S(1)}, u32[]{:S(2)}, u32[]{:S(2)}) collective-permute-start(bf16[480,128]{1,0:T(8,128)(2,1)S(1)} %get-tuple-element.20.refs_0_.refs_3_), channel_id=1, source_target_pairs={{0,5},{1,0},{2,7},{3,2},{4,1},{5,4},{6,3},{7,6},{8,13},{9,8},{10,1... | collective-permute-start | bytes 368648 | tf_op jit(solution)/shard_map/ppermute | solution.py:241
  15.5 4.9 %collective-permute-start.3 = (bf16[480,128]{1,0:T(8,128)(2,1)S(1)}, bf16[480,128]{1,0:T(8,128)(2,1)S(1)}, u32[]{:S(2)}, u32[]{:S(2)}) collective-permute-start(bf16[480,128]{1,0:T(8,128)(2,1)S(1)} %get-tuple-element.20.refs_0_.refs_3_), channel_id=1, source_target_pairs={{0,7},{1,0},{2,5},{3,2},{4,3},{5,4},{6,1},{7,6},{8,15},{9,8},{10,1... | collective-permute-start | bytes 368648 | tf_op jit(solution)/shard_map/ppermute | solution.py:241
  19.5 1.6 %collective-permute-start.7 = (bf16[480,128]{1,0:T(8,128)(2,1)S(1)}, bf16[480,128]{1,0:T(8,128)(2,1)S(1)}, u32[]{:S(2)}, u32[]{:S(2)}) collective-permute-start(bf16[480,128]{1,0:T(8,128)(2,1)S(1)} %broadcast_select_fusion), channel_id=1, source_target_pairs={{0,1},{1,0},{2,3},{3,2},{4,5},{5,4},{6,7},{7,6},{8,9},{9,8},{10,11... | collective-permute-start | bytes 368648 | tf_op jit(solution)/shard_map/ppermute | solution.py:241
  22.4 3.7 %collective-permute-start.8 = (f32[4,480]{1,0:T(4,128)S(1)}, f32[4,480]{1,0:T(4,128)S(1)}, u32[]{:S(2)}, u32[]{:S(2)}) collective-permute-start(f32[4,480]{1,0:T(4,128)S(1)} %get-tuple-element.15), channel_id=1, source_target_pairs={{0,2},{1,7},{2,0},{3,5},{4,6},{5,3},{6,4},{7,1},{8,10},{9,15},{10,... | collective-permute-start | bytes 23048 | tf_op jit(solution)/shard_map/ppermute | solution.py:241
  22.8 3.7 %collective-permute-start.9 = (f32[4,480]{1,0:T(4,128)S(1)}, f32[4,480]{1,0:T(4,128)S(1)}, u32[]{:S(2)}, u32[]{:S(2)}) collective-permute-start(f32[4,480]{1,0:T(4,128)S(1)} %get-tuple-element.16), channel_id=1, source_target_pairs={{0,2},{1,5},{2,0},{3,7},{4,6},{5,1},{6,4},{7,3},{8,10},{9,13},{10,... | collective-permute-start | bytes 23048 | tf_op jit(solution)/shard_map/ppermute | solution.py:241
  26.6 1.3 %collective-permute-start.10 = (f32[4,480]{1,0:T(4,128)S(1)}, f32[4,480]{1,0:T(4,128)S(1)}, u32[]{:S(2)}, u32[]{:S(2)}) collective-permute-start(f32[4,480]{1,0:T(4,128)S(1)} %pad_maximum_fusion.own_ref), channel_id=1, source_target_pairs={{0,1},{1,0},{2,3},{3,2},{4,5},{5,4},{6,7},{7,6},{8,9},{9,8},{10,11... | collective-permute-start | bytes 23048 | tf_op jit(solution)/shard_map/ppermute | solution.py:241
